TPU v7x, 32 devices: a whole 2x2x4 slice. The times are simulated.
32 devices in a mesh: dp: 8 (over y, x, core), expert: 4 (over z).
Axes of the slice: x: 2, y: 2, z: 4, core: 2. Of those that a mesh axis runs over, the one named last changes fastest.
Arguments:
- tokens: bfloat16 [96, 2048], P('dp', 'expert'), may hold values from -6 to 6
- cotangent: bfloat16 [96, 2048], P('dp', 'expert'), may hold values from -6 to 6
- route: int32 [96, 2], P('dp'), may hold values from 0 to 3, all different within a row; in each aligned block of 12 rows (0 to 11, 12 to 23, ...) at most 9 rows name the same one
- gates: float32 [96, 2], P('dp'), may hold values from 0.25 to 1
- w_gate: bfloat16 [4, 12288, 2048], P('expert', 'dp'), may hold values from -0.125 to 0.125
- w_up: bfloat16 [4, 12288, 2048], P('expert', 'dp'), may hold values from -0.125 to 0.125
- w_down: bfloat16 [4, 12288, 2048], P('expert', 'dp'), may hold values from -0.0546875 to 0.0546875
Outputs:
- mixed: bfloat16 [96, 2048], P('dp', 'expert')
- grad_tokens: bfloat16 [96, 2048], P('dp', 'expert')
- grad_gate: bfloat16 [4, 12288, 2048], P('expert', 'dp')
- grad_up: bfloat16 [4, 12288, 2048], P('expert', 'dp')
- grad_down: bfloat16 [4, 12288, 2048], P('expert', 'dp')
Inputs may be any that keep to these rules, and one draw needn't show every extreme that they name: `route`: the two experts of a token differ. Among the 12 tokens of one index of dp, at most 9 name the same expert, and in some such block one expert is named by exactly 9 tokens. Every expert is named by some token.
All inputs are finite; a program needn't handle non-finite values.
Results may differ from a plain program's by a relative error of at most 0.0065.
Values may be sent and summed in bfloat16 or wider, within the bound.
No kernel may reach another device: no remote copies, remote signals or barrier semaphores. Data moves between devices by JAX's collectives and lax.ppermute only.
A program may use at most 128 MiB of HBM per device.

v0:
```python
import jax
import jax.numpy as jnp
from jax import lax
from jax.sharding import PartitionSpec as P


def contract_rows(left, right):
    return lax.dot_general(
        left, right, (((0,), (0,)), ((), ())), preferred_element_type=jnp.float32
    )


def contract_cols(left, right):
    return lax.dot_general(
        left, right, (((1,), (1,)), ((), ())), preferred_element_type=jnp.float32
    )


def apart_home(term_rows, capacity):
    summed = lax.psum_scatter(
        term_rows(jnp.int32(0), capacity * lax.axis_size("dp")),
        "dp",
        scatter_dimension=0,
        tiled=True,
    )
    return lax.all_to_all(
        summed.astype(jnp.bfloat16)[None], "expert", split_axis=2, concat_axis=0, tiled=True
    )


def per_device(tokens, cotangent, route, gates, w_gate, w_up, w_down):
    n_dp = lax.axis_size("dp")
    n_owner = lax.axis_size("expert")
    tok_rows = tokens.shape[0]
    feat_local = tokens.shape[1]
    full_width = feat_local * n_owner
    experts = w_gate.shape[0] * n_owner
    pairs = route.shape[1] * tok_rows
    capacity = min(tok_rows, max(2, 3 * tok_rows // experts))
    total_rows = n_dp * capacity
    assign = route.reshape(pairs)
    order = jnp.arange(pairs, dtype=jnp.int32)
    same = (assign[:, None] == assign[None, :]) & (order[None, :] < order[:, None])
    slot = jnp.sum(same.astype(jnp.int32), axis=1)
    expert_ids = jnp.arange(experts, dtype=jnp.int32)
    slot_ids = jnp.arange(capacity, dtype=jnp.int32)
    select = (
        (assign[None, None, :] == expert_ids[:, None, None])
        & (slot[None, None, :] == slot_ids[None, :, None])
    ).astype(jnp.bfloat16)
    gate_flat = gates.reshape(pairs)
    token_pairs = jnp.repeat(tokens, 2, axis=0)
    weighted = (gate_flat[:, None] * jnp.repeat(cotangent, 2, axis=0).astype(jnp.float32)).astype(
        jnp.bfloat16
    )
    send_tokens = jnp.einsum(
        "ecj,jd->ecd", select, token_pairs, preferred_element_type=jnp.float32
    ).astype(jnp.bfloat16)
    send_grads = jnp.einsum(
        "ecj,jd->ecd", select, weighted, preferred_element_type=jnp.float32
    ).astype(jnp.bfloat16)
    owned_tokens, owned_grads = (
        lax.all_to_all(send_tokens, "expert", split_axis=0, concat_axis=2, tiled=True),
        lax.all_to_all(send_grads, "expert", split_axis=0, concat_axis=2, tiled=True),
    )
    rows_tokens, rows_grads = (
        lax.all_gather(owned_tokens, "dp", axis=1, tiled=True),
        lax.all_gather(owned_grads, "dp", axis=1, tiled=True),
    )
    dys = rows_grads.reshape(total_rows, full_width)
    xs = rows_tokens.reshape(total_rows, full_width)
    w_g = w_gate[0]
    w_u = w_up[0]
    w_d = w_down[0]
    pre_gate = contract_cols(xs, w_g)
    pre_up = contract_cols(xs, w_u)
    sig = jax.nn.sigmoid(pre_gate)
    silu = pre_gate * sig
    hidden = (silu * pre_up).astype(jnp.bfloat16)

    def output_rows(start, count):
        return jnp.dot(hidden, w_d, preferred_element_type=jnp.float32)

    expert_home = apart_home(output_rows, capacity)
    grad_down = contract_rows(hidden, dys).astype(jnp.bfloat16)
    grad_hidden = contract_cols(dys, w_d)
    grad_pre_gate = (grad_hidden * pre_up * sig * (1.0 + pre_gate * (1.0 - sig))).astype(
        jnp.bfloat16
    )
    grad_pre_up = (grad_hidden * silu).astype(jnp.bfloat16)
    grad_gate = contract_rows(grad_pre_gate, xs).astype(jnp.bfloat16)
    grad_up = contract_rows(grad_pre_up, xs).astype(jnp.bfloat16)

    def input_rows(start, count):
        return jnp.dot(grad_pre_gate, w_g, preferred_element_type=jnp.float32) + jnp.dot(
            grad_pre_up, w_u, preferred_element_type=jnp.float32
        )

    grads_home = apart_home(input_rows, capacity)
    picked_out = jnp.einsum("ecj,ecd->jd", select, expert_home, preferred_element_type=jnp.float32)
    mixed = (
        (gate_flat[:, None] * picked_out)
        .reshape(tok_rows, 2, feat_local)
        .sum(axis=1)
        .astype(jnp.bfloat16)
    )
    picked_grad = jnp.einsum("ecj,ecd->jd", select, grads_home, preferred_element_type=jnp.float32)
    grad_tokens = picked_grad.reshape(tok_rows, 2, feat_local).sum(axis=1).astype(jnp.bfloat16)
    return (mixed, grad_tokens, grad_gate[None], grad_up[None], grad_down[None])


def solution(mesh):
    return jax.shard_map(
        per_device,
        mesh=mesh,
        in_specs=(
            P("dp", "expert"),
            P("dp", "expert"),
            P("dp", None),
            P("dp", None),
            P("expert", "dp", None),
            P("expert", "dp", None),
            P("expert", "dp", None),
        ),
        out_specs=(
            P("dp", "expert"),
            P("dp", "expert"),
            P("expert", "dp", None),
            P("expert", "dp", None),
            P("expert", "dp", None),
        ),
        check_vma=False,
    )
```

profile of v0, /device:TPU:0, one launch (start us, length us, event | category | flops | bytes accessed | tf_op | source)
XLA Modules:
  0.0 167.7 jit_solution(15957985572493378429)
XLA Ops:
  0.6 0.8 copy.47
  1.4 0.1 eq.69
  1.5 0.2 convert_reduce_fusion
  1.7 0.7 broadcast_in_dim.26
  2.5 0.8 convolution_convert_fusion.4
  3.2 6.3 %all-to-all-start = ((bf16[4,9,512]{2,1,0:T(8,128)(2,1)}), bf16[4,9,512]{2,1,0:T(8,128)(2,1)S(1)}, u32[]{:S(2)}, u32[]{:S(2)}) async-start(bf16[4,9,512]{2,1,0:T(8,128)(2,1)} %convolution_convert_fusion.4), calls=%async_computation | async-start | bytes 131072 | tf_op jit(solution)/shard_map/all_to_all | solution.py:63
  9.5 0.1 eq.82
  9.6 0.8 copy.46
  10.4 0.1 mul.37
  10.5 0.1 copy.53
  10.6 0.7 broadcast_in_dim.28
  11.4 0.8 convolution_convert_fusion.3
  12.2 0.1 iota_compare_fusion
  12.3 3.0 %all-to-all-done = bf16[4,9,512]{2,1,0:T(8,128)(2,1)S(1)} async-done(((bf16[4,9,512]{2,1,0:T(8,128)(2,1)}), bf16[4,9,512]{2,1,0:T(8,128)(2,1)S(1)}, u32[]{:S(2)}, u32[]{:S(2)}) %all-to-all-start) | async-done | bytes 36896 | tf_op jit(solution)/shard_map/all_to_all | solution.py:63
  15.3 3.3 %all-to-all-start.2 = ((bf16[4,9,512]{2,1,0:T(8,128)(2,1)}), bf16[4,9,512]{2,1,0:T(8,128)(2,1)S(1)}, u32[]{:S(2)}, u32[]{:S(2)}) async-start(bf16[4,9,512]{2,1,0:T(8,128)(2,1)} %convolution_convert_fusion.3), calls=%async_computation.2 | async-start | bytes 131072 | tf_op jit(solution)/shard_map/all_to_all | solution.py:64
  18.6 0.7 iota_compare_fusion.3
  19.3 1.2 dynamic-slice
  21.2 3.1 %all-to-all-done.2 = bf16[4,9,512]{2,1,0:T(8,128)(2,1)S(1)} async-done(((bf16[4,9,512]{2,1,0:T(8,128)(2,1)}), bf16[4,9,512]{2,1,0:T(8,128)(2,1)S(1)}, u32[]{:S(2)}, u32[]{:S(2)}) %all-to-all-start.2) | async-done | bytes 36896 | tf_op jit(solution)/shard_map/all_to_all | solution.py:64
  24.4 0.0 copy-start
  24.4 10.3 %all_gather.7 = bf16[1,72,2048]{2,0,1:T(2,128)(2,1)S(1)} all-gather(bf16[1,9,2048]{2,0,1:T(2,128)(2,1)S(1)} %all_to_all.69), channel_id=1, replica_groups=mesh['dp'=8,'expert'=4] {'dp'}, dimensions={1}, use_global_device_ids=true | all-gather | bytes 331776 | tf_op jit(solution)/shard_map/all_gather | solution.py:68
  34.6 10.0 %all_gather.6 = bf16[1,72,2048]{2,0,1:T(2,128)(2,1)S(1)} all-gather(bf16[1,9,2048]{2,0,1:T(2,128)(2,1)S(1)} %all_to_all.68), channel_id=1, replica_groups=mesh['dp'=8,'expert'=4] {'dp'}, dimensions={1}, use_global_device_ids=true | all-gather | bytes 331776 | tf_op jit(solution)/shard_map/all_gather | solution.py:67
  44.6 0.0 slice-start
  44.6 0.2 copy.60
  44.8 0.0 slice-start.1
  44.8 5.0 %fusion.3 = f32[72,1536]{1,0:T(8,128)S(1)} fusion(bf16[1,1536,2048]{2,1,0:T(8,128)(2,1)} %param.13, bf16[1,72,2048]{2,0,1:T(2,128)(2,1)S(1)} %all_gather.7), kind=kOutput, calls=%fused_computation.6 | convolution fusion | flops 452984832 | bytes 7028736 | tf_op jit(solution)/shard_map/dot_general | solution.py:14
  49.8 0.0 copy-done
  49.8 0.0 slice-start.2
  49.8 2.0 %fusion.9 = f32[72,1536]{1,0:T(8,128)S(1)} fusion(bf16[1,1536,2048]{2,1,0:T(8,128)(2,1)S(1)} %copy-done, bf16[1,72,2048]{2,1,0:T(8,128)(2,1)S(1)} %copy.60), kind=kOutput, calls=%fused_computation.12 | convolution fusion | flops 452984832 | bytes 7028736 | tf_op jit(solution)/shard_map/dot_general | solution.py:14
  51.8 0.0 slice-done
  51.8 0.0 slice-done.1
  51.8 0.0 slice-start.3
  51.9 2.2 %multiply_convert_fusion.1 = (bf16[72,1536]{1,0:T(8,128)(2,1)S(1)}, bf16[72,1536]{1,0:T(8,128)(2,1)S(1)}, bf16[72,1536]{1,0:T(8,128)(2,1)S(1)}) fusion(f32[72,1536]{1,0:T(8,128)S(1)} %fusion.3, f32[72,1536]{1,0:T(8,128)S(1)} %fusion.9, bf16[1,1536,2048]{2,1,0:T(8,128)(2,1)S(1)} %bitcast.88, bf16[1,72,2048]{2,1,0:T(8,128)(2,1)S(1)} %copy.60), kind=kOutput, calls=%fused_computation.26 | convolution fusion | flops 454643712 | bytes 8134656 | tf_op jit(solution)/shard_map/dot_general | solution.py:14
  54.0 0.0 slice-done.2
  54.0 0.0 slice-done.3
  54.1 1.3 fusion.5
  55.3 4.6 %fusion.2 = bf16[1,1536,2048]{2,1,0:T(8,128)(2,1)} fusion(bf16[72,1536]{1,0:T(8,128)(2,1)S(1)} %get-tuple-element.9, bf16[1,72,2048]{2,0,1:T(2,128)(2,1)S(1)} %all_gather.7), kind=kOutput, calls=%fused_computation.5 | convolution fusion | flops 456130560 | bytes 6807552 | tf_op jit(solution)/shard_map/dot_general | solution.py:8
  59.9 1.3 fusion.7
  61.1 4.5 %fusion = bf16[1,1536,2048]{2,1,0:T(8,128)(2,1)} fusion(bf16[72,1536]{1,0:T(8,128)(2,1)S(1)} %get-tuple-element.7, bf16[1,72,2048]{2,1,0:T(8,128)(2,1)S(1)} %copy.60), kind=kOutput, calls=%fused_computation.3 | convolution fusion | flops 456130560 | bytes 6807552 | tf_op jit(solution)/shard_map/dot_general | solution.py:8
  65.7 1.3 fusion.15
  66.9 50.8 %all-reduce.4 = (bf16[72,2048]{1,0:T(8,128)(2,1)S(1)}, bf16[72,2048]{1,0:T(8,128)(2,1)S(1)}) all-reduce(f32[72,2048]{1,0:T(8,128)S(1)} %fusion.5, f32[72,2048]{1,0:T(8,128)S(1)} %fusion.15), channel_id=2, replica_groups=mesh['dp'=8,'expert'=4] {'dp'}, use_global_device_ids=true, to_apply=%region_1.0.clone | all-reduce | flops 294912 | bytes 1769472
  117.8 0.8 copy.50
  118.7 0.5 broadcast.52
  119.2 11.5 %reduce = bf16[2048,9]{1,0:T(8,128)(2,1)S(1)} reduce(bf16[2048,1,9]{2,1,0:T(2,128)(2,1)S(1)} %bitcast.91, bf16[]{:T(256)} %broadcast.52), dimensions={1}, to_apply=%bitcast.72.reduce_sub_computation | reduce | bytes 73730
  130.7 1.4 reshape.103
  132.1 3.5 %all-to-all-start.1 = ((bf16[4,2,2304]{2,1,0:T(2,128)(2,1)}), bf16[4,2,2304]{2,1,0:T(2,128)(2,1)S(1)}, u32[]{:S(2)}, u32[]{:S(2)}) async-start(bf16[4,2,2304]{2,1,0:T(2,128)(2,1)} %reshape.103), calls=%async_computation.1 | async-start | bytes 73728 | tf_op jit(solution)/shard_map/all_to_all | solution.py:26
  135.6 4.5 %fusion.1 = bf16[1,1536,2048]{2,1,0:T(8,128)(2,1)} fusion(bf16[72,1536]{1,0:T(8,128)(2,1)S(1)} %get-tuple-element.8, bf16[1,72,2048]{2,1,0:T(8,128)(2,1)S(1)} %copy.60), kind=kOutput, calls=%fused_computation.4 | convolution fusion | flops 456130560 | bytes 6807552 | tf_op jit(solution)/shard_map/dot_general | solution.py:8
  140.1 0.8 copy.56
  141.0 11.5 %reduce.1 = bf16[2048,9]{1,0:T(8,128)(2,1)S(1)} reduce(bf16[2048,1,9]{2,1,0:T(2,128)(2,1)S(1)} %bitcast.92, bf16[]{:T(256)} %broadcast.52), dimensions={1}, to_apply=%bitcast.74.reduce_sub_computation | reduce | bytes 73730
  152.5 1.4 reshape.105
  153.9 0.0 all-to-all-done.1
  153.9 4.8 %all-to-all-start.3 = ((bf16[4,2,2304]{2,1,0:T(2,128)(2,1)}), bf16[4,2,2304]{2,1,0:T(2,128)(2,1)S(1)}, u32[]{:S(2)}, u32[]{:S(2)}) async-start(bf16[4,2,2304]{2,1,0:T(2,128)(2,1)} %reshape.105), calls=%async_computation.3 | async-start | bytes 73728 | tf_op jit(solution)/shard_map/all_to_all | solution.py:26
  158.7 1.1 reshape.104
  159.8 0.6 copy.51
  160.5 0.2 fusion.19
  160.7 3.7 %all-to-all-done.3 = bf16[4,2,2304]{2,1,0:T(2,128)(2,1)S(1)} async-done(((bf16[4,2,2304]{2,1,0:T(2,128)(2,1)}), bf16[4,2,2304]{2,1,0:T(2,128)(2,1)S(1)}, u32[]{:S(2)}, u32[]{:S(2)}) %all-to-all-start.3) | async-done | bytes 36896 | tf_op jit(solution)/shard_map/all_to_all | solution.py:26
  164.4 1.1 reshape.106
  165.5 0.6 copy.57
  166.1 0.7 reduce_sum.28
  166.8 0.9 fusion.18
  (14 shorter events, 0.3 us)
Async XLA Ops:
  3.2 12.1 %all-to-all-start = ((bf16[4,9,512]{2,1,0:T(8,128)(2,1)}), bf16[4,9,512]{2,1,0:T(8,128)(2,1)S(1)}, u32[]{:S(2)}, u32[]{:S(2)}) async-start(bf16[4,9,512]{2,1,0:T(8,128)(2,1)} %convolution_convert_fusion.4), calls=%async_computation | async-start | bytes 131072 | tf_op jit(solution)/shard_map/all_to_all | solution.py:63
  15.3 9.0 %all-to-all-start.2 = ((bf16[4,9,512]{2,1,0:T(8,128)(2,1)}), bf16[4,9,512]{2,1,0:T(8,128)(2,1)S(1)}, u32[]{:S(2)}, u32[]{:S(2)}) async-start(bf16[4,9,512]{2,1,0:T(8,128)(2,1)} %convolution_convert_fusion.3), calls=%async_computation.2 | async-start | bytes 131072 | tf_op jit(solution)/shard_map/all_to_all | solution.py:64
  24.4 25.4 %copy-start = (bf16[1,1536,2048]{2,1,0:T(8,128)(2,1)S(1)}, bf16[1,1536,2048]{2,1,0:T(8,128)(2,1)}, u32[]{:S(2)}) copy-start(bf16[1,1536,2048]{2,1,0:T(8,128)(2,1)} %param.12) | copy-start | bytes 18874372
  44.6 7.2 %slice-start = ((s8[6291456]{0:T(1024)(128)(4,1)}), s8[4194304]{0:T(1024)(128)(4,1)S(1)}, s32[]{:S(2)}) async-start(s8[6291456]{0:T(1024)(128)(4,1)} %bitcast.87), calls=%async_computation.4 | async-start | bytes 8388608
  44.8 7.1 %slice-start.1 = ((s8[6291456]{0:T(1024)(128)(4,1)}), s8[2097152]{0:T(1024)(128)(4,1)S(1)}, s32[]{:S(2)}) async-start(s8[6291456]{0:T(1024)(128)(4,1)} %bitcast.87), calls=%async_computation.5 | async-start | bytes 4194304
  49.8 4.3 %slice-start.2 = ((s8[6291456]{0:T(1024)(128)(4,1)}), s8[4194304]{0:T(1024)(128)(4,1)S(1)}, s32[]{:S(2)}) async-start(s8[6291456]{0:T(1024)(128)(4,1)} %bitcast.89), calls=%async_computation.6 | async-start | bytes 8388608
  51.8 2.2 %slice-start.3 = ((s8[6291456]{0:T(1024)(128)(4,1)}), s8[2097152]{0:T(1024)(128)(4,1)S(1)}, s32[]{:S(2)}) async-start(s8[6291456]{0:T(1024)(128)(4,1)} %bitcast.89), calls=%async_computation.7 | async-start | bytes 4194304
  132.1 21.8 %all-to-all-start.1 = ((bf16[4,2,2304]{2,1,0:T(2,128)(2,1)}), bf16[4,2,2304]{2,1,0:T(2,128)(2,1)S(1)}, u32[]{:S(2)}, u32[]{:S(2)}) async-start(bf16[4,2,2304]{2,1,0:T(2,128)(2,1)} %reshape.103), calls=%async_computation.1 | async-start | bytes 73728 | tf_op jit(solution)/shard_map/all_to_all | solution.py:26
  153.9 10.5 %all-to-all-start.3 = ((bf16[4,2,2304]{2,1,0:T(2,128)(2,1)}), bf16[4,2,2304]{2,1,0:T(2,128)(2,1)S(1)}, u32[]{:S(2)}, u32[]{:S(2)}) async-start(bf16[4,2,2304]{2,1,0:T(2,128)(2,1)} %reshape.105), calls=%async_computation.3 | async-start | bytes 73728 | tf_op jit(solution)/shard_map/all_to_all | solution.py:26
where the time goes:
time: 169 us; the launch traced here: 168 us
  blocking collectives  71.1 us (42%)
  matrix products  29.3 us (17%)
  other arithmetic  24.7 us (15%)
  starting transfers between devices  17.9 us (11%)
  local copies, waits for them, and re-layouts  13.4 us (8%)
  waiting for transfers between devices  9.76 us (6%)
    unnamed x1, blocking collectives  50.8 us
    unnamed x4, other arithmetic  23.1 us
    dot_general x3, matrix products, contract_rows(): lax.dot_general(left, right, (((0,), (0,)), ((), ())), preferred_element_...  13.6 us
    all_gather x1, blocking collectives, per_device(): lax.all_gather(owned_grads, 'dp', axis=1, tiled=True)  10.3 us
    all_gather x1, blocking collectives, per_device(): lax.all_gather(owned_tokens, 'dp', axis=1, tiled=True)  9.96 us
    dot_general x3, matrix products, contract_cols(): lax.dot_general(left, right, (((1,), (1,)), ((), ())), preferred_element_...  9.17 us
    unnamed x19, local copies, waits for them, and re-layouts  8.44 us
    all_to_all x2, starting transfers between devices, apart_home(): lax.all_to_all(summed.astype(jnp.bfloat16)[None], 'expert', split_axis=2,...  8.32 us
  transfers between devices with their start and end apart: 4, of which 3 were waited for; matrix products, arithmetic and copies ran while one was open for 15% of the time, Pallas kernels for 0%

commit v1 on v0

v1 whole, which is shorter than its diff:
```python
import jax
import jax.numpy as jnp
from jax import lax
from jax.experimental import pallas as pl
from jax.experimental.pallas import tpu as pltpu
from jax.sharding import PartitionSpec as P

BF = jnp.bfloat16
F32 = jnp.float32
VM = pl.BlockSpec(memory_space=pltpu.VMEM)
SM = pl.BlockSpec(memory_space=pltpu.SMEM)
ROWS = 16


def dot_nn(a, b):
    return lax.dot_general(a, b, (((1,), (0,)), ((), ())), preferred_element_type=F32)


def dot_nt(a, b):
    return lax.dot_general(a, b, (((1,), (1,)), ((), ())), preferred_element_type=F32)


def dot_tn(a, b):
    return lax.dot_general(a, b, (((0,), (0,)), ((), ())), preferred_element_type=F32)


def share(route, gates, expert):
    return jnp.sum(jnp.where(route == expert, gates, 0.0), axis=1, keepdims=True)


def params(mib):
    return pltpu.CompilerParams(vmem_limit_bytes=mib << 20)


def pack_kernel(tok_ref, cot_ref, route_ref, gates_ref, out_ref):
    width = tok_ref.shape[1]
    tok = tok_ref[...]
    cot = cot_ref[...].astype(F32)
    route = route_ref[...]
    gates = gates_ref[...]
    for e in range(out_ref.shape[0]):
        out_ref[e, :, :width] = tok
        out_ref[e, :, width:] = (share(route, gates, e) * cot).astype(BF)


def expert_kernel(
    parity_ref, got_ref, wg_ref, wu_ref, wd_ref,
    keep_ref, send_ref, xs_ref, dys_ref, hid_ref, gpg_ref, gpu_ref,
    out_acc, grad_acc,
):
    step = pl.program_id(0)
    n_dp, n_e, tok, pair = got_ref.shape
    width = pair // 2
    d = n_e * width

    @pl.when(step == 0)
    def _():
        xs_ref[...] = jnp.zeros_like(xs_ref)
        dys_ref[...] = jnp.zeros_like(dys_ref)
        for b in range(n_dp):
            for e in range(n_e):
                cols = slice(e * width, (e + 1) * width)
                xs_ref[b * ROWS : b * ROWS + tok, cols] = got_ref[b, e, :, :width]
                dys_ref[b * ROWS : b * ROWS + tok, cols] = got_ref[b, e, :, width:]
        out_acc[...] = jnp.zeros_like(out_acc)
        grad_acc[...] = jnp.zeros_like(grad_acc)

    xs = xs_ref[...]
    dys = dys_ref[...]
    wg = wg_ref[...]
    wu = wu_ref[...]
    wd = wd_ref[...]
    pre_gate = dot_nt(xs, wg)
    pre_up = dot_nt(xs, wu)
    sig = jax.nn.sigmoid(pre_gate)
    silu = pre_gate * sig
    hidden = (silu * pre_up).astype(BF)
    grad_hidden = dot_nt(dys, wd)
    gpg = (grad_hidden * pre_up * sig * (1.0 + pre_gate * (1.0 - sig))).astype(BF)
    gpu = (grad_hidden * silu).astype(BF)
    hid_ref[...] = hidden
    gpg_ref[...] = gpg
    gpu_ref[...] = gpu
    out_acc[...] += dot_nn(hidden, wd)
    grad_acc[...] += dot_nn(gpg, wg) + dot_nn(gpu, wu)

    @pl.when(step == pl.num_programs(0) - 1)
    def _():
        c = parity_ref[0]
        for i in range(n_dp // 2):
            mine = pl.ds(pl.multiple_of((2 * i + c) * ROWS, ROWS), ROWS)
            other = pl.ds(pl.multiple_of((2 * i + 1 - c) * ROWS, ROWS), ROWS)
            keep_ref[i, :, :d] = out_acc[mine, :].astype(BF)
            keep_ref[i, :, d:] = grad_acc[mine, :].astype(BF)
            send_ref[i, :, :d] = out_acc[other, :].astype(BF)
            send_ref[i, :, d:] = grad_acc[other, :].astype(BF)


def weight_grad_kernel(left_ref, right_ref, out_ref):
    out_ref[...] = dot_tn(left_ref[...], right_ref[...]).astype(BF)


def cores_kernel(chip_ref, keep_ref, got_ref, *out_refs):
    chip = chip_ref[0]
    for k, out_ref in enumerate(out_refs):
        i = chip ^ k
        out_ref[...] = (keep_ref[i].astype(F32) + got_ref[i].astype(F32)).astype(BF)


def chips_kernel(*refs):
    out_ref = refs[-1]
    n_e, _, pair = out_ref.shape
    width = pair // 2
    d = n_e * width
    total = refs[0][...].astype(F32)
    for r in refs[1:-1]:
        total = total + r[...].astype(F32)
    total = total.astype(BF)
    for e in range(n_e):
        out_ref[e, :, :width] = total[:, e * width : (e + 1) * width]
        out_ref[e, :, width:] = total[:, d + e * width : d + (e + 1) * width]


def home_kernel(got_ref, route_ref, gates_ref, mixed_ref, grad_ref):
    tok, width = mixed_ref.shape
    route = route_ref[...]
    gates = gates_ref[...]
    mixed = jnp.zeros((tok, width), F32)
    grad = jnp.zeros((tok, width), F32)
    for e in range(got_ref.shape[0]):
        rows = got_ref[e].astype(F32)[:tok]
        mixed = mixed + share(route, gates, e) * rows[:, :width]
        grad = grad + rows[:, width:]
    mixed_ref[...] = mixed.astype(BF)
    grad_ref[...] = grad.astype(BF)


def weight_grad(left, right, tile):
    rows, f = left.shape
    d = right.shape[1]
    return pl.pallas_call(
        weight_grad_kernel,
        grid=(f // tile,),
        in_specs=[
            pl.BlockSpec((rows, tile), lambda i: (0, i)),
            pl.BlockSpec((rows, d), lambda i: (0, 0)),
        ],
        out_specs=pl.BlockSpec((tile, d), lambda i: (i, 0)),
        out_shape=jax.ShapeDtypeStruct((f, d), BF),
        compiler_params=params(24),
        cost_estimate=pl.CostEstimate(
            flops=2 * rows * f * d, bytes_accessed=2 * f * d, transcendentals=0
        ),
        name="weight_grad",
    )(left, right)


def per_device(tokens, cotangent, route, gates, w_gate, w_up, w_down):
    n_dp = lax.axis_size("dp")
    n_e = lax.axis_size("expert")
    tok, width = tokens.shape
    d = width * n_e
    f = w_gate.shape[1]
    tile = 256 if f % 256 == 0 else f
    rows = n_dp * ROWS
    n_chip = n_dp // 2
    me = lax.axis_index("dp").astype(jnp.int32)
    parity = (me % 2).reshape(1)
    chip = (me // 2).reshape(1)
    sds = jax.ShapeDtypeStruct

    packed = pl.pallas_call(
        pack_kernel,
        in_specs=[VM] * 4,
        out_specs=VM,
        out_shape=sds((n_e, tok, 2 * width), BF),
        name="pack",
    )(tokens, cotangent, route, gates)
    packed = lax.all_to_all(packed, "expert", split_axis=0, concat_axis=0, tiled=True)
    got = lax.all_gather(packed, "dp", axis=0, tiled=False)

    weight_spec = pl.BlockSpec((None, tile, d), lambda i: (0, i, 0))
    unit_spec = pl.BlockSpec((rows, tile), lambda i: (0, i))
    keep, send, xs, dys, hidden, gpg, gpu = pl.pallas_call(
        expert_kernel,
        grid=(f // tile,),
        in_specs=[SM, VM] + [weight_spec] * 3,
        out_specs=[VM] * 4 + [unit_spec] * 3,
        out_shape=[sds((n_chip, ROWS, 2 * d), BF)] * 2
        + [sds((rows, d), BF)] * 2
        + [sds((rows, f), BF)] * 3,
        scratch_shapes=[pltpu.VMEM((rows, d), F32)] * 2,
        compiler_params=params(56),
        cost_estimate=pl.CostEstimate(
            flops=12 * rows * f * d, bytes_accessed=6 * f * d, transcendentals=rows * f
        ),
        name="expert",
    )(parity, got, w_gate, w_up, w_down)

    received = lax.ppermute(send, "dp", [(i, i ^ 1) for i in range(n_dp)])
    grad_down = weight_grad(hidden, dys, tile)
    grad_gate = weight_grad(gpg, xs, tile)
    grad_up = weight_grad(gpu, xs, tile)
    parts = pl.pallas_call(
        cores_kernel,
        in_specs=[SM, VM, VM],
        out_specs=[VM] * n_chip,
        out_shape=[sds((ROWS, 2 * d), BF)] * n_chip,
        name="cores",
    )(chip, keep, received)
    arrived = [
        lax.ppermute(parts[k], "dp", [(i, i ^ (2 * k)) for i in range(n_dp)])
        for k in range(1, n_chip)
    ]
    summed = pl.pallas_call(
        chips_kernel,
        in_specs=[VM] * n_chip,
        out_specs=VM,
        out_shape=sds((n_e, ROWS, 2 * width), BF),
        name="chips",
    )(parts[0], *arrived)
    home = lax.all_to_all(summed, "expert", split_axis=0, concat_axis=0, tiled=True)
    mixed, grad_tokens = pl.pallas_call(
        home_kernel,
        in_specs=[VM] * 3,
        out_specs=[VM] * 2,
        out_shape=[sds((tok, width), BF)] * 2,
        name="home",
    )(home, route, gates)
    return mixed, grad_tokens, grad_gate[None], grad_up[None], grad_down[None]


def solution(mesh):
    return jax.shard_map(
        per_device,
        mesh=mesh,
        in_specs=(
            P("dp", "expert"),
            P("dp", "expert"),
            P("dp", None),
            P("dp", None),
            P("expert", "dp", None),
            P("expert", "dp", None),
            P("expert", "dp", None),
        ),
        out_specs=(
            P("dp", "expert"),
            P("dp", "expert"),
            P("expert", "dp", None),
            P("expert", "dp", None),
            P("expert", "dp", None),
        ),
        check_vma=False,
    )
```

time: 169 us -> 86.9 us (0.51)
  blocking collectives: 71.1 us -> 12 us
  Pallas kernels: 0 us -> 39 us
  matrix products: 29.3 us -> 0 us
  other arithmetic: 24.7 us -> 0 us
  local copies, waits for them, and re-layouts: 13.4 us -> 6.87 us
  waiting for transfers between devices: 9.76 us -> 14.2 us
  starting transfers between devices: 17.9 us -> 13.6 us
    unnamed x1 -> x0, blocking collectives: 50.8 us -> none
    pallas_call x0 -> x8, Pallas kernels: none -> 39 us  [the longest x1 17.7 us: per_device(): pl.pallas_call(expert_kernel, grid=(f // tile,), in_specs=[SM, VM] + [wei...]
    dot_general x13 -> x0, matrix products: 29.3 us -> none  [the longest x3 13.6 us: contract_rows(): lax.dot_general(left, right, (((0,), (0,)), ((), ())), preferred_element_...]
    unnamed x4 -> x0, other arithmetic: 23.1 us -> none
    all_to_all x4 -> x2, starting transfers between devices: 17.9 us -> 9.64 us  [the longest x1 6.32 us: per_device(): lax.all_to_all(packed, 'expert', split_axis=0, concat_axis=0, tiled=True)]
    all_gather x2 -> x1, blocking collectives: 20.2 us -> 12 us  [per_device(): got = lax.all_gather(packed, 'dp', axis=0, tiled=False)]
    ppermute x0 -> x4, waiting for transfers between devices: none -> 8.16 us  [the longest x3 6.4 us: per_device(): lax.ppermute(parts[k], 'dp', [(i, i ^ 2 * k) for i in range(n_dp)])]
    ppermute x0 -> x4, starting transfers between devices: none -> 3.93 us  [the longest x3 3.5 us: per_device(): lax.ppermute(parts[k], 'dp', [(i, i ^ 2 * k) for i in range(n_dp)])]
  transfers between devices with their start and end apart: 4 -> 6, of which waited for: 3 -> 4; matrix products, arithmetic and copies ran while one was open for 15% -> 0% of each run, Pallas kernels for 0% -> 17%
where the time goes in v1:
time: 86.9 us; the launch traced here: 86.4 us
  Pallas kernels  39 us (45%)
  waiting for transfers between devices  14.2 us (16%)
  starting transfers between devices  13.6 us (16%)
  blocking collectives  12 us (14%)
  local copies, waits for them, and re-layouts  6.87 us (8%)
    pallas_call x1, Pallas kernels, per_device(): pl.pallas_call(expert_kernel, grid=(f // tile,), in_specs=[SM, VM] + [wei...  17.7 us
    pallas_call x3, Pallas kernels, weight_grad(): pl.pallas_call(weight_grad_kernel, grid=(f // tile,), in_specs=[pl.BlockS...  14.3 us
    all_gather x1, blocking collectives, per_device(): got = lax.all_gather(packed, 'dp', axis=0, tiled=False)  12 us
    unnamed x22, local copies, waits for them, and re-layouts  6.87 us
    ppermute x3, waiting for transfers between devices, per_device(): lax.ppermute(parts[k], 'dp', [(i, i ^ 2 * k) for i in range(n_dp)])  6.4 us
    all_to_all x1, starting transfers between devices, per_device(): lax.all_to_all(packed, 'expert', split_axis=0, concat_axis=0, tiled=True)  6.32 us
    all_to_all x1, waiting for transfers between devices, per_device(): lax.all_to_all(packed, 'expert', split_axis=0, concat_axis=0, tiled=True)  6.07 us
    ppermute x3, starting transfers between devices, per_device(): lax.ppermute(parts[k], 'dp', [(i, i ^ 2 * k) for i in range(n_dp)])  3.5 us
  transfers between devices with their start and end apart: 6, of which 4 were waited for; matrix products, arithmetic and copies ran while one was open for 0% of the time, Pallas kernels for 17%

profile of v1, /device:TPU:0, one launch (start us, length us, event | category | flops | bytes accessed | tf_op | source)
XLA Modules:
  0.0 86.4 jit_solution(8186306877704974269)
XLA Ops:
  0.6 1.4 %copy.16.route_ref = s32[12,2]{1,0:T(8,128)} copy(s32[12,2]{0,1:T(2,128)} %param.9) | data formatting | bytes 192 | tf_op args[2]
  2.0 1.4 %copy.17.gates_ref = f32[12,2]{1,0:T(8,128)} copy(f32[12,2]{0,1:T(2,128)} %param.10) | data formatting | bytes 192 | tf_op args[3]
  3.3 1.5 %pack.1 = bf16[4,12,1024]{2,1,0:T(8,128)(2,1)} custom-call(bf16[12,512]{1,0:T(8,128)(2,1)} %tok_ref.1, bf16[12,512]{1,0:T(8,128)(2,1)} %cot_ref.1, s32[12,2]{1,0:T(8,128)} %copy.16.route_ref, f32[12,2]{1,0:T(8,128)} %copy.17.gates_ref), custom_call_target="tpu_custom_call" | custom-call | tf_op jit(solution)/shard_map/pack/pallas_call | solution.py:172
  4.8 6.3 %all-to-all-start = ((bf16[4,12,1024]{2,1,0:T(8,128)(2,1)}), bf16[4,12,1024]{2,1,0:T(8,128)(2,1)S(1)}, u32[]{:S(2)}, u32[]{:S(2)}) async-start(bf16[4,12,1024]{2,1,0:T(8,128)(2,1)} %pack.1), calls=%async_computation | async-start | bytes 262144 | tf_op jit(solution)/shard_map/all_to_all | solution.py:179
  11.1 6.1 %all-to-all-done = bf16[4,12,1024]{2,1,0:T(8,128)(2,1)S(1)} async-done(((bf16[4,12,1024]{2,1,0:T(8,128)(2,1)}), bf16[4,12,1024]{2,1,0:T(8,128)(2,1)S(1)}, u32[]{:S(2)}, u32[]{:S(2)}) %all-to-all-start) | async-done | bytes 98336 | tf_op jit(solution)/shard_map/all_to_all | solution.py:179
  17.2 12.0 %all-gather = bf16[32,12,1024]{2,1,0:T(8,128)(2,1)} all-gather(bf16[4,12,1024]{2,1,0:T(8,128)(2,1)S(1)} %all-to-all-done), channel_id=2, replica_groups=mesh['dp'=8,'expert'=4] {'dp'}, dimensions={0}, use_global_device_ids=true | all-gather | bytes 884736 | tf_op jit(solution)/shard_map/all_gather | solution.py:180
  29.2 17.7 %expert.1 = (bf16[4,16,4096]{2,1,0:T(8,128)(2,1)}, bf16[4,16,4096]{2,1,0:T(8,128)(2,1)}, bf16[128,2048]{1,0:T(8,128)(2,1)}, bf16[128,2048]{1,0:T(8,128)(2,1)}, b...) custom-call(s32[1]{0:T(128)} %bitcast.1.parity_ref, ...), custom_call_target="tpu_custom_call" | custom-call | flops 4831838208 | bytes 18874368 | tf_op jit(solution)/shard_map/expert/pallas_call | solution.py:184
  46.9 0.0 copy-start.3
  46.9 0.4 collective-permute-start
  47.4 1.8 %collective-permute-done.got_ref = bf16[4,16,4096]{2,1,0:T(8,128)(2,1)S(1)} collective-permute-done((bf16[4,16,4096]{2,1,0:T(8,128)(2,1)}, bf16[4,16,4096]{2,1,0:T(8,128)(2,1)S(1)}, u32[]{:S(2)}, u32[]{:S(2)}) %collective-permute-start) | collective-permute-done | bytes 524320 | tf_op jit(solution)/shard_map/ppermute | solution.py:200
  49.1 0.0 copy-start.6
  49.1 0.8 copy-done.6
  49.9 2.0 %cores.1 = (bf16[16,4096]{1,0:T(8,128)(2,1)}, bf16[16,4096]{1,0:T(8,128)(2,1)}, bf16[16,4096]{1,0:T(8,128)(2,1)}, bf16[16,4096]{1,0:T(8,128)(2,1)}) custom-call(s32[1]{0:T(128)} %bitcast.chip_ref, bf16[4,16,4096]{2,1,0:T(8,128)(2,1)} %get-tuple-element.18.keep_ref, bf16[4,16,4096]{2,1,0:T(8,128)(2,1)} %copy-done.6), custom_call_target="tpu_custom_call" | custom-call | tf_op jit(solution)/shard_map/cores/pallas_call | solution.py:204
  52.0 1.4 %collective-permute-start.1 = (bf16[16,4096]{1,0:T(8,128)(2,1)}, bf16[16,4096]{1,0:T(8,128)(2,1)S(1)}, u32[]{:S(2)}, u32[]{:S(2)}) collective-permute-start(bf16[16,4096]{1,0:T(8,128)(2,1)} %get-tuple-element.21), channel_id=1, source_target_pairs={{0,8},{4,12},{8,0},{12,4},{16,24},{20,28},{24,16},{28,20},{1,9},{5... | collective-permute-start | bytes 393224 | tf_op jit(solution)/shard_map/ppermute | solution.py:212
  53.4 0.6 collective-permute-start.2
  54.0 1.5 %collective-permute-start.3 = (bf16[16,4096]{1,0:T(8,128)(2,1)}, bf16[16,4096]{1,0:T(8,128)(2,1)S(1)}, u32[]{:S(2)}, u32[]{:S(2)}) collective-permute-start(bf16[16,4096]{1,0:T(8,128)(2,1)} %get-tuple-element.23), channel_id=1, source_target_pairs={{0,24},{4,28},{8,16},{12,20},{16,8},{20,12},{24,0},{28,4},{1,25},{... | collective-permute-start | bytes 393224 | tf_op jit(solution)/shard_map/ppermute | solution.py:212
  55.5 2.9 %collective-permute-done.1.refs_1_ = bf16[16,4096]{1,0:T(8,128)(2,1)S(1)} collective-permute-done((bf16[16,4096]{1,0:T(8,128)(2,1)}, bf16[16,4096]{1,0:T(8,128)(2,1)S(1)}, u32[]{:S(2)}, u32[]{:S(2)}) %collective-permute-start.1) | collective-permute-done | bytes 131104 | tf_op jit(solution)/shard_map/ppermute | solution.py:212
  58.4 0.0 copy-start.7
  58.4 3.5 %collective-permute-done.2.refs_2_ = bf16[16,4096]{1,0:T(8,128)(2,1)S(1)} collective-permute-done((bf16[16,4096]{1,0:T(8,128)(2,1)}, bf16[16,4096]{1,0:T(8,128)(2,1)S(1)}, u32[]{:S(2)}, u32[]{:S(2)}) %collective-permute-start.2) | collective-permute-done | bytes 131104 | tf_op jit(solution)/shard_map/ppermute | solution.py:212
  61.9 0.0 copy-start.8
  61.9 0.0 collective-permute-done.3.refs_3_
  61.9 0.0 copy-start.9
  61.9 0.0 copy-done.7
  61.9 0.6 copy-done.8
  62.5 0.0 copy-done.9
  62.5 1.8 %chips.1 = bf16[4,16,1024]{2,1,0:T(8,128)(2,1)} custom-call(bf16[16,4096]{1,0:T(8,128)(2,1)} %get-tuple-element.20.refs_0_, bf16[16,4096]{1,0:T(8,128)(2,1)} %copy-done.7, bf16[16,4096]{1,0:T(8,128)(2,1)} %copy-done.8, bf16[16,4096]{1,0:T(8,128)(2,1)} %copy-done.9), custom_call_target="tpu_custom_call" | custom-call | tf_op jit(solution)/shard_map/chips/pallas_call | solution.py:215
  64.4 3.3 %all-to-all-start.1 = ((bf16[4,16,1024]{2,1,0:T(8,128)(2,1)}), bf16[4,16,1024]{2,1,0:T(8,128)(2,1)S(1)}, u32[]{:S(2)}, u32[]{:S(2)}) async-start(bf16[4,16,1024]{2,1,0:T(8,128)(2,1)} %chips.1), calls=%async_computation.1 | async-start | bytes 262144 | tf_op jit(solution)/shard_map/all_to_all | solution.py:222
  67.7 0.0 copy-start
  67.7 1.0 %copy-done = bf16[128,2048]{1,0:T(8,128)(2,1)S(1)} copy-done((bf16[128,2048]{1,0:T(8,128)(2,1)S(1)}, bf16[128,2048]{1,0:T(8,128)(2,1)}, u32[]{:S(2)}) %copy-start) | copy-done | bytes 524312
  68.7 0.0 copy-start.4
  68.7 1.0 %copy-done.4 = bf16[128,1536]{1,0:T(8,128)(2,1)S(1)} copy-done((bf16[128,1536]{1,0:T(8,128)(2,1)S(1)}, bf16[128,1536]{1,0:T(8,128)(2,1)}, u32[]{:S(2)}) %copy-start.4) | copy-done | bytes 393240
  69.7 0.0 copy-start.1
  69.7 0.0 copy-start.2
  69.7 4.8 %weight_grad.3 = bf16[1536,2048]{1,0:T(8,128)(2,1)} custom-call(bf16[128,1536]{1,0:T(8,128)(2,1)S(1)} %copy-done.4, bf16[128,2048]{1,0:T(8,128)(2,1)S(1)} %copy-done), custom_call_target="tpu_custom_call" | custom-call | flops 805306368 | bytes 6291456 | tf_op jit(solution)/shard_map/weight_grad/pallas_call | solution.py:141
  74.5 0.0 copy-done.3
  74.5 4.8 %weight_grad.4 = bf16[1536,2048]{1,0:T(8,128)(2,1)} custom-call(bf16[128,1536]{1,0:T(8,128)(2,1)S(1)} %copy-done.3, bf16[128,2048]{1,0:T(8,128)(2,1)S(1)} %copy-done), custom_call_target="tpu_custom_call" | custom-call | flops 805306368 | bytes 6291456 | tf_op jit(solution)/shard_map/weight_grad/pallas_call | solution.py:141
  79.3 0.0 copy-done.1
  79.3 0.0 copy-done.2
  79.3 4.8 %weight_grad.5 = bf16[1536,2048]{1,0:T(8,128)(2,1)} custom-call(bf16[128,1536]{1,0:T(8,128)(2,1)S(1)} %copy-done.2, bf16[128,2048]{1,0:T(8,128)(2,1)S(1)} %copy-done.1), custom_call_target="tpu_custom_call" | custom-call | flops 805306368 | bytes 6291456 | tf_op jit(solution)/shard_map/weight_grad/pallas_call | solution.py:141
  84.1 0.0 all-to-all-done.1.got_ref
  84.1 0.0 copy-start.5
  84.1 0.6 copy-done.5
  84.7 1.6 %home.1 = (bf16[12,512]{1,0:T(8,128)(2,1)}, bf16[12,512]{1,0:T(8,128)(2,1)}) custom-call(bf16[4,16,1024]{2,1,0:T(8,128)(2,1)} %copy-done.5, s32[12,2]{1,0:T(8,128)} %copy.16.route_ref, f32[12,2]{1,0:T(8,128)} %copy.17.gates_ref), custom_call_target="tpu_custom_call" | custom-call | tf_op jit(solution)/shard_map/home/pallas_call | solution.py:223
Async XLA Ops:
  4.8 12.4 %all-to-all-start = ((bf16[4,12,1024]{2,1,0:T(8,128)(2,1)}), bf16[4,12,1024]{2,1,0:T(8,128)(2,1)S(1)}, u32[]{:S(2)}, u32[]{:S(2)}) async-start(bf16[4,12,1024]{2,1,0:T(8,128)(2,1)} %pack.1), calls=%async_computation | async-start | bytes 262144 | tf_op jit(solution)/shard_map/all_to_all | solution.py:179
  46.9 27.6 %copy-start.3 = (bf16[128,1536]{1,0:T(8,128)(2,1)S(1)}, bf16[128,1536]{1,0:T(8,128)(2,1)}, u32[]{:S(2)}) copy-start(bf16[128,1536]{1,0:T(8,128)(2,1)} %get-tuple-element.28.left_ref) | copy-start | bytes 1179652
  46.9 2.2 %collective-permute-start = (bf16[4,16,4096]{2,1,0:T(8,128)(2,1)}, bf16[4,16,4096]{2,1,0:T(8,128)(2,1)S(1)}, u32[]{:S(2)}, u32[]{:S(2)}) collective-permute-start(bf16[4,16,4096]{2,1,0:T(8,128)(2,1)} %get-tuple-element.19), channel_id=1, source_target_pairs={{0,4},{4,0},{8,12},{12,8},{16,20},{20,16},{24,28},{28,24},{1,5},{5... | collective-permute-start | bytes 1572872 | tf_op jit(solution)/shard_map/ppermute | solution.py:200
  49.1 0.8 copy-start.6
  52.0 6.4 %collective-permute-start.1 = (bf16[16,4096]{1,0:T(8,128)(2,1)}, bf16[16,4096]{1,0:T(8,128)(2,1)S(1)}, u32[]{:S(2)}, u32[]{:S(2)}) collective-permute-start(bf16[16,4096]{1,0:T(8,128)(2,1)} %get-tuple-element.21), channel_id=1, source_target_pairs={{0,8},{4,12},{8,0},{12,4},{16,24},{20,28},{24,16},{28,20},{1,9},{5... | collective-permute-start | bytes 393224 | tf_op jit(solution)/shard_map/ppermute | solution.py:212
  53.4 8.5 %collective-permute-start.2 = (bf16[16,4096]{1,0:T(8,128)(2,1)}, bf16[16,4096]{1,0:T(8,128)(2,1)S(1)}, u32[]{:S(2)}, u32[]{:S(2)}) collective-permute-start(bf16[16,4096]{1,0:T(8,128)(2,1)} %get-tuple-element.22), channel_id=1, source_target_pairs={{0,16},{4,20},{8,24},{12,28},{16,0},{20,4},{24,8},{28,12},{1,17},{... | collective-permute-start | bytes 393224 | tf_op jit(solution)/shard_map/ppermute | solution.py:212
  54.0 7.9 %collective-permute-start.3 = (bf16[16,4096]{1,0:T(8,128)(2,1)}, bf16[16,4096]{1,0:T(8,128)(2,1)S(1)}, u32[]{:S(2)}, u32[]{:S(2)}) collective-permute-start(bf16[16,4096]{1,0:T(8,128)(2,1)} %get-tuple-element.23), channel_id=1, source_target_pairs={{0,24},{4,28},{8,16},{12,20},{16,8},{20,12},{24,0},{28,4},{1,25},{... | collective-permute-start | bytes 393224 | tf_op jit(solution)/shard_map/ppermute | solution.py:212
  58.4 3.5 %copy-start.7 = (bf16[16,4096]{1,0:T(8,128)(2,1)}, bf16[16,4096]{1,0:T(8,128)(2,1)S(1)}, u32[]{:S(2)}) copy-start(bf16[16,4096]{1,0:T(8,128)(2,1)S(1)} %collective-permute-done.1.refs_1_) | copy-start | bytes 393220
  61.9 0.7 copy-start.8
  61.9 0.7 copy-start.9
  64.4 19.7 %all-to-all-start.1 = ((bf16[4,16,1024]{2,1,0:T(8,128)(2,1)}), bf16[4,16,1024]{2,1,0:T(8,128)(2,1)S(1)}, u32[]{:S(2)}, u32[]{:S(2)}) async-start(bf16[4,16,1024]{2,1,0:T(8,128)(2,1)} %chips.1), calls=%async_computation.1 | async-start | bytes 262144 | tf_op jit(solution)/shard_map/all_to_all | solution.py:222
  67.7 1.0 %copy-start = (bf16[128,2048]{1,0:T(8,128)(2,1)S(1)}, bf16[128,2048]{1,0:T(8,128)(2,1)}, u32[]{:S(2)}) copy-start(bf16[128,2048]{1,0:T(8,128)(2,1)} %get-tuple-element.27.right_ref) | copy-start | bytes 1572868
  68.7 1.0 %copy-start.4 = (bf16[128,1536]{1,0:T(8,128)(2,1)S(1)}, bf16[128,1536]{1,0:T(8,128)(2,1)}, u32[]{:S(2)}) copy-start(bf16[128,1536]{1,0:T(8,128)(2,1)} %get-tuple-element.26.left_ref) | copy-start | bytes 1179652
  69.7 9.6 %copy-start.1 = (bf16[128,2048]{1,0:T(8,128)(2,1)S(1)}, bf16[128,2048]{1,0:T(8,128)(2,1)}, u32[]{:S(2)}) copy-start(bf16[128,2048]{1,0:T(8,128)(2,1)} %get-tuple-element.30.right_ref) | copy-start | bytes 1572868
  69.7 9.6 %copy-start.2 = (bf16[128,1536]{1,0:T(8,128)(2,1)S(1)}, bf16[128,1536]{1,0:T(8,128)(2,1)}, u32[]{:S(2)}) copy-start(bf16[128,1536]{1,0:T(8,128)(2,1)} %get-tuple-element.29.left_ref) | copy-start | bytes 1179652
  84.1 0.6 copy-start.5

commit v2 on v1

v2 whole, which is shorter than its diff:
```python
import functools

import jax
import jax.numpy as jnp
from jax import lax
from jax.experimental import pallas as pl
from jax.experimental.pallas import tpu as pltpu
from jax.sharding import PartitionSpec as P

BF = jnp.bfloat16
F32 = jnp.float32
VM = pl.BlockSpec(memory_space=pltpu.VMEM)
HBM = pl.BlockSpec(memory_space=pltpu.HBM)
ANY = pl.BlockSpec(memory_space=pl.ANY)
ROWS = 16


def dot_nn(a, b):
    return lax.dot_general(a, b, (((1,), (0,)), ((), ())), preferred_element_type=F32)


def dot_nt(a, b):
    return lax.dot_general(a, b, (((1,), (1,)), ((), ())), preferred_element_type=F32)


def dot_tn(a, b):
    return lax.dot_general(a, b, (((0,), (0,)), ((), ())), preferred_element_type=F32)


def share(route, gates, expert):
    tok = route.shape[1]
    row = jnp.sum(jnp.where(route == expert, gates, 0.0), axis=0, keepdims=True)
    square = jnp.broadcast_to(row, (tok, tok))
    diagonal = lax.broadcasted_iota(jnp.int32, (tok, tok), 0) == lax.broadcasted_iota(
        jnp.int32, (tok, tok), 1
    )
    return jnp.sum(jnp.where(diagonal, square, 0.0), axis=1, keepdims=True)


def params(mib):
    return pltpu.CompilerParams(vmem_limit_bytes=mib << 20)


def pack_kernel(
    tok_hbm, cot_hbm, route_hbm, gates_hbm, *refs
):
    outs, (tok_ref, cot_ref, route_ref, gates_ref, sems) = refs[:-5], refs[-5:]
    pairs = (
        (tok_hbm, tok_ref), (cot_hbm, cot_ref), (route_hbm, route_ref), (gates_hbm, gates_ref)
    )
    copies = [pltpu.make_async_copy(a, b, sems.at[i]) for i, (a, b) in enumerate(pairs)]
    for copy in copies:
        copy.start()
    for copy in copies:
        copy.wait()
    tok, width = tok_ref.shape
    token_rows = tok_ref[...]
    cot = cot_ref[...].astype(F32)
    route = route_ref[...]
    gates = gates_ref[...]
    me = lax.axis_index("expert")
    for k, out_ref in enumerate(outs):
        out_ref[...] = jnp.zeros_like(out_ref)
        out_ref[:tok, :width] = token_rows
        out_ref[:tok, width:] = (share(route, gates, me ^ k) * cot).astype(BF)


def load_kernel(after_ref, *refs):
    n = (len(refs) - 1) // 2
    sems = refs[-1]
    copies = [pltpu.make_async_copy(refs[i], refs[n + i], sems.at[i]) for i in range(n)]
    for copy in copies:
        copy.start()
    for copy in copies:
        copy.wait()


def join_kernel(*refs):
    ins, out_ref = refs[:-1], refs[-1]
    width = ins[0].shape[1] // 2
    d = len(ins) * width
    me = lax.axis_index("expert")
    for e in range(len(ins)):
        for k, ref in enumerate(ins):

            @pl.when(me ^ k == e)
            def _(e=e, ref=ref):
                out_ref[:, e * width : (e + 1) * width] = ref[:, :width]
                out_ref[:, d + e * width : d + (e + 1) * width] = ref[:, width:]


def stack_kernel(*refs):
    out_ref = refs[-1]
    for k, ref in enumerate(refs[:-1]):
        out_ref[k * ROWS : (k + 1) * ROWS] = ref[...]


def expert_kernel(
    near_ref, far_ref, wg_ref, wu_ref, wd_ref,
    keep_ref, send_ref, xs_ref, dys_ref, hidt_ref, gpgt_ref, gput_ref,
    hid_ref, gpg_ref, gpu_ref,
    *, tile, cols,
):
    half = near_ref.shape[0]
    f, d = wg_ref.shape
    xs_ref[:half] = near_ref[:, :d]
    xs_ref[half:] = far_ref[:, :d]
    dys_ref[:half] = near_ref[:, d:]
    dys_ref[half:] = far_ref[:, d:]
    xs = xs_ref[...]
    dys = dys_ref[...]
    for i in range(f // tile):
        units = slice(i * tile, (i + 1) * tile)
        pre_gate = dot_nt(xs, wg_ref[units, :])
        pre_up = dot_nt(xs, wu_ref[units, :])
        grad_hidden = dot_nt(dys, wd_ref[units, :])
        sig = jax.nn.sigmoid(pre_gate)
        silu = pre_gate * sig
        hidden = (silu * pre_up).astype(BF)
        gpg = (grad_hidden * pre_up * sig * (1.0 + pre_gate * (1.0 - sig))).astype(BF)
        gpu = (grad_hidden * silu).astype(BF)
        hid_ref[:, units] = hidden
        gpg_ref[:, units] = gpg
        gpu_ref[:, units] = gpu
        hidt_ref[units, :] = hidden.T
        gpgt_ref[units, :] = gpg.T
        gput_ref[units, :] = gpu.T
    hidden = hid_ref[...]
    gpg = gpg_ref[...]
    gpu = gpu_ref[...]
    for j in range(d // cols):
        part = slice(j * cols, (j + 1) * cols)
        out = dot_nn(hidden, wd_ref[:, part]).astype(BF)
        grad = (dot_nn(gpg, wg_ref[:, part]) + dot_nn(gpu, wu_ref[:, part])).astype(BF)
        for at, value in ((j * cols, out), (d + j * cols, grad)):
            keep_ref[:, at : at + cols] = value[:half]
            send_ref[:, at : at + cols] = value[half:]


def grads_kernel(jobs, n, n_old, *refs):
    lefts, rights = refs[:n], refs[n : 2 * n]
    outs, (buf, sems) = refs[2 * n + n_old : 3 * n + n_old], refs[3 * n + n_old :]
    slots = buf.shape[0]
    copies = []
    for i, (a, start, size) in enumerate(jobs):
        slot = i % slots
        if i >= slots:
            copies[i - slots].wait()
        rows = pl.ds(start, size)
        buf[slot, :size] = dot_nn(lefts[a][rows, :], rights[a][...]).astype(BF)
        copy = pltpu.make_async_copy(buf.at[slot, pl.ds(0, size)], outs[a].at[rows, :], sems.at[slot])
        copy.start()
        copies.append(copy)
    for copy in copies[-slots:]:
        copy.wait()


def cores_kernel(keep_ref, got_ref, *out_refs):
    for k, out_ref in enumerate(out_refs):
        rows = slice(k * ROWS, (k + 1) * ROWS)
        out_ref[...] = (keep_ref[rows].astype(F32) + got_ref[rows].astype(F32)).astype(BF)


def chips_kernel(n, *refs):
    ins, outs = refs[:n], refs[n:]
    width = outs[0].shape[1] // 2
    d = len(outs) * width
    total = ins[0][...].astype(F32)
    for ref in ins[1:]:
        total = total + ref[...].astype(F32)
    total = total.astype(BF)
    me = lax.axis_index("expert")
    for e in range(len(outs)):
        for k, out_ref in enumerate(outs):

            @pl.when(me ^ k == e)
            def _(e=e, out_ref=out_ref):
                out_ref[:, :width] = total[:, e * width : (e + 1) * width]
                out_ref[:, width:] = total[:, d + e * width : d + (e + 1) * width]


def home_kernel(*refs):
    ins, (route_ref, gates_ref, mixed_ref, grad_ref) = refs[:-4], refs[-4:]
    tok, width = mixed_ref.shape
    route = route_ref[...]
    gates = gates_ref[...]
    mixed = jnp.zeros((tok, width), F32)
    grad = jnp.zeros((tok, width), F32)
    me = lax.axis_index("expert")
    for k, ref in enumerate(ins):
        got = ref[...].astype(F32)[:tok]
        mixed = mixed + share(route, gates, me ^ k) * got[:, :width]
        grad = grad + got[:, width:]
    mixed_ref[...] = mixed.astype(BF)
    grad_ref[...] = grad.astype(BF)


def grads(jobs, lefts, rights, old):
    n = len(lefts)
    f, rows = lefts[0].shape
    d = rights[0].shape[1]
    kept = [a for a in range(n) if old[a] is not None]
    size = max(job[2] for job in jobs)
    done = sum(job[2] for job in jobs)
    return pl.pallas_call(
        functools.partial(grads_kernel, jobs, n, len(kept)),
        in_specs=[VM] * (2 * n) + [HBM] * len(kept),
        out_specs=[HBM] * n,
        out_shape=[jax.ShapeDtypeStruct((f, d), BF)] * n,
        scratch_shapes=[pltpu.VMEM((3, size, d), BF), pltpu.SemaphoreType.DMA((3,))],
        input_output_aliases={2 * n + i: a for i, a in enumerate(kept)},
        compiler_params=params(((6 * size * d + n * 2 * rows * (f + d)) >> 20) + 4),
        cost_estimate=pl.CostEstimate(
            flops=2 * rows * done * d, bytes_accessed=3 * done * d, transcendentals=0
        ),
        name="grads",
    )(*lefts, *rights, *[old[a] for a in kept])


def load(mib, after, *arrays):
    size = sum(a.size for a in arrays) * 2
    return pl.pallas_call(
        load_kernel,
        in_specs=[ANY] + [HBM] * len(arrays),
        out_specs=[VM] * len(arrays),
        out_shape=[jax.ShapeDtypeStruct(a.shape, a.dtype) for a in arrays],
        scratch_shapes=[pltpu.SemaphoreType.DMA((len(arrays),))],
        compiler_params=params(mib),
        cost_estimate=pl.CostEstimate(flops=0, bytes_accessed=size, transcendentals=0),
        name="load",
    )(after, *arrays)


def stack(kernel, arrays, shape, name):
    size = 2 * sum(a.size for a in arrays)
    return pl.pallas_call(
        kernel,
        in_specs=[VM] * len(arrays),
        out_specs=VM,
        out_shape=jax.ShapeDtypeStruct(shape, BF),
        compiler_params=params((size >> 19) + 2),
        name=name,
    )(*arrays)


def per_device(tokens, cotangent, route, gates, w_gate, w_up, w_down):
    n_dp = lax.axis_size("dp")
    n_e = lax.axis_size("expert")
    tok, width = tokens.shape
    d = width * n_e
    f = w_gate.shape[1]
    tile = 256 if f % 256 == 0 else f
    rows = n_dp * ROWS
    n_chip = n_dp // 2
    sds = jax.ShapeDtypeStruct

    def swap(x, axis, size, k):
        return lax.ppermute(x, axis, [(i, i ^ k) for i in range(size)])

    small = n_chip + 4
    packed = pl.pallas_call(
        pack_kernel,
        in_specs=[HBM] * 4,
        out_specs=[VM] * n_e,
        out_shape=[sds((ROWS, 2 * width), BF)] * n_e,
        scratch_shapes=[
            pltpu.VMEM(tokens.shape, BF),
            pltpu.VMEM(tokens.shape, BF),
            pltpu.VMEM((2, tok), jnp.int32),
            pltpu.VMEM((2, tok), F32),
            pltpu.SemaphoreType.DMA((4,)),
        ],
        name="pack",
    )(tokens, cotangent, route.T, gates.T)
    mine = [packed[0]] + [swap(packed[k], "expert", n_e, k) for k in range(1, n_e)]
    weight_mib = f * d >> 19
    (wg,) = load(weight_mib + 3, packed[0], w_gate[0])
    mine, wg = lax.optimization_barrier((mine, wg))
    block = stack(join_kernel, mine, (ROWS, 2 * d), "join")
    blocks = [block] + [swap(block, "dp", n_dp, 2 * k) for k in range(1, n_chip)]
    wu, wd = load(2 * weight_mib + 3, block, w_up[0], w_down[0])
    blocks, wu, wd = lax.optimization_barrier((blocks, wu, wd))
    near = stack(stack_kernel, blocks, (n_chip * ROWS, 2 * d), "stack")
    far = swap(near, "dp", n_dp, 1)

    held = 2 * f * d + rows * (16 * d + 12 * f)
    keep, send, xs, dys, hidden, gpg, gpu = pl.pallas_call(
        functools.partial(expert_kernel, tile=tile, cols=256),
        in_specs=[VM] * 5,
        out_specs=[VM] * 7,
        out_shape=[sds((n_chip * ROWS, 2 * d), BF)] * 2
        + [sds((rows, d), BF)] * 2
        + [sds((f, rows), BF)] * 3,
        scratch_shapes=[pltpu.VMEM((rows, f), BF)] * 3,
        compiler_params=params((held >> 20) + 4),
        cost_estimate=pl.CostEstimate(
            flops=12 * rows * f * d, bytes_accessed=6 * f * d, transcendentals=rows * f
        ),
        name="expert",
    )(near, far, wg, wu, wd)

    received = swap(send, "dp", n_dp, 1)
    third = f // 3
    whole = [(1, i * third, third) for i in range(3)]
    (down,) = grads([(0, 0, third)], [hidden], [dys], [None])
    received, down = lax.optimization_barrier((received, down))
    parts = pl.pallas_call(
        cores_kernel,
        in_specs=[VM, VM],
        out_specs=[VM] * n_chip,
        out_shape=[sds((ROWS, 2 * d), BF)] * n_chip,
        compiler_params=params(small),
        name="cores",
    )(keep, received)
    arrived = [swap(parts[k], "dp", n_dp, 2 * k) for k in range(1, n_chip)]
    down, grad_gate = grads([(0, third, third)] + whole, [hidden, gpg], [dys, xs], [down, None])
    arrived, down, grad_gate = lax.optimization_barrier((arrived, down, grad_gate))
    summed = pl.pallas_call(
        functools.partial(chips_kernel, n_chip),
        in_specs=[VM] * n_chip,
        out_specs=[VM] * n_e,
        out_shape=[sds((ROWS, 2 * width), BF)] * n_e,
        compiler_params=params(small),
        name="chips",
    )(parts[0], *arrived)
    home = [summed[0]] + [swap(summed[k], "expert", n_e, k) for k in range(1, n_e)]
    grad_down, grad_up = grads(
        [(0, 2 * third, third)] + whole, [hidden, gpu], [dys, xs], [down, None]
    )
    home, grad_down, grad_up = lax.optimization_barrier((home, grad_down, grad_up))
    mixed, grad_tokens = pl.pallas_call(
        home_kernel,
        in_specs=[VM] * (n_e + 2),
        out_specs=[VM] * 2,
        out_shape=[sds((tok, width), BF)] * 2,
        compiler_params=params(4),
        name="home",
    )(*home, route.T, gates.T)
    return mixed, grad_tokens, grad_gate[None], grad_up[None], grad_down[None]


def solution(mesh):
    return jax.shard_map(
        per_device,
        mesh=mesh,
        in_specs=(
            P("dp", "expert"),
            P("dp", "expert"),
            P("dp", None),
            P("dp", None),
            P("expert", "dp", None),
            P("expert", "dp", None),
            P("expert", "dp", None),
        ),
        out_specs=(
            P("dp", "expert"),
            P("dp", "expert"),
            P("expert", "dp", None),
            P("expert", "dp", None),
            P("expert", "dp", None),
        ),
        check_vma=False,
    )
```

time: 86.9 us -> 54.7 us (0.63)
  Pallas kernels: 39 us -> 22.9 us
  blocking collectives: 12 us -> 0 us
  waiting for transfers between devices: 14.2 us -> 9.64 us
  starting transfers between devices: 13.6 us -> 17.5 us
  local copies, waits for them, and re-layouts: 6.87 us -> 3.56 us
    pallas_call x8 -> x12, Pallas kernels: 39 us -> 22.9 us  [the longest x3 10.1 us: grads(): pl.pallas_call(functools.partial(grads_kernel, jobs, n, len(kept)), in_sp...]
    ppermute x4 -> x14, starting transfers between devices: 3.93 us -> 17.5 us  [swap(): return lax.ppermute(x, axis, [(i, i ^ k) for i in range(size)])]
    all_gather x1 -> x0, blocking collectives: 12 us -> none  [per_device(): got = lax.all_gather(packed, 'dp', axis=0, tiled=False)]
    all_to_all x2 -> x0, starting transfers between devices: 9.64 us -> none  [the longest x1 6.32 us: per_device(): lax.all_to_all(packed, 'expert', split_axis=0, concat_axis=0, tiled=True)]
    all_to_all x2 -> x0, waiting for transfers between devices: 6.08 us -> none  [the longest x1 6.07 us: per_device(): lax.all_to_all(packed, 'expert', split_axis=0, concat_axis=0, tiled=True)]
    unnamed x22 -> x12, local copies, waits for them, and re-layouts: 6.87 us -> 3.56 us
    ppermute x4 -> x14, waiting for transfers between devices: 8.16 us -> 9.64 us  [swap(): return lax.ppermute(x, axis, [(i, i ^ k) for i in range(size)])]
  transfers between devices with their start and end apart: 6 -> 14, of which waited for: 4 -> 6; matrix products, arithmetic and copies ran while one was open for 0% -> 0% of each run, Pallas kernels for 17% -> 21%
where the time goes in v2:
time: 54.7 us; the launch traced here: 54.4 us
  Pallas kernels  22.9 us (42%)
  starting transfers between devices  17.5 us (32%)
  waiting for transfers between devices  9.64 us (18%)
  local copies, waits for them, and re-layouts  3.56 us (7%)
  between operations  0.82 us (1%)
    ppermute x14, starting transfers between devices, swap(): return lax.ppermute(x, axis, [(i, i ^ k) for i in range(size)])  17.5 us
    pallas_call x3, Pallas kernels, grads(): pl.pallas_call(functools.partial(grads_kernel, jobs, n, len(kept)), in_sp...  10.1 us
    ppermute x14, waiting for transfers between devices, swap(): return lax.ppermute(x, axis, [(i, i ^ k) for i in range(size)])  9.64 us
    pallas_call x1, Pallas kernels, per_device(): pl.pallas_call(functools.partial(expert_kernel, tile=tile, cols=256), in_...  8.71 us
    unnamed x12, local copies, waits for them, and re-layouts  3.56 us
    pallas_call x1, Pallas kernels, per_device(): pl.pallas_call(pack_kernel, in_specs=[HBM] * 4, out_specs=[VM] * n_e, out...  1.51 us
    pallas_call x2, Pallas kernels, load(): pl.pallas_call(load_kernel, in_specs=[ANY] + [HBM] * len(arrays), out_spe...  1.28 us
  transfers between devices with their start and end apart: 14, of which 6 were waited for; matrix products, arithmetic and copies ran while one was open for 0% of the time, Pallas kernels for 21%

profile of v2, /device:TPU:0, one launch (start us, length us, event | category | flops | bytes accessed | tf_op | source)
XLA Modules:
  0.0 54.4 jit_solution(12728190017496013145)
XLA Ops:
  0.6 1.5 %pack.1 = (bf16[16,1024]{1,0:T(8,128)(2,1)}, bf16[16,1024]{1,0:T(8,128)(2,1)}, bf16[16,1024]{1,0:T(8,128)(2,1)}, bf16[16,1024]{1,0:T(8,128)(2,1)}) custom-call(bf16[12,512]{1,0:T(8,128)(2,1)} %tok_hbm.1, bf16[12,512]{1,0:T(8,128)(2,1)} %cot_hbm.1, s32[2,12]{1,0:T(2,128)} %bitcast.11, f32[2,12]{1,0:T(2,128)} %bitcast.13), custom_call_target="tpu_custom_call" | custom-call | tf_op jit(solution)/shard_map/pack/pallas_call | solution.py:261
  2.1 3.1 %collective-permute-start = (bf16[16,1024]{1,0:T(8,128)(2,1)}, bf16[16,1024]{1,0:T(8,128)(2,1)S(1)}, u32[]{:S(2)}, u32[]{:S(2)}) collective-permute-start(bf16[16,1024]{1,0:T(8,128)(2,1)} %get-tuple-element.57), channel_id=1, source_target_pairs={{0,1},{1,0},{2,3},{3,2},{4,5},{5,4},{6,7},{7,6},{8,9},{9,8},{10,11... | collective-permute-start | bytes 98312 | tf_op jit(solution)/shard_map/ppermute | solution.py:258
  5.2 2.6 %collective-permute-start.1 = (bf16[16,1024]{1,0:T(8,128)(2,1)}, bf16[16,1024]{1,0:T(8,128)(2,1)S(1)}, u32[]{:S(2)}, u32[]{:S(2)}) collective-permute-start(bf16[16,1024]{1,0:T(8,128)(2,1)} %get-tuple-element.58), channel_id=1, source_target_pairs={{0,2},{1,3},{2,0},{3,1},{4,6},{5,7},{6,4},{7,5},{8,10},{9,11},{10,... | collective-permute-start | bytes 98312 | tf_op jit(solution)/shard_map/ppermute | solution.py:258
  7.8 0.0 collective-permute-start.2
  7.8 0.0 copy-start
  7.8 2.8 %copy-done = bf16[1,1536,2048]{2,1,0:T(8,128)(2,1)S(1)} copy-done((bf16[1,1536,2048]{2,1,0:T(8,128)(2,1)S(1)}, bf16[1,1536,2048]{2,1,0:T(8,128)(2,1)}, u32[]{:S(2)}) %copy-start) | copy-done | bytes 6291480
  10.6 0.0 copy-start.3
  10.6 0.8 %copy-done.3 = bf16[16,1024]{1,0:T(8,128)(2,1)S(1)} copy-done((bf16[16,1024]{1,0:T(8,128)(2,1)S(1)}, bf16[16,1024]{1,0:T(8,128)(2,1)}, u32[]{:S(2)}) %copy-start.3) | copy-done | bytes 32792
  11.4 0.0 copy-start.1
  11.4 0.0 copy-start.2
  11.4 0.4 load.2.wg_ref
  11.8 0.0 collective-permute-done.refs_1_
  11.8 0.0 collective-permute-done.1.refs_2_
  11.8 1.9 %collective-permute-done.2.refs_3_ = bf16[16,1024]{1,0:T(8,128)(2,1)S(1)} collective-permute-done((bf16[16,1024]{1,0:T(8,128)(2,1)}, bf16[16,1024]{1,0:T(8,128)(2,1)S(1)}, u32[]{:S(2)}, u32[]{:S(2)}) %collective-permute-start.2) | collective-permute-done | bytes 32800 | tf_op jit(solution)/shard_map/ppermute | solution.py:258
  13.8 2.5 %collective-permute-start.5 = (bf16[16,4096]{1,0:T(8,128)(2,1)S(1)}, bf16[16,4096]{1,0:T(8,128)(2,1)S(1)}, u32[]{:S(2)}, u32[]{:S(2)}) collective-permute-start(bf16[16,4096]{1,0:T(8,128)(2,1)S(1)} %join.1.after_ref.refs_0_), channel_id=1, source_target_pairs={{0,24},{4,28},{8,16},{12,20},{16,8},{20,12},{24,0},{28,4},{1,25},{... | collective-permute-start | bytes 393224 | tf_op jit(solution)/shard_map/ppermute | solution.py:258
  16.3 0.5 collective-permute-start.4
  16.8 0.5 collective-permute-start.3
  17.3 0.0 copy-done.1
  17.3 0.0 copy-done.2
  17.3 0.9 %load.3 = (bf16[1536,2048]{1,0:T(8,128)(2,1)S(1)}, bf16[1536,2048]{1,0:T(8,128)(2,1)S(1)}) custom-call(bf16[16,4096]{1,0:T(8,128)(2,1)S(1)} %join.1.after_ref.refs_0_, bf16[1536,2048]{1,0:T(8,128)(2,1)S(1)} %bitcast.9, bf16[1536,2048]{1,0:T(8,128)(2,1)S(1)} %bitcast.10), custom_call_target="tpu_custom_call" | custom-call | bytes 12582912 | tf_op jit(solution)/shard_map/load/pallas_call | solution.py:222
  18.2 2.7 %collective-permute-done.5.refs_3_ = bf16[16,4096]{1,0:T(8,128)(2,1)S(1)} collective-permute-done((bf16[16,4096]{1,0:T(8,128)(2,1)S(1)}, bf16[16,4096]{1,0:T(8,128)(2,1)S(1)}, u32[]{:S(2)}, u32[]{:S(2)}) %collective-permute-start.5) | collective-permute-done | bytes 131104 | tf_op jit(solution)/shard_map/ppermute | solution.py:258
  20.9 1.0 %collective-permute-done.4.refs_2_ = bf16[16,4096]{1,0:T(8,128)(2,1)S(1)} collective-permute-done((bf16[16,4096]{1,0:T(8,128)(2,1)S(1)}, bf16[16,4096]{1,0:T(8,128)(2,1)S(1)}, u32[]{:S(2)}, u32[]{:S(2)}) %collective-permute-start.4) | collective-permute-done | bytes 131104 | tf_op jit(solution)/shard_map/ppermute | solution.py:258
  21.9 0.0 collective-permute-done.3.refs_1_
  21.9 0.1 collective-permute-start.6
  22.0 1.9 %collective-permute-done.6.far_ref = bf16[64,4096]{1,0:T(8,128)(2,1)S(1)} collective-permute-done((bf16[64,4096]{1,0:T(8,128)(2,1)S(1)}, bf16[64,4096]{1,0:T(8,128)(2,1)S(1)}, u32[]{:S(2)}, u32[]{:S(2)}) %collective-permute-start.6) | collective-permute-done | bytes 524320 | tf_op jit(solution)/shard_map/ppermute | solution.py:258
  23.9 8.7 %expert.1 = (bf16[64,4096]{1,0:T(8,128)(2,1)S(1)}, bf16[64,4096]{1,0:T(8,128)(2,1)S(1)}, bf16[128,2048]{1,0:T(8,128)(2,1)S(1)}, bf16[128,2048]{1,0:T(8,128)(2,1)...) custom-call(bf16[64,4096]{1,0:T(8,128)(2,1)S(1)} %stack.1.near_ref, ...), custom_call_target="tpu_custom_call" | custom-call | flops 4831838208 | bytes 18874368 | tf_op jit(solution)/shard_map/expert/pallas_call | solution.py:287
  32.6 0.2 collective-permute-start.7
  32.8 2.0 %grads.3.refs_4_ = bf16[1536,2048]{1,0:T(8,128)(2,1)} custom-call(bf16[1536,128]{1,0:T(8,128)(2,1)S(1)} %get-tuple-element.75.refs_0_, bf16[128,2048]{1,0:T(8,128)(2,1)S(1)} %get-tuple-element.76.refs_1_.refs_2_), custom_call_target="tpu_custom_call" | custom-call | flops 268435456 | bytes 3145728 | tf_op jit(solution)/shard_map/grads/pallas_call | solution.py:205
  34.9 0.0 collective-permute-done.7.got_ref
  34.9 0.1 cores.1
  35.0 1.0 %collective-permute-start.8 = (bf16[16,4096]{1,0:T(8,128)(2,1)S(1)}, bf16[16,4096]{1,0:T(8,128)(2,1)S(1)}, u32[]{:S(2)}, u32[]{:S(2)}) collective-permute-start(bf16[16,4096]{1,0:T(8,128)(2,1)S(1)} %get-tuple-element.79), channel_id=1, source_target_pairs={{0,8},{4,12},{8,0},{12,4},{16,24},{20,28},{24,16},{28,20},{1,9},{5... | collective-permute-start | bytes 393224 | tf_op jit(solution)/shard_map/ppermute | solution.py:258
  36.0 1.0 %collective-permute-start.9 = (bf16[16,4096]{1,0:T(8,128)(2,1)S(1)}, bf16[16,4096]{1,0:T(8,128)(2,1)S(1)}, u32[]{:S(2)}, u32[]{:S(2)}) collective-permute-start(bf16[16,4096]{1,0:T(8,128)(2,1)S(1)} %get-tuple-element.80), channel_id=1, source_target_pairs={{0,16},{4,20},{8,24},{12,28},{16,0},{20,4},{24,8},{28,12},{1,17},{... | collective-permute-start | bytes 393224 | tf_op jit(solution)/shard_map/ppermute | solution.py:258
  37.0 1.6 %collective-permute-start.10 = (bf16[16,4096]{1,0:T(8,128)(2,1)S(1)}, bf16[16,4096]{1,0:T(8,128)(2,1)S(1)}, u32[]{:S(2)}, u32[]{:S(2)}) collective-permute-start(bf16[16,4096]{1,0:T(8,128)(2,1)S(1)} %get-tuple-element.81), channel_id=1, source_target_pairs={{0,24},{4,28},{8,16},{12,20},{16,8},{20,12},{24,0},{28,4},{1,25},{... | collective-permute-start | bytes 393224 | tf_op jit(solution)/shard_map/ppermute | solution.py:258
  38.6 4.1 %grads.4 = (bf16[1536,2048]{1,0:T(8,128)(2,1)}, bf16[1536,2048]{1,0:T(8,128)(2,1)}) custom-call(bf16[1536,128]{1,0:T(8,128)(2,1)S(1)} %get-tuple-element.75.refs_0_, bf16[1536,128]{1,0:T(8,128)(2,1)S(1)} %get-tuple-element.82.refs_1_, bf16[128,2048]{1,0:T(8,128)(2,1)S(1)} %get-tuple-element.76.refs_1_.refs_2_, ...), custom_call_target="tpu_custom_call", output_to_operand_aliasing={{0}: (4, {})} | custom-call | flops 1073741824 | bytes 12582912 | tf_op jit(solution)/shard_map/grads/pallas_call | solution.py:205
  42.7 0.0 copy-start.4
  42.7 0.0 copy-start.5
  42.7 0.0 collective-permute-done.8.refs_1_
  42.7 0.0 collective-permute-done.9.refs_2_
  42.7 1.8 %collective-permute-done.10.refs_3_ = bf16[16,4096]{1,0:T(8,128)(2,1)S(1)} collective-permute-done((bf16[16,4096]{1,0:T(8,128)(2,1)S(1)}, bf16[16,4096]{1,0:T(8,128)(2,1)S(1)}, u32[]{:S(2)}, u32[]{:S(2)}) %collective-permute-start.10) | collective-permute-done | bytes 131104 | tf_op jit(solution)/shard_map/ppermute | solution.py:258
  44.5 0.3 chips.1
  44.8 0.1 collective-permute-start.11
  44.9 3.1 %collective-permute-start.12 = (bf16[16,1024]{1,0:T(8,128)(2,1)S(1)}, bf16[16,1024]{1,0:T(8,128)(2,1)S(1)}, u32[]{:S(2)}, u32[]{:S(2)}) collective-permute-start(bf16[16,1024]{1,0:T(8,128)(2,1)S(1)} %get-tuple-element.92), channel_id=1, source_target_pairs={{0,2},{1,3},{2,0},{3,1},{4,6},{5,7},{6,4},{7,5},{8,10},{9,11},{10,... | collective-permute-start | bytes 98312 | tf_op jit(solution)/shard_map/ppermute | solution.py:258
  48.0 1.3 %collective-permute-start.13 = (bf16[16,1024]{1,0:T(8,128)(2,1)S(1)}, bf16[16,1024]{1,0:T(8,128)(2,1)S(1)}, u32[]{:S(2)}, u32[]{:S(2)}) collective-permute-start(bf16[16,1024]{1,0:T(8,128)(2,1)S(1)} %get-tuple-element.93), channel_id=1, source_target_pairs={{0,3},{1,2},{2,1},{3,0},{4,7},{5,6},{6,5},{7,4},{8,11},{9,10},{10,... | collective-permute-start | bytes 98312 | tf_op jit(solution)/shard_map/ppermute | solution.py:258
  49.3 4.0 %grads.5 = (bf16[1536,2048]{1,0:T(8,128)(2,1)}, bf16[1536,2048]{1,0:T(8,128)(2,1)}) custom-call(bf16[1536,128]{1,0:T(8,128)(2,1)S(1)} %get-tuple-element.75.refs_0_, bf16[1536,128]{1,0:T(8,128)(2,1)S(1)} %get-tuple-element.94.refs_1_, bf16[128,2048]{1,0:T(8,128)(2,1)S(1)} %get-tuple-element.76.refs_1_.refs_2_, ...), custom_call_target="tpu_custom_call", output_to_operand_aliasing={{0}: (4, {})} | custom-call | flops 1073741824 | bytes 12582912 | tf_op jit(solution)/shard_map/grads/pallas_call | solution.py:205
  53.3 0.0 collective-permute-done.11.refs_1_
  53.3 0.0 collective-permute-done.12.refs_2_
  53.4 0.3 collective-permute-done.13.refs_3_
  53.7 0.0 copy-done.4
  53.7 0.0 copy-done.5
  53.7 0.7 %home.1 = (bf16[12,512]{1,0:T(8,128)(2,1)}, bf16[12,512]{1,0:T(8,128)(2,1)}) custom-call(bf16[16,1024]{1,0:T(8,128)(2,1)S(1)} %get-tuple-element.98.refs_0_, bf16[16,1024]{1,0:T(8,128)(2,1)S(1)} %collective-permute-done.11.refs_1_, bf16[16,1024]{1,0:T(8,128)(2,1)S(1)} %collective-permute-done.12.refs_2_, ...), custom_call_target="tpu_custom_call" | custom-call | tf_op jit(solution)/shard_map/home/pallas_call | solution.py:331
  (2 shorter events, 0.1 us)
Async XLA Ops:
  2.1 9.7 %collective-permute-start = (bf16[16,1024]{1,0:T(8,128)(2,1)}, bf16[16,1024]{1,0:T(8,128)(2,1)S(1)}, u32[]{:S(2)}, u32[]{:S(2)}) collective-permute-start(bf16[16,1024]{1,0:T(8,128)(2,1)} %get-tuple-element.57), channel_id=1, source_target_pairs={{0,1},{1,0},{2,3},{3,2},{4,5},{5,4},{6,7},{7,6},{8,9},{9,8},{10,11... | collective-permute-start | bytes 98312 | tf_op jit(solution)/shard_map/ppermute | solution.py:258
  5.2 6.6 %collective-permute-start.1 = (bf16[16,1024]{1,0:T(8,128)(2,1)}, bf16[16,1024]{1,0:T(8,128)(2,1)S(1)}, u32[]{:S(2)}, u32[]{:S(2)}) collective-permute-start(bf16[16,1024]{1,0:T(8,128)(2,1)} %get-tuple-element.58), channel_id=1, source_target_pairs={{0,2},{1,3},{2,0},{3,1},{4,6},{5,7},{6,4},{7,5},{8,10},{9,11},{10,... | collective-permute-start | bytes 98312 | tf_op jit(solution)/shard_map/ppermute | solution.py:258
  7.8 5.9 %collective-permute-start.2 = (bf16[16,1024]{1,0:T(8,128)(2,1)}, bf16[16,1024]{1,0:T(8,128)(2,1)S(1)}, u32[]{:S(2)}, u32[]{:S(2)}) collective-permute-start(bf16[16,1024]{1,0:T(8,128)(2,1)} %get-tuple-element.59), channel_id=1, source_target_pairs={{0,3},{1,2},{2,1},{3,0},{4,7},{5,6},{6,5},{7,4},{8,11},{9,10},{10,... | collective-permute-start | bytes 98312 | tf_op jit(solution)/shard_map/ppermute | solution.py:258
  7.8 2.8 %copy-start = (bf16[1,1536,2048]{2,1,0:T(8,128)(2,1)S(1)}, bf16[1,1536,2048]{2,1,0:T(8,128)(2,1)}, u32[]{:S(2)}) copy-start(bf16[1,1536,2048]{2,1,0:T(8,128)(2,1)} %param.11) | copy-start | bytes 18874372
  10.6 0.8 %copy-start.3 = (bf16[16,1024]{1,0:T(8,128)(2,1)S(1)}, bf16[16,1024]{1,0:T(8,128)(2,1)}, u32[]{:S(2)}) copy-start(bf16[16,1024]{1,0:T(8,128)(2,1)} %get-tuple-element.60.after_ref.refs_0_) | copy-start | bytes 98308
  11.4 6.0 %copy-start.1 = (bf16[1,1536,2048]{2,1,0:T(8,128)(2,1)S(1)}, bf16[1,1536,2048]{2,1,0:T(8,128)(2,1)}, u32[]{:S(2)}) copy-start(bf16[1,1536,2048]{2,1,0:T(8,128)(2,1)} %param.12) | copy-start | bytes 18874372
  11.4 6.0 %copy-start.2 = (bf16[1,1536,2048]{2,1,0:T(8,128)(2,1)S(1)}, bf16[1,1536,2048]{2,1,0:T(8,128)(2,1)}, u32[]{:S(2)}) copy-start(bf16[1,1536,2048]{2,1,0:T(8,128)(2,1)} %param.13) | copy-start | bytes 18874372
  13.8 7.2 %collective-permute-start.5 = (bf16[16,4096]{1,0:T(8,128)(2,1)S(1)}, bf16[16,4096]{1,0:T(8,128)(2,1)S(1)}, u32[]{:S(2)}, u32[]{:S(2)}) collective-permute-start(bf16[16,4096]{1,0:T(8,128)(2,1)S(1)} %join.1.after_ref.refs_0_), channel_id=1, source_target_pairs={{0,24},{4,28},{8,16},{12,20},{16,8},{20,12},{24,0},{28,4},{1,25},{... | collective-permute-start | bytes 393224 | tf_op jit(solution)/shard_map/ppermute | solution.py:258
  16.3 5.6 %collective-permute-start.4 = (bf16[16,4096]{1,0:T(8,128)(2,1)S(1)}, bf16[16,4096]{1,0:T(8,128)(2,1)S(1)}, u32[]{:S(2)}, u32[]{:S(2)}) collective-permute-start(bf16[16,4096]{1,0:T(8,128)(2,1)S(1)} %join.1.after_ref.refs_0_), channel_id=1, source_target_pairs={{0,16},{4,20},{8,24},{12,28},{16,0},{20,4},{24,8},{28,12},{1,17},{... | collective-permute-start | bytes 393224 | tf_op jit(solution)/shard_map/ppermute | solution.py:258
  16.8 5.1 %collective-permute-start.3 = (bf16[16,4096]{1,0:T(8,128)(2,1)S(1)}, bf16[16,4096]{1,0:T(8,128)(2,1)S(1)}, u32[]{:S(2)}, u32[]{:S(2)}) collective-permute-start(bf16[16,4096]{1,0:T(8,128)(2,1)S(1)} %join.1.after_ref.refs_0_), channel_id=1, source_target_pairs={{0,8},{4,12},{8,0},{12,4},{16,24},{20,28},{24,16},{28,20},{1,9},{5... | collective-permute-start | bytes 393224 | tf_op jit(solution)/shard_map/ppermute | solution.py:258
  21.9 2.0 %collective-permute-start.6 = (bf16[64,4096]{1,0:T(8,128)(2,1)S(1)}, bf16[64,4096]{1,0:T(8,128)(2,1)S(1)}, u32[]{:S(2)}, u32[]{:S(2)}) collective-permute-start(bf16[64,4096]{1,0:T(8,128)(2,1)S(1)} %stack.1.near_ref), channel_id=1, source_target_pairs={{0,4},{4,0},{8,12},{12,8},{16,20},{20,16},{24,28},{28,24},{1,5},{5... | collective-permute-start | bytes 1572872 | tf_op jit(solution)/shard_map/ppermute | solution.py:258
  32.6 2.2 %collective-permute-start.7 = (bf16[64,4096]{1,0:T(8,128)(2,1)S(1)}, bf16[64,4096]{1,0:T(8,128)(2,1)S(1)}, u32[]{:S(2)}, u32[]{:S(2)}) collective-permute-start(bf16[64,4096]{1,0:T(8,128)(2,1)S(1)} %get-tuple-element.74), channel_id=1, source_target_pairs={{0,4},{4,0},{8,12},{12,8},{16,20},{20,16},{24,28},{28,24},{1,5},{5... | collective-permute-start | bytes 1572872 | tf_op jit(solution)/shard_map/ppermute | solution.py:258
  35.0 7.7 %collective-permute-start.8 = (bf16[16,4096]{1,0:T(8,128)(2,1)S(1)}, bf16[16,4096]{1,0:T(8,128)(2,1)S(1)}, u32[]{:S(2)}, u32[]{:S(2)}) collective-permute-start(bf16[16,4096]{1,0:T(8,128)(2,1)S(1)} %get-tuple-element.79), channel_id=1, source_target_pairs={{0,8},{4,12},{8,0},{12,4},{16,24},{20,28},{24,16},{28,20},{1,9},{5... | collective-permute-start | bytes 393224 | tf_op jit(solution)/shard_map/ppermute | solution.py:258
  36.0 6.7 %collective-permute-start.9 = (bf16[16,4096]{1,0:T(8,128)(2,1)S(1)}, bf16[16,4096]{1,0:T(8,128)(2,1)S(1)}, u32[]{:S(2)}, u32[]{:S(2)}) collective-permute-start(bf16[16,4096]{1,0:T(8,128)(2,1)S(1)} %get-tuple-element.80), channel_id=1, source_target_pairs={{0,16},{4,20},{8,24},{12,28},{16,0},{20,4},{24,8},{28,12},{1,17},{... | collective-permute-start | bytes 393224 | tf_op jit(solution)/shard_map/ppermute | solution.py:258
  37.0 7.5 %collective-permute-start.10 = (bf16[16,4096]{1,0:T(8,128)(2,1)S(1)}, bf16[16,4096]{1,0:T(8,128)(2,1)S(1)}, u32[]{:S(2)}, u32[]{:S(2)}) collective-permute-start(bf16[16,4096]{1,0:T(8,128)(2,1)S(1)} %get-tuple-element.81), channel_id=1, source_target_pairs={{0,24},{4,28},{8,16},{12,20},{16,8},{20,12},{24,0},{28,4},{1,25},{... | collective-permute-start | bytes 393224 | tf_op jit(solution)/shard_map/ppermute | solution.py:258
  42.7 11.0 %copy-start.4 = (s32[12,2]{0,1:T(2,128)S(1)}, s32[12,2]{0,1:T(2,128)}, u32[]{:S(2)}) copy-start(s32[12,2]{0,1:T(2,128)} %param.9) | copy-start | bytes 292
  42.7 11.0 %copy-start.5 = (f32[12,2]{0,1:T(2,128)S(1)}, f32[12,2]{0,1:T(2,128)}, u32[]{:S(2)}) copy-start(f32[12,2]{0,1:T(2,128)} %param.10) | copy-start | bytes 292
  44.8 8.5 %collective-permute-start.11 = (bf16[16,1024]{1,0:T(8,128)(2,1)S(1)}, bf16[16,1024]{1,0:T(8,128)(2,1)S(1)}, u32[]{:S(2)}, u32[]{:S(2)}) collective-permute-start(bf16[16,1024]{1,0:T(8,128)(2,1)S(1)} %get-tuple-element.91), channel_id=1, source_target_pairs={{0,1},{1,0},{2,3},{3,2},{4,5},{5,4},{6,7},{7,6},{8,9},{9,8},{10,11... | collective-permute-start | bytes 98312 | tf_op jit(solution)/shard_map/ppermute | solution.py:258
  44.9 8.4 %collective-permute-start.12 = (bf16[16,1024]{1,0:T(8,128)(2,1)S(1)}, bf16[16,1024]{1,0:T(8,128)(2,1)S(1)}, u32[]{:S(2)}, u32[]{:S(2)}) collective-permute-start(bf16[16,1024]{1,0:T(8,128)(2,1)S(1)} %get-tuple-element.92), channel_id=1, source_target_pairs={{0,2},{1,3},{2,0},{3,1},{4,6},{5,7},{6,4},{7,5},{8,10},{9,11},{10,... | collective-permute-start | bytes 98312 | tf_op jit(solution)/shard_map/ppermute | solution.py:258
  48.0 5.7 %collective-permute-start.13 = (bf16[16,1024]{1,0:T(8,128)(2,1)S(1)}, bf16[16,1024]{1,0:T(8,128)(2,1)S(1)}, u32[]{:S(2)}, u32[]{:S(2)}) collective-permute-start(bf16[16,1024]{1,0:T(8,128)(2,1)S(1)} %get-tuple-element.93), channel_id=1, source_target_pairs={{0,3},{1,2},{2,1},{3,0},{4,7},{5,6},{6,5},{7,4},{8,11},{9,10},{10,... | collective-permute-start | bytes 98312 | tf_op jit(solution)/shard_map/ppermute | solution.py:258

commit v3 on v2

--- a/solution.py
+++ b/solution.py
@@ -11,7 +11,6 @@
 F32 = jnp.float32
 VM = pl.BlockSpec(memory_space=pltpu.VMEM)
 HBM = pl.BlockSpec(memory_space=pltpu.HBM)
-ANY = pl.BlockSpec(memory_space=pl.ANY)
 ROWS = 16
 
 
@@ -41,52 +40,35 @@
     return pltpu.CompilerParams(vmem_limit_bytes=mib << 20)
 
 
-def pack_kernel(
-    tok_hbm, cot_hbm, route_hbm, gates_hbm, *refs
-):
-    outs, (tok_ref, cot_ref, route_ref, gates_ref, sems) = refs[:-5], refs[-5:]
-    pairs = (
-        (tok_hbm, tok_ref), (cot_hbm, cot_ref), (route_hbm, route_ref), (gates_hbm, gates_ref)
-    )
-    copies = [pltpu.make_async_copy(a, b, sems.at[i]) for i, (a, b) in enumerate(pairs)]
-    for copy in copies:
-        copy.start()
-    for copy in copies:
-        copy.wait()
-    tok, width = tok_ref.shape
-    token_rows = tok_ref[...]
-    cot = cot_ref[...].astype(F32)
-    route = route_ref[...]
-    gates = gates_ref[...]
+def share_kernel(route_ref, gates_ref, out_ref):
+    tok = route_ref.shape[1]
+    out_ref[...] = jnp.zeros_like(out_ref)
+    column = share(route_ref[...], gates_ref[...], lax.axis_index("expert"))
+    out_ref[:tok] = jnp.broadcast_to(column, (tok, out_ref.shape[1]))
+
+
+def pair_kernel(a_ref, b_ref, out_ref):
+    n = a_ref.shape[0]
+    out_ref[:n] = a_ref[...]
+    out_ref[n:] = b_ref[...]
+
+
+def join_kernel(patterns, share_ref, a_ref, b_ref, out_ref):
+    half, tok, width = a_ref.shape
+    width //= 2
+    d = len(patterns) * width
     me = lax.axis_index("expert")
-    for k, out_ref in enumerate(outs):
-        out_ref[...] = jnp.zeros_like(out_ref)
-        out_ref[:tok, :width] = token_rows
-        out_ref[:tok, width:] = (share(route, gates, me ^ k) * cot).astype(BF)
-
-
-def load_kernel(after_ref, *refs):
-    n = (len(refs) - 1) // 2
-    sems = refs[-1]
-    copies = [pltpu.make_async_copy(refs[i], refs[n + i], sems.at[i]) for i in range(n)]
-    for copy in copies:
-        copy.start()
-    for copy in copies:
-        copy.wait()
-
-
-def join_kernel(*refs):
-    ins, out_ref = refs[:-1], refs[-1]
-    width = ins[0].shape[1] // 2
-    d = len(ins) * width
-    me = lax.axis_index("expert")
-    for e in range(len(ins)):
-        for k, ref in enumerate(ins):
+    weight = share_ref[:tok, :1]
+    out_ref[...] = jnp.zeros_like(out_ref)
+    for i, k in enumerate(patterns):
+        block = a_ref[i] if i < half else b_ref[i - half]
+        dys = (weight * block[:, width:].astype(F32)).astype(BF)
+        for e in range(len(patterns)):
 
             @pl.when(me ^ k == e)
-            def _(e=e, ref=ref):
-                out_ref[:, e * width : (e + 1) * width] = ref[:, :width]
-                out_ref[:, d + e * width : d + (e + 1) * width] = ref[:, width:]
+            def _(e=e, block=block, dys=dys):
+                out_ref[:tok, e * width : (e + 1) * width] = block[:, :width]
+                out_ref[:tok, d + e * width : d + (e + 1) * width] = dys
 
 
 def stack_kernel(*refs):
@@ -161,38 +143,34 @@
         out_ref[...] = (keep_ref[rows].astype(F32) + got_ref[rows].astype(F32)).astype(BF)
 
 
-def chips_kernel(n, *refs):
+def chips_kernel(n, share_ref, *refs):
     ins, outs = refs[:n], refs[n:]
     width = outs[0].shape[1] // 2
     d = len(outs) * width
     total = ins[0][...].astype(F32)
     for ref in ins[1:]:
         total = total + ref[...].astype(F32)
-    total = total.astype(BF)
+    out = (share_ref[:, :1] * total[:, :d]).astype(BF)
+    grad = total[:, d:].astype(BF)
     me = lax.axis_index("expert")
     for e in range(len(outs)):
+        part = slice(e * width, (e + 1) * width)
         for k, out_ref in enumerate(outs):
 
             @pl.when(me ^ k == e)
-            def _(e=e, out_ref=out_ref):
-                out_ref[:, :width] = total[:, e * width : (e + 1) * width]
-                out_ref[:, width:] = total[:, d + e * width : d + (e + 1) * width]
+            def _(part=part, out_ref=out_ref):
+                out_ref[:, :width] = out[:, part]
+                out_ref[:, width:] = grad[:, part]
 
 
 def home_kernel(*refs):
-    ins, (route_ref, gates_ref, mixed_ref, grad_ref) = refs[:-4], refs[-4:]
+    ins, (mixed_ref, grad_ref) = refs[:-2], refs[-2:]
     tok, width = mixed_ref.shape
-    route = route_ref[...]
-    gates = gates_ref[...]
-    mixed = jnp.zeros((tok, width), F32)
-    grad = jnp.zeros((tok, width), F32)
-    me = lax.axis_index("expert")
-    for k, ref in enumerate(ins):
-        got = ref[...].astype(F32)[:tok]
-        mixed = mixed + share(route, gates, me ^ k) * got[:, :width]
-        grad = grad + got[:, width:]
-    mixed_ref[...] = mixed.astype(BF)
-    grad_ref[...] = grad.astype(BF)
+    total = ins[0][...].astype(F32)
+    for ref in ins[1:]:
+        total = total + ref[...].astype(F32)
+    mixed_ref[...] = total[:tok, :width].astype(BF)
+    grad_ref[...] = total[:tok, width:].astype(BF)
 
 
 def grads(jobs, lefts, rights, old):
@@ -217,27 +195,13 @@
     )(*lefts, *rights, *[old[a] for a in kept])
 
 
-def load(mib, after, *arrays):
-    size = sum(a.size for a in arrays) * 2
-    return pl.pallas_call(
-        load_kernel,
-        in_specs=[ANY] + [HBM] * len(arrays),
-        out_specs=[VM] * len(arrays),
-        out_shape=[jax.ShapeDtypeStruct(a.shape, a.dtype) for a in arrays],
-        scratch_shapes=[pltpu.SemaphoreType.DMA((len(arrays),))],
-        compiler_params=params(mib),
-        cost_estimate=pl.CostEstimate(flops=0, bytes_accessed=size, transcendentals=0),
-        name="load",
-    )(after, *arrays)
-
-
-def stack(kernel, arrays, shape, name):
-    size = 2 * sum(a.size for a in arrays)
+def stack(kernel, arrays, shape, name, dtype=BF):
+    size = sum(a.size * a.dtype.itemsize for a in arrays)
     return pl.pallas_call(
         kernel,
         in_specs=[VM] * len(arrays),
         out_specs=VM,
-        out_shape=jax.ShapeDtypeStruct(shape, BF),
+        out_shape=jax.ShapeDtypeStruct(shape, dtype),
         compiler_params=params((size >> 19) + 2),
         name=name,
     )(*arrays)
@@ -258,28 +222,36 @@
         return lax.ppermute(x, axis, [(i, i ^ k) for i in range(size)])
 
     small = n_chip + 4
-    packed = pl.pallas_call(
-        pack_kernel,
-        in_specs=[HBM] * 4,
-        out_specs=[VM] * n_e,
-        out_shape=[sds((ROWS, 2 * width), BF)] * n_e,
-        scratch_shapes=[
-            pltpu.VMEM(tokens.shape, BF),
-            pltpu.VMEM(tokens.shape, BF),
-            pltpu.VMEM((2, tok), jnp.int32),
-            pltpu.VMEM((2, tok), F32),
-            pltpu.SemaphoreType.DMA((4,)),
-        ],
-        name="pack",
-    )(tokens, cotangent, route.T, gates.T)
-    mine = [packed[0]] + [swap(packed[k], "expert", n_e, k) for k in range(1, n_e)]
-    weight_mib = f * d >> 19
-    (wg,) = load(weight_mib + 3, packed[0], w_gate[0])
-    mine, wg = lax.optimization_barrier((mine, wg))
-    block = stack(join_kernel, mine, (ROWS, 2 * d), "join")
+    mine = jnp.concatenate([tokens, cotangent], axis=1)[None]
+    patterns, hop, first = [0], n_e // 2, True
+    while hop:
+        patterns = patterns + [p ^ hop for p in patterns]
+        got = swap(mine, "expert", n_e, hop)
+        if first:
+            weight = pl.pallas_call(
+                share_kernel,
+                in_specs=[VM, VM],
+                out_specs=VM,
+                out_shape=sds((ROWS, 128), F32),
+                compiler_params=params(2),
+                cost_estimate=pl.CostEstimate(
+                    flops=40 * rows * f * d, bytes_accessed=24 * f * d, transcendentals=0
+                ),
+                name="share",
+            )(route.T, gates.T)
+            first = False
+            got, weight = lax.optimization_barrier((got, weight))
+        if hop == 1:
+            block = stack(
+                functools.partial(join_kernel, tuple(patterns)),
+                [weight, mine, got],
+                (ROWS, 2 * d),
+                "join",
+            )
+        else:
+            mine = stack(pair_kernel, [mine, got], (len(patterns), tok, 2 * width), "pair")
+        hop //= 2
     blocks = [block] + [swap(block, "dp", n_dp, 2 * k) for k in range(1, n_chip)]
-    wu, wd = load(2 * weight_mib + 3, block, w_up[0], w_down[0])
-    blocks, wu, wd = lax.optimization_barrier((blocks, wu, wd))
     near = stack(stack_kernel, blocks, (n_chip * ROWS, 2 * d), "stack")
     far = swap(near, "dp", n_dp, 1)
 
@@ -297,12 +269,12 @@
             flops=12 * rows * f * d, bytes_accessed=6 * f * d, transcendentals=rows * f
         ),
         name="expert",
-    )(near, far, wg, wu, wd)
+    )(near, far, w_gate[0], w_up[0], w_down[0])
 
     received = swap(send, "dp", n_dp, 1)
-    third = f // 3
+    third, sixth = f // 3, f // 6
     whole = [(1, i * third, third) for i in range(3)]
-    (down,) = grads([(0, 0, third)], [hidden], [dys], [None])
+    (down,) = grads([(0, 0, sixth)], [hidden], [dys], [None])
     received, down = lax.optimization_barrier((received, down))
     parts = pl.pallas_call(
         cores_kernel,
@@ -312,30 +284,30 @@
         compiler_params=params(small),
         name="cores",
     )(keep, received)
-    arrived = [swap(parts[k], "dp", n_dp, 2 * k) for k in range(1, n_chip)]
-    down, grad_gate = grads([(0, third, third)] + whole, [hidden, gpg], [dys, xs], [down, None])
+    arrived = [swap(parts[k], "dp", n_dp, 2 * k) for k in range(n_chip - 1, 0, -1)]
+    down, grad_gate = grads([(0, sixth, third), (0, 3 * sixth, third)] + whole, [hidden, gpg], [dys, xs], [down, None])
     arrived, down, grad_gate = lax.optimization_barrier((arrived, down, grad_gate))
     summed = pl.pallas_call(
         functools.partial(chips_kernel, n_chip),
-        in_specs=[VM] * n_chip,
+        in_specs=[VM] * (n_chip + 1),
         out_specs=[VM] * n_e,
         out_shape=[sds((ROWS, 2 * width), BF)] * n_e,
         compiler_params=params(small),
         name="chips",
-    )(parts[0], *arrived)
-    home = [summed[0]] + [swap(summed[k], "expert", n_e, k) for k in range(1, n_e)]
+    )(weight, parts[0], *arrived)
+    home = [summed[0]] + [swap(summed[k], "expert", n_e, k) for k in range(n_e - 1, 0, -1)]
     grad_down, grad_up = grads(
-        [(0, 2 * third, third)] + whole, [hidden, gpu], [dys, xs], [down, None]
+        [(0, 5 * sixth, sixth)] + whole, [hidden, gpu], [dys, xs], [down, None]
     )
     home, grad_down, grad_up = lax.optimization_barrier((home, grad_down, grad_up))
     mixed, grad_tokens = pl.pallas_call(
         home_kernel,
-        in_specs=[VM] * (n_e + 2),
+        in_specs=[VM] * n_e,
         out_specs=[VM] * 2,
         out_shape=[sds((tok, width), BF)] * 2,
         compiler_params=params(4),
         name="home",
-    )(*home, route.T, gates.T)
+    )(*home)
     return mixed, grad_tokens, grad_gate[None], grad_up[None], grad_down[None]
 
 

time: 54.7 us -> 52.2 us (0.954)
  Pallas kernels: 22.9 us -> 19.7 us
  local copies, waits for them, and re-layouts: 3.56 us -> 1.37 us
  waiting for transfers between devices: 9.64 us -> 11.8 us
  other arithmetic: 0 us -> 0.74 us
    pallas_call x5 -> x3, Pallas kernels: 3.83 us -> 0.87 us  [the longest x1 0.63 us: per_device(): pl.pallas_call(home_kernel, in_specs=[VM] * n_e, out_specs=[VM] * 2, out_...]
    unnamed x12 -> x10, local copies, waits for them, and re-layouts: 3.56 us -> 1.37 us
    ppermute x14 -> x13, waiting for transfers between devices: 9.64 us -> 11.8 us  [swap(): return lax.ppermute(x, axis, [(i, i ^ k) for i in range(size)])]
    broadcast_in_dim x0 -> x1, other arithmetic: none -> 0.74 us  [per_device(): mine = jnp.concatenate([tokens, cotangent], axis=1)[None]]
    ppermute x14 -> x13, starting transfers between devices: 17.5 us -> 17.4 us  [swap(): return lax.ppermute(x, axis, [(i, i ^ k) for i in range(size)])]
  transfers between devices with their start and end apart: 14 -> 13, of which waited for: 6 -> 10; matrix products, arithmetic and copies ran while one was open for 0% -> 0% of each run, Pallas kernels for 21% -> 19%
where the time goes in v3:
time: 52.2 us; the launch traced here: 51.8 us
  Pallas kernels  19.7 us (38%)
  starting transfers between devices  17.4 us (33%)
  waiting for transfers between devices  11.8 us (23%)
  local copies, waits for them, and re-layouts  1.37 us (3%)
  other arithmetic  0.74 us (1%)
  between operations  0.73 us (1%)
    ppermute x13, starting transfers between devices, swap(): return lax.ppermute(x, axis, [(i, i ^ k) for i in range(size)])  17.4 us
    ppermute x13, waiting for transfers between devices, swap(): return lax.ppermute(x, axis, [(i, i ^ k) for i in range(size)])  11.8 us
    pallas_call x3, Pallas kernels, grads(): pl.pallas_call(functools.partial(grads_kernel, jobs, n, len(kept)), in_sp...  9.85 us
    pallas_call x1, Pallas kernels, per_device(): pl.pallas_call(functools.partial(expert_kernel, tile=tile, cols=256), in_...  8.7 us
    unnamed x10, local copies, waits for them, and re-layouts  1.37 us
  transfers between devices with their start and end apart: 13, of which 10 were waited for; matrix products, arithmetic and copies ran while one was open for 0% of the time, Pallas kernels for 19%

profile of v3, /device:TPU:0, one launch (start us, length us, event | category | flops | bytes accessed | tf_op | source)
XLA Modules:
  0.0 51.8 jit_solution(12877373008648584855)
XLA Ops:
  0.6 0.7 %maximum_bitcast_fusion.a_ref = bf16[1,12,1024]{2,1,0:T(8,128)(2,1)S(1)} fusion(bf16[12,512]{1,0:T(8,128)(2,1)} %param.8, bf16[12,512]{1,0:T(8,128)(2,1)} %param.7), kind=kLoop, calls=%fused_computation | loop fusion | flops 49152 | bytes 49152 | tf_op jit(solution)/shard_map/broadcast_in_dim | solution.py:225
  1.4 4.0 %collective-permute-start = (bf16[1,12,1024]{2,1,0:T(8,128)(2,1)S(1)}, bf16[1,12,1024]{2,1,0:T(8,128)(2,1)S(1)}, u32[]{:S(2)}, u32[]{:S(2)}) collective-permute-start(bf16[1,12,1024]{2,1,0:T(8,128)(2,1)S(1)} %maximum_bitcast_fusion.a_ref), channel_id=1, source_target_pairs={{0,2},{1,3},{2,0},{3,1},{4,6},{5,7},{6,4},{7,5},{8,10},{9,11},{10,... | collective-permute-start | bytes 73736 | tf_op jit(solution)/shard_map/ppermute | solution.py:222
  5.4 0.0 copy-start.3
  5.4 0.7 %copy-done.3 = s32[12,2]{0,1:T(2,128)S(1)} copy-done((s32[12,2]{0,1:T(2,128)S(1)}, s32[12,2]{0,1:T(2,128)}, u32[]{:S(2)}) %copy-start.3) | copy-done | bytes 120
  6.1 0.0 copy-start.4
  6.1 0.7 %copy-done.4 = f32[12,2]{0,1:T(2,128)S(1)} copy-done((f32[12,2]{0,1:T(2,128)S(1)}, f32[12,2]{0,1:T(2,128)}, u32[]{:S(2)}) %copy-start.4) | copy-done | bytes 120
  6.8 0.0 copy-start
  6.8 0.0 copy-start.1
  6.8 0.0 copy-start.2
  6.8 0.1 share.1.share_ref
  6.9 0.8 %collective-permute-done.b_ref = bf16[1,12,1024]{2,1,0:T(8,128)(2,1)S(1)} collective-permute-done((bf16[1,12,1024]{2,1,0:T(8,128)(2,1)S(1)}, bf16[1,12,1024]{2,1,0:T(8,128)(2,1)S(1)}, u32[]{:S(2)}, u32[]{:S(2)}) %collective-permute-start) | collective-permute-done | bytes 24608 | tf_op jit(solution)/shard_map/ppermute | solution.py:222
  7.7 1.6 %collective-permute-start.1 = (bf16[2,12,1024]{2,1,0:T(8,128)(2,1)S(1)}, bf16[2,12,1024]{2,1,0:T(8,128)(2,1)S(1)}, u32[]{:S(2)}, u32[]{:S(2)}) collective-permute-start(bf16[2,12,1024]{2,1,0:T(8,128)(2,1)S(1)} %pair.1.a_ref), channel_id=1, source_target_pairs={{0,1},{1,0},{2,3},{3,2},{4,5},{5,4},{6,7},{7,6},{8,9},{9,8},{10,11... | collective-permute-start | bytes 147464 | tf_op jit(solution)/shard_map/ppermute | solution.py:222
  9.2 2.7 %collective-permute-done.1.b_ref = bf16[2,12,1024]{2,1,0:T(8,128)(2,1)S(1)} collective-permute-done((bf16[2,12,1024]{2,1,0:T(8,128)(2,1)S(1)}, bf16[2,12,1024]{2,1,0:T(8,128)(2,1)S(1)}, u32[]{:S(2)}, u32[]{:S(2)}) %collective-permute-start.1) | collective-permute-done | bytes 49184 | tf_op jit(solution)/shard_map/ppermute | solution.py:222
  11.9 0.1 join.1.refs_0_
  12.0 2.7 %collective-permute-start.4 = (bf16[16,4096]{1,0:T(8,128)(2,1)S(1)}, bf16[16,4096]{1,0:T(8,128)(2,1)S(1)}, u32[]{:S(2)}, u32[]{:S(2)}) collective-permute-start(bf16[16,4096]{1,0:T(8,128)(2,1)S(1)} %join.1.refs_0_), channel_id=1, source_target_pairs={{0,24},{4,28},{8,16},{12,20},{16,8},{20,12},{24,0},{28,4},{1,25},{... | collective-permute-start | bytes 393224 | tf_op jit(solution)/shard_map/ppermute | solution.py:222
  14.8 0.5 collective-permute-start.3
  15.3 0.3 collective-permute-start.2
  15.6 3.0 %collective-permute-done.4.refs_3_ = bf16[16,4096]{1,0:T(8,128)(2,1)S(1)} collective-permute-done((bf16[16,4096]{1,0:T(8,128)(2,1)S(1)}, bf16[16,4096]{1,0:T(8,128)(2,1)S(1)}, u32[]{:S(2)}, u32[]{:S(2)}) %collective-permute-start.4) | collective-permute-done | bytes 131104 | tf_op jit(solution)/shard_map/ppermute | solution.py:222
  18.6 1.4 %collective-permute-done.3.refs_2_ = bf16[16,4096]{1,0:T(8,128)(2,1)S(1)} collective-permute-done((bf16[16,4096]{1,0:T(8,128)(2,1)S(1)}, bf16[16,4096]{1,0:T(8,128)(2,1)S(1)}, u32[]{:S(2)}, u32[]{:S(2)}) %collective-permute-start.3) | collective-permute-done | bytes 131104 | tf_op jit(solution)/shard_map/ppermute | solution.py:222
  20.0 0.3 collective-permute-done.2.refs_1_
  20.3 0.1 collective-permute-start.5
  20.4 1.9 %collective-permute-done.5.far_ref = bf16[64,4096]{1,0:T(8,128)(2,1)S(1)} collective-permute-done((bf16[64,4096]{1,0:T(8,128)(2,1)S(1)}, bf16[64,4096]{1,0:T(8,128)(2,1)S(1)}, u32[]{:S(2)}, u32[]{:S(2)}) %collective-permute-start.5) | collective-permute-done | bytes 524320 | tf_op jit(solution)/shard_map/ppermute | solution.py:222
  22.3 0.0 copy-done
  22.3 0.0 copy-done.1
  22.3 0.0 copy-done.2
  22.3 8.7 %expert.1 = (bf16[64,4096]{1,0:T(8,128)(2,1)S(1)}, bf16[64,4096]{1,0:T(8,128)(2,1)S(1)}, bf16[128,2048]{1,0:T(8,128)(2,1)S(1)}, bf16[128,2048]{1,0:T(8,128)(2,1)...) custom-call(bf16[64,4096]{1,0:T(8,128)(2,1)S(1)} %stack.1.near_ref, ...), custom_call_target="tpu_custom_call" | custom-call | flops 4831838208 | bytes 18874368 | tf_op jit(solution)/shard_map/expert/pallas_call | solution.py:259
  31.0 0.2 collective-permute-start.6
  31.2 1.4 %grads.3.refs_4_ = bf16[1536,2048]{1,0:T(8,128)(2,1)} custom-call(bf16[1536,128]{1,0:T(8,128)(2,1)S(1)} %get-tuple-element.45.refs_0_, bf16[128,2048]{1,0:T(8,128)(2,1)S(1)} %get-tuple-element.46.refs_1_.refs_2_), custom_call_target="tpu_custom_call" | custom-call | flops 134217728 | bytes 1572864 | tf_op jit(solution)/shard_map/grads/pallas_call | solution.py:183
  32.6 0.4 collective-permute-done.6.got_ref
  33.0 0.1 cores.1
  33.1 1.6 %collective-permute-start.7 = (bf16[16,4096]{1,0:T(8,128)(2,1)S(1)}, bf16[16,4096]{1,0:T(8,128)(2,1)S(1)}, u32[]{:S(2)}, u32[]{:S(2)}) collective-permute-start(bf16[16,4096]{1,0:T(8,128)(2,1)S(1)} %get-tuple-element.49), channel_id=1, source_target_pairs={{0,24},{4,28},{8,16},{12,20},{16,8},{20,12},{24,0},{28,4},{1,25},{... | collective-permute-start | bytes 393224 | tf_op jit(solution)/shard_map/ppermute | solution.py:222
  34.6 0.9 %collective-permute-start.8 = (bf16[16,4096]{1,0:T(8,128)(2,1)S(1)}, bf16[16,4096]{1,0:T(8,128)(2,1)S(1)}, u32[]{:S(2)}, u32[]{:S(2)}) collective-permute-start(bf16[16,4096]{1,0:T(8,128)(2,1)S(1)} %get-tuple-element.50), channel_id=1, source_target_pairs={{0,16},{4,20},{8,24},{12,28},{16,0},{20,4},{24,8},{28,12},{1,17},{... | collective-permute-start | bytes 393224 | tf_op jit(solution)/shard_map/ppermute | solution.py:222
  35.6 1.1 %collective-permute-start.9 = (bf16[16,4096]{1,0:T(8,128)(2,1)S(1)}, bf16[16,4096]{1,0:T(8,128)(2,1)S(1)}, u32[]{:S(2)}, u32[]{:S(2)}) collective-permute-start(bf16[16,4096]{1,0:T(8,128)(2,1)S(1)} %get-tuple-element.51), channel_id=1, source_target_pairs={{0,8},{4,12},{8,0},{12,4},{16,24},{20,28},{24,16},{28,20},{1,9},{5... | collective-permute-start | bytes 393224 | tf_op jit(solution)/shard_map/ppermute | solution.py:222
  36.6 4.7 %grads.4 = (bf16[1536,2048]{1,0:T(8,128)(2,1)}, bf16[1536,2048]{1,0:T(8,128)(2,1)}) custom-call(bf16[1536,128]{1,0:T(8,128)(2,1)S(1)} %get-tuple-element.45.refs_0_, bf16[1536,128]{1,0:T(8,128)(2,1)S(1)} %get-tuple-element.52.refs_1_, bf16[128,2048]{1,0:T(8,128)(2,1)S(1)} %get-tuple-element.46.refs_1_.refs_2_, ...), custom_call_target="tpu_custom_call", output_to_operand_aliasing={{0}: (4, {})} | custom-call | flops 1342177280 | bytes 15728640 | tf_op jit(solution)/shard_map/grads/pallas_call | solution.py:183
  41.4 0.0 collective-permute-done.7.refs_1_
  41.4 1.0 %collective-permute-done.8.refs_2_ = bf16[16,4096]{1,0:T(8,128)(2,1)S(1)} collective-permute-done((bf16[16,4096]{1,0:T(8,128)(2,1)S(1)}, bf16[16,4096]{1,0:T(8,128)(2,1)S(1)}, u32[]{:S(2)}, u32[]{:S(2)}) %collective-permute-start.8) | collective-permute-done | bytes 131104 | tf_op jit(solution)/shard_map/ppermute | solution.py:222
  42.4 0.1 collective-permute-done.9.refs_3_
  42.5 0.1 chips.1
  42.7 3.7 %collective-permute-start.10 = (bf16[16,1024]{1,0:T(8,128)(2,1)S(1)}, bf16[16,1024]{1,0:T(8,128)(2,1)S(1)}, u32[]{:S(2)}, u32[]{:S(2)}) collective-permute-start(bf16[16,1024]{1,0:T(8,128)(2,1)S(1)} %get-tuple-element.61), channel_id=1, source_target_pairs={{0,3},{1,2},{2,1},{3,0},{4,7},{5,6},{6,5},{7,4},{8,11},{9,10},{10,... | collective-permute-start | bytes 98312 | tf_op jit(solution)/shard_map/ppermute | solution.py:222
  46.3 0.0 collective-permute-start.11
  46.3 0.8 %collective-permute-start.12 = (bf16[16,1024]{1,0:T(8,128)(2,1)S(1)}, bf16[16,1024]{1,0:T(8,128)(2,1)S(1)}, u32[]{:S(2)}, u32[]{:S(2)}) collective-permute-start(bf16[16,1024]{1,0:T(8,128)(2,1)S(1)} %get-tuple-element.63), channel_id=1, source_target_pairs={{0,1},{1,0},{2,3},{3,2},{4,5},{5,4},{6,7},{7,6},{8,9},{9,8},{10,11... | collective-permute-start | bytes 98312 | tf_op jit(solution)/shard_map/ppermute | solution.py:222
  47.1 3.7 %grads.5 = (bf16[1536,2048]{1,0:T(8,128)(2,1)}, bf16[1536,2048]{1,0:T(8,128)(2,1)}) custom-call(bf16[1536,128]{1,0:T(8,128)(2,1)S(1)} %get-tuple-element.45.refs_0_, bf16[1536,128]{1,0:T(8,128)(2,1)S(1)} %get-tuple-element.64.refs_1_, bf16[128,2048]{1,0:T(8,128)(2,1)S(1)} %get-tuple-element.46.refs_1_.refs_2_, ...), custom_call_target="tpu_custom_call", output_to_operand_aliasing={{0}: (4, {})} | custom-call | flops 939524096 | bytes 11010048 | tf_op jit(solution)/shard_map/grads/pallas_call | solution.py:183
  50.8 0.0 collective-permute-done.10.refs_1_
  50.8 0.3 collective-permute-done.11.refs_2_
  51.1 0.0 collective-permute-done.12.refs_3_
  51.1 0.6 %home.1 = (bf16[12,512]{1,0:T(8,128)(2,1)}, bf16[12,512]{1,0:T(8,128)(2,1)}) custom-call(bf16[16,1024]{1,0:T(8,128)(2,1)S(1)} %get-tuple-element.68.refs_0_, bf16[16,1024]{1,0:T(8,128)(2,1)S(1)} %collective-permute-done.10.refs_1_, bf16[16,1024]{1,0:T(8,128)(2,1)S(1)} %collective-permute-done.11.refs_2_, bf16[16,1024]{1,0:T(8,128)(2,1)S(1)} %collective-permute-done.12.refs_3_), custom_call_target="tpu_custom_call" | custom-call | tf_op jit(solution)/shard_map/home/pallas_call | solution.py:303
  (2 shorter events, 0.0 us)
Async XLA Ops:
  1.4 6.3 %collective-permute-start = (bf16[1,12,1024]{2,1,0:T(8,128)(2,1)S(1)}, bf16[1,12,1024]{2,1,0:T(8,128)(2,1)S(1)}, u32[]{:S(2)}, u32[]{:S(2)}) collective-permute-start(bf16[1,12,1024]{2,1,0:T(8,128)(2,1)S(1)} %maximum_bitcast_fusion.a_ref), channel_id=1, source_target_pairs={{0,2},{1,3},{2,0},{3,1},{4,6},{5,7},{6,4},{7,5},{8,10},{9,11},{10,... | collective-permute-start | bytes 73736 | tf_op jit(solution)/shard_map/ppermute | solution.py:222
  5.4 0.7 %copy-start.3 = (s32[12,2]{0,1:T(2,128)S(1)}, s32[12,2]{0,1:T(2,128)}, u32[]{:S(2)}) copy-start(s32[12,2]{0,1:T(2,128)} %param.9) | copy-start | bytes 292
  6.1 0.7 %copy-start.4 = (f32[12,2]{0,1:T(2,128)S(1)}, f32[12,2]{0,1:T(2,128)}, u32[]{:S(2)}) copy-start(f32[12,2]{0,1:T(2,128)} %param.10) | copy-start | bytes 292
  6.8 15.5 %copy-start = (bf16[1,1536,2048]{2,1,0:T(8,128)(2,1)S(1)}, bf16[1,1536,2048]{2,1,0:T(8,128)(2,1)}, u32[]{:S(2)}) copy-start(bf16[1,1536,2048]{2,1,0:T(8,128)(2,1)} %param.11) | copy-start | bytes 18874372
  6.8 15.5 %copy-start.1 = (bf16[1,1536,2048]{2,1,0:T(8,128)(2,1)S(1)}, bf16[1,1536,2048]{2,1,0:T(8,128)(2,1)}, u32[]{:S(2)}) copy-start(bf16[1,1536,2048]{2,1,0:T(8,128)(2,1)} %param.12) | copy-start | bytes 18874372
  6.8 15.5 %copy-start.2 = (bf16[1,1536,2048]{2,1,0:T(8,128)(2,1)S(1)}, bf16[1,1536,2048]{2,1,0:T(8,128)(2,1)}, u32[]{:S(2)}) copy-start(bf16[1,1536,2048]{2,1,0:T(8,128)(2,1)} %param.13) | copy-start | bytes 18874372
  7.7 4.3 %collective-permute-start.1 = (bf16[2,12,1024]{2,1,0:T(8,128)(2,1)S(1)}, bf16[2,12,1024]{2,1,0:T(8,128)(2,1)S(1)}, u32[]{:S(2)}, u32[]{:S(2)}) collective-permute-start(bf16[2,12,1024]{2,1,0:T(8,128)(2,1)S(1)} %pair.1.a_ref), channel_id=1, source_target_pairs={{0,1},{1,0},{2,3},{3,2},{4,5},{5,4},{6,7},{7,6},{8,9},{9,8},{10,11... | collective-permute-start | bytes 147464 | tf_op jit(solution)/shard_map/ppermute | solution.py:222
  12.0 6.5 %collective-permute-start.4 = (bf16[16,4096]{1,0:T(8,128)(2,1)S(1)}, bf16[16,4096]{1,0:T(8,128)(2,1)S(1)}, u32[]{:S(2)}, u32[]{:S(2)}) collective-permute-start(bf16[16,4096]{1,0:T(8,128)(2,1)S(1)} %join.1.refs_0_), channel_id=1, source_target_pairs={{0,24},{4,28},{8,16},{12,20},{16,8},{20,12},{24,0},{28,4},{1,25},{... | collective-permute-start | bytes 393224 | tf_op jit(solution)/shard_map/ppermute | solution.py:222
  14.8 5.2 %collective-permute-start.3 = (bf16[16,4096]{1,0:T(8,128)(2,1)S(1)}, bf16[16,4096]{1,0:T(8,128)(2,1)S(1)}, u32[]{:S(2)}, u32[]{:S(2)}) collective-permute-start(bf16[16,4096]{1,0:T(8,128)(2,1)S(1)} %join.1.refs_0_), channel_id=1, source_target_pairs={{0,16},{4,20},{8,24},{12,28},{16,0},{20,4},{24,8},{28,12},{1,17},{... | collective-permute-start | bytes 393224 | tf_op jit(solution)/shard_map/ppermute | solution.py:222
  15.3 5.0 %collective-permute-start.2 = (bf16[16,4096]{1,0:T(8,128)(2,1)S(1)}, bf16[16,4096]{1,0:T(8,128)(2,1)S(1)}, u32[]{:S(2)}, u32[]{:S(2)}) collective-permute-start(bf16[16,4096]{1,0:T(8,128)(2,1)S(1)} %join.1.refs_0_), channel_id=1, source_target_pairs={{0,8},{4,12},{8,0},{12,4},{16,24},{20,28},{24,16},{28,20},{1,9},{5... | collective-permute-start | bytes 393224 | tf_op jit(solution)/shard_map/ppermute | solution.py:222
  20.3 2.0 %collective-permute-start.5 = (bf16[64,4096]{1,0:T(8,128)(2,1)S(1)}, bf16[64,4096]{1,0:T(8,128)(2,1)S(1)}, u32[]{:S(2)}, u32[]{:S(2)}) collective-permute-start(bf16[64,4096]{1,0:T(8,128)(2,1)S(1)} %stack.1.near_ref), channel_id=1, source_target_pairs={{0,4},{4,0},{8,12},{12,8},{16,20},{20,16},{24,28},{28,24},{1,5},{5... | collective-permute-start | bytes 1572872 | tf_op jit(solution)/shard_map/ppermute | solution.py:222
  31.0 2.0 %collective-permute-start.6 = (bf16[64,4096]{1,0:T(8,128)(2,1)S(1)}, bf16[64,4096]{1,0:T(8,128)(2,1)S(1)}, u32[]{:S(2)}, u32[]{:S(2)}) collective-permute-start(bf16[64,4096]{1,0:T(8,128)(2,1)S(1)} %get-tuple-element.44), channel_id=1, source_target_pairs={{0,4},{4,0},{8,12},{12,8},{16,20},{20,16},{24,28},{28,24},{1,5},{5... | collective-permute-start | bytes 1572872 | tf_op jit(solution)/shard_map/ppermute | solution.py:222
  33.1 8.3 %collective-permute-start.7 = (bf16[16,4096]{1,0:T(8,128)(2,1)S(1)}, bf16[16,4096]{1,0:T(8,128)(2,1)S(1)}, u32[]{:S(2)}, u32[]{:S(2)}) collective-permute-start(bf16[16,4096]{1,0:T(8,128)(2,1)S(1)} %get-tuple-element.49), channel_id=1, source_target_pairs={{0,24},{4,28},{8,16},{12,20},{16,8},{20,12},{24,0},{28,4},{1,25},{... | collective-permute-start | bytes 393224 | tf_op jit(solution)/shard_map/ppermute | solution.py:222
  34.6 7.8 %collective-permute-start.8 = (bf16[16,4096]{1,0:T(8,128)(2,1)S(1)}, bf16[16,4096]{1,0:T(8,128)(2,1)S(1)}, u32[]{:S(2)}, u32[]{:S(2)}) collective-permute-start(bf16[16,4096]{1,0:T(8,128)(2,1)S(1)} %get-tuple-element.50), channel_id=1, source_target_pairs={{0,16},{4,20},{8,24},{12,28},{16,0},{20,4},{24,8},{28,12},{1,17},{... | collective-permute-start | bytes 393224 | tf_op jit(solution)/shard_map/ppermute | solution.py:222
  35.6 6.9 %collective-permute-start.9 = (bf16[16,4096]{1,0:T(8,128)(2,1)S(1)}, bf16[16,4096]{1,0:T(8,128)(2,1)S(1)}, u32[]{:S(2)}, u32[]{:S(2)}) collective-permute-start(bf16[16,4096]{1,0:T(8,128)(2,1)S(1)} %get-tuple-element.51), channel_id=1, source_target_pairs={{0,8},{4,12},{8,0},{12,4},{16,24},{20,28},{24,16},{28,20},{1,9},{5... | collective-permute-start | bytes 393224 | tf_op jit(solution)/shard_map/ppermute | solution.py:222
  42.7 8.2 %collective-permute-start.10 = (bf16[16,1024]{1,0:T(8,128)(2,1)S(1)}, bf16[16,1024]{1,0:T(8,128)(2,1)S(1)}, u32[]{:S(2)}, u32[]{:S(2)}) collective-permute-start(bf16[16,1024]{1,0:T(8,128)(2,1)S(1)} %get-tuple-element.61), channel_id=1, source_target_pairs={{0,3},{1,2},{2,1},{3,0},{4,7},{5,6},{6,5},{7,4},{8,11},{9,10},{10,... | collective-permute-start | bytes 98312 | tf_op jit(solution)/shard_map/ppermute | solution.py:222
  46.3 4.8 %collective-permute-start.11 = (bf16[16,1024]{1,0:T(8,128)(2,1)S(1)}, bf16[16,1024]{1,0:T(8,128)(2,1)S(1)}, u32[]{:S(2)}, u32[]{:S(2)}) collective-permute-start(bf16[16,1024]{1,0:T(8,128)(2,1)S(1)} %get-tuple-element.62), channel_id=1, source_target_pairs={{0,2},{1,3},{2,0},{3,1},{4,6},{5,7},{6,4},{7,5},{8,10},{9,11},{10,... | collective-permute-start | bytes 98312 | tf_op jit(solution)/shard_map/ppermute | solution.py:222
  46.3 4.8 %collective-permute-start.12 = (bf16[16,1024]{1,0:T(8,128)(2,1)S(1)}, bf16[16,1024]{1,0:T(8,128)(2,1)S(1)}, u32[]{:S(2)}, u32[]{:S(2)}) collective-permute-start(bf16[16,1024]{1,0:T(8,128)(2,1)S(1)} %get-tuple-element.63), channel_id=1, source_target_pairs={{0,1},{1,0},{2,3},{3,2},{4,5},{5,4},{6,7},{7,6},{8,9},{9,8},{10,11... | collective-permute-start | bytes 98312 | tf_op jit(solution)/shard_map/ppermute | solution.py:222

commit v4 on v3

v4 whole, which is shorter than its diff:
```python
import functools

import jax
import jax.numpy as jnp
from jax import lax
from jax.experimental import pallas as pl
from jax.experimental.pallas import tpu as pltpu
from jax.sharding import PartitionSpec as P

BF = jnp.bfloat16
F32 = jnp.float32
VM = pl.BlockSpec(memory_space=pltpu.VMEM)
HBM = pl.BlockSpec(memory_space=pltpu.HBM)
ROWS = 16
EIGHT = 8


def dot_nn(a, b):
    return lax.dot_general(a, b, (((1,), (0,)), ((), ())), preferred_element_type=F32)


def dot_nt(a, b):
    return lax.dot_general(a, b, (((1,), (1,)), ((), ())), preferred_element_type=F32)


def dot_tn(a, b):
    return lax.dot_general(a, b, (((0,), (0,)), ((), ())), preferred_element_type=F32)


def params(mib):
    return pltpu.CompilerParams(vmem_limit_bytes=mib << 20)


def share_kernel(route_ref, gates_ref, out_ref):
    tok = route_ref.shape[1]
    lanes = out_ref.shape[1]
    hit = route_ref[...] == lax.axis_index("expert")
    routed = jnp.sum(jnp.where(hit, 1.0, 0.0), axis=0, keepdims=True)
    gate = jnp.sum(jnp.where(hit, gates_ref[...], 0.0), axis=0, keepdims=True)
    row = lax.broadcasted_iota(jnp.int32, (tok, tok), 0)
    col = lax.broadcasted_iota(jnp.int32, (tok, tok), 1)
    square = jnp.broadcast_to(routed, (tok, tok))
    routed_col = jnp.sum(jnp.where(row == col, square, 0.0), axis=1, keepdims=True)
    slot_col = jnp.sum(jnp.where(col < row, square, 0.0), axis=1, keepdims=True)
    slot = jnp.sum(jnp.where(row < col, routed_col, 0.0), axis=0, keepdims=True)
    at = lax.broadcasted_iota(jnp.int32, (ROWS, tok), 0).astype(F32)
    pick = jnp.where(at == slot, routed, 0.0)
    weight = jnp.sum(pick * gate, axis=1, keepdims=True)
    out_ref[...] = jnp.zeros_like(out_ref)
    out_ref[:ROWS] = jnp.broadcast_to(weight, (ROWS, lanes))
    out_ref[ROWS : 2 * ROWS, :tok] = pick
    at = lax.broadcasted_iota(jnp.int32, (tok, lanes), 1).astype(F32)
    out_ref[2 * ROWS : 2 * ROWS + tok] = jnp.where(at == slot_col, routed_col, 0.0)


def odd(k):
    return (k ^ (k >> 1) ^ (k >> 2)) & 1


def extra_place(column, extra, d):
    piece = 2 * d // EIGHT
    if isinstance(column, int):
        return column // piece, extra * piece + column % piece
    return lax.div(column, piece), extra * piece + lax.rem(column, piece)


def lanes_at(column, width):
    if not isinstance(column, int):
        column = pl.multiple_of(column, 128)
    return pl.ds(column, width)


def pair_kernel(a_ref, b_ref, out_ref):
    n = a_ref.shape[0]
    out_ref[:n] = a_ref[...]
    out_ref[n:] = b_ref[...]


def join_kernel(patterns, slots, mine_ref, other_ref, a_ref, b_ref, out_ref, tail_ref):
    half, tok, width = a_ref.shape
    width //= 2
    d = len(patterns) * width
    me = lax.axis_index("expert")
    for i, k in enumerate(patterns):
        info = other_ref if odd(k) else mine_ref
        block = a_ref[i] if i < half else b_ref[i - half]
        picked = dot_nn(info[ROWS : 2 * ROWS, :tok].astype(BF), block)
        dys = info[:ROWS, :1] * picked[:, width:]
        for at, rows in ((0, picked[:, :width]), (d, dys)):
            column = at + (me ^ k) * width
            out_ref[:, lanes_at(column, width)] = rows[:EIGHT].astype(BF)
            for x in range(slots - EIGHT):
                r, c = extra_place(column, x, d)
                tail_ref[pl.ds(r, 1), lanes_at(c, width)] = rows[EIGHT + x : EIGHT + x + 1]
    if slots > EIGHT:
        out_ref[:, 2 * d :] = tail_ref[...].astype(BF)


def stack_kernel(*refs):
    out_ref = refs[-1]
    for k, ref in enumerate(refs[:-1]):
        out_ref[k] = ref[...]


def expert_kernel(
    near_ref, far_ref, wg_ref, wu_ref, wd_ref,
    keep_ref, send_ref, xs_ref, dys_ref, hidt_ref, gpgt_ref, gput_ref,
    hid_ref, gpg_ref, gpu_ref, tail_ref,
    *, tile, cols, slots,
):
    n = near_ref.shape[0]
    f, d = wg_ref.shape
    width = d // lax.axis_size("expert")
    piece = 2 * d // EIGHT
    me = lax.axis_index("expert")
    first = lax.broadcasted_iota(jnp.int32, (EIGHT, width), 0)
    for j in range(d // width):
        for crossed in range(2):

            @pl.when(odd(me ^ j) == crossed)
            def _(j=j, crossed=crossed):
                for b in range(n):
                    near, far = near_ref.at[b], far_ref.at[b]
                    if crossed ^ (b > 0):
                        near, far = far, near
                    for at, ref in ((b * ROWS, near), ((n + b) * ROWS, far)):
                        for base, to in ((0, xs_ref), (d, dys_ref)):
                            part = slice(j * width, (j + 1) * width)
                            column = base + j * width
                            to[at : at + EIGHT, part] = ref[:, column : column + width]
                            rest = jnp.zeros((EIGHT, width), F32)
                            for x in range(slots - EIGHT):
                                r, c = extra_place(column, x, d)
                                tail = ref[:, 2 * d + c : 2 * d + c + width].astype(F32)
                                rest = jnp.where(first == x, tail[r : r + 1], rest)
                            to[at + EIGHT : at + ROWS, part] = rest.astype(BF)

    xs = xs_ref[...]
    dys = dys_ref[...]
    for i in range(f // tile):
        units = slice(i * tile, (i + 1) * tile)
        pre_gate = dot_nt(xs, wg_ref[units, :])
        pre_up = dot_nt(xs, wu_ref[units, :])
        grad_hidden = dot_nt(dys, wd_ref[units, :])
        sig = jax.nn.sigmoid(pre_gate)
        silu = pre_gate * sig
        hidden = (silu * pre_up).astype(BF)
        gpg = (grad_hidden * pre_up * sig * (1.0 + pre_gate * (1.0 - sig))).astype(BF)
        gpu = (grad_hidden * silu).astype(BF)
        hid_ref[:, units] = hidden
        gpg_ref[:, units] = gpg
        gpu_ref[:, units] = gpu
        hidt_ref[units, :] = hidden.T
        gpgt_ref[units, :] = gpg.T
        gput_ref[units, :] = gpu.T
    hidden = hid_ref[...]
    gpg = gpg_ref[...]
    gpu = gpu_ref[...]
    for j in range(d // cols):
        part = slice(j * cols, (j + 1) * cols)
        out = dot_nn(hidden, wd_ref[:, part])
        grad = dot_nn(gpg, wg_ref[:, part]) + dot_nn(gpu, wu_ref[:, part])
        own = me == j * cols // width
        for at, value in ((j * cols, out), (d + j * cols, grad)):
            near, far = value[: n * ROWS], value[n * ROWS :]
            near, far = jnp.where(own, near, far), jnp.where(own, far, near)
            for b in range(n):
                pairs = ((0, keep_ref, near), (1, send_ref, far))
                if b > 0:
                    pairs = ((0, keep_ref, far), (1, send_ref, near))
                for h, to, rows in pairs:
                    rows = rows[b * ROWS : (b + 1) * ROWS]
                    to[b, :, at : at + cols] = rows[:EIGHT].astype(BF)
                    for x in range(slots - EIGHT):
                        r, c = extra_place(at, x, d)
                        tail_ref[h, b, r : r + 1, c : c + cols] = rows[EIGHT + x : EIGHT + x + 1]
    if slots > EIGHT:
        keep_ref[:, :, 2 * d :] = tail_ref[0].astype(BF)
        send_ref[:, :, 2 * d :] = tail_ref[1].astype(BF)


def grads_kernel(jobs, n, n_old, *refs):
    lefts, rights = refs[:n], refs[n : 2 * n]
    outs, (buf, sems) = refs[2 * n + n_old : 3 * n + n_old], refs[3 * n + n_old :]
    slots = buf.shape[0]
    copies = []
    for i, (a, start, size) in enumerate(jobs):
        slot = i % slots
        if i >= slots:
            copies[i - slots].wait()
        rows = pl.ds(start, size)
        buf[slot, :size] = dot_nn(lefts[a][rows, :], rights[a][...]).astype(BF)
        copy = pltpu.make_async_copy(buf.at[slot, pl.ds(0, size)], outs[a].at[rows, :], sems.at[slot])
        copy.start()
        copies.append(copy)
    for copy in copies[-slots:]:
        copy.wait()


def cores_kernel(keep_ref, got_ref, *out_refs):
    for k, out_ref in enumerate(out_refs):
        out_ref[...] = (keep_ref[k].astype(F32) + got_ref[k].astype(F32)).astype(BF)


def chips_kernel(n, slots, mine_ref, other_ref, *refs):
    ins, outs, total_ref = refs[:n], refs[n:-1], refs[-1]
    tok, width = outs[0].shape
    width //= 2
    d = len(outs) * width
    total = ins[0][...].astype(F32)
    for ref in ins[1:]:
        total = total + ref[...].astype(F32)
    total_ref[...] = total
    first = lax.broadcasted_iota(jnp.int32, (EIGHT, width), 0)
    me = lax.axis_index("expert")

    def rows_at(column):
        rest = jnp.zeros((EIGHT, width), F32)
        for x in range(slots - EIGHT):
            r, c = extra_place(column, x, d)
            row = total_ref[pl.ds(r, 1), lanes_at(2 * d + c, width)]
            rest = jnp.where(first == x, row, rest)
        return jnp.concatenate([total_ref[:, lanes_at(column, width)], rest], axis=0)

    for k, out_ref in enumerate(outs):
        info = other_ref if k else mine_ref
        column = (me ^ k) * width
        rows = jnp.concatenate(
            [(info[:ROWS, :1] * rows_at(column)).astype(BF), rows_at(d + column).astype(BF)], axis=1
        )
        back = info[2 * ROWS : 2 * ROWS + tok, :ROWS].astype(BF)
        out_ref[...] = dot_nn(back, rows).astype(BF)


def home_kernel(*refs):
    ins, (mixed_ref, grad_ref) = refs[:-2], refs[-2:]
    width = mixed_ref.shape[1]
    total = ins[0][...].astype(F32)
    for ref in ins[1:]:
        total = total + ref[...].astype(F32)
    mixed_ref[...] = total[:, :width].astype(BF)
    grad_ref[...] = total[:, width:].astype(BF)


def grads(jobs, lefts, rights, old):
    n = len(lefts)
    f, rows = lefts[0].shape
    d = rights[0].shape[1]
    kept = [a for a in range(n) if old[a] is not None]
    size = max(job[2] for job in jobs)
    done = sum(job[2] for job in jobs)
    return pl.pallas_call(
        functools.partial(grads_kernel, jobs, n, len(kept)),
        in_specs=[VM] * (2 * n) + [HBM] * len(kept),
        out_specs=[HBM] * n,
        out_shape=[jax.ShapeDtypeStruct((f, d), BF)] * n,
        scratch_shapes=[pltpu.VMEM((3, size, d), BF), pltpu.SemaphoreType.DMA((3,))],
        input_output_aliases={2 * n + i: a for i, a in enumerate(kept)},
        compiler_params=params(((6 * size * d + n * 2 * rows * (f + d)) >> 20) + 4),
        cost_estimate=pl.CostEstimate(
            flops=2 * rows * done * d, bytes_accessed=3 * done * d, transcendentals=0
        ),
        name="grads",
    )(*lefts, *rights, *[old[a] for a in kept])


def stack(kernel, arrays, shape, name, scratch=()):
    size = sum(a.size * a.dtype.itemsize for a in arrays)
    return pl.pallas_call(
        kernel,
        in_specs=[VM] * len(arrays),
        out_specs=VM,
        out_shape=jax.ShapeDtypeStruct(shape, BF),
        scratch_shapes=scratch,
        compiler_params=params((size >> 19) + 2),
        name=name,
    )(*arrays)


def per_device(tokens, cotangent, route, gates, w_gate, w_up, w_down):
    n_dp = lax.axis_size("dp")
    n_e = lax.axis_size("expert")
    tok, width = tokens.shape
    d = width * n_e
    f = w_gate.shape[1]
    tile = 256 if f % 256 == 0 else f
    rows = n_dp * ROWS
    n_chip = n_dp // 2
    sds = jax.ShapeDtypeStruct

    def swap(x, chips, experts, core):
        return lax.ppermute(
            x,
            ("dp", "expert"),
            [
                (i * n_e + j, (i ^ (2 * chips + core)) * n_e + (j ^ experts))
                for i in range(n_dp)
                for j in range(n_e)
            ],
        )

    small = n_chip + 4
    slots = min(tok, max(2, 3 * tok // n_e))
    piece = 2 * d // EIGHT
    tail = max(0, slots - EIGHT) * piece
    block_shape = (EIGHT, 2 * d + tail)
    tail_scratch = (EIGHT, max(tail, 128))
    mine = jnp.concatenate([tokens, cotangent], axis=1)[None]
    patterns, hop, first = [0], n_e // 2, True
    while hop:
        patterns = patterns + [p ^ hop for p in patterns]
        got = swap(mine, 0, hop, 1)
        if first:
            info = pl.pallas_call(
                share_kernel,
                in_specs=[VM, VM],
                out_specs=VM,
                out_shape=sds((3 * ROWS, 128), F32),
                compiler_params=params(2),
                cost_estimate=pl.CostEstimate(
                    flops=40 * rows * f * d, bytes_accessed=24 * f * d, transcendentals=0
                ),
                name="share",
            )(route.T, gates.T)
            first = False
            got, info = lax.optimization_barrier((got, info))
            other = swap(info, 0, 0, 1)
        if hop == 1:
            block = stack(
                functools.partial(join_kernel, tuple(patterns), slots),
                [info, other, mine, got],
                block_shape,
                "join",
                [pltpu.VMEM(tail_scratch, F32)],
            )
        else:
            mine = stack(pair_kernel, [mine, got], (len(patterns), tok, 2 * width), "pair")
        hop //= 2
    blocks = [block] + [swap(block, k, 0, 1) for k in range(1, n_chip)]
    near = stack(stack_kernel, blocks, (n_chip,) + block_shape, "stack")
    far = swap(near, 0, 0, 1)

    held = 2 * f * d + rows * (16 * d + 12 * f)
    keep, send, xs, dys, hidden, gpg, gpu = pl.pallas_call(
        functools.partial(expert_kernel, tile=tile, cols=256, slots=slots),
        in_specs=[VM] * 5,
        out_specs=[VM] * 7,
        out_shape=[sds((n_chip,) + block_shape, BF)] * 2
        + [sds((rows, d), BF)] * 2
        + [sds((f, rows), BF)] * 3,
        scratch_shapes=[pltpu.VMEM((rows, f), BF)] * 3
        + [pltpu.VMEM((2, n_chip) + tail_scratch, F32)],
        compiler_params=params((held >> 20) + 4),
        cost_estimate=pl.CostEstimate(
            flops=12 * rows * f * d, bytes_accessed=6 * f * d, transcendentals=rows * f
        ),
        name="expert",
    )(near, far, w_gate[0], w_up[0], w_down[0])

    received = swap(send, 0, 0, 1)
    third, part = f // 3, f // 12
    whole = [(1, i * third, third) for i in range(3)]
    (down,) = grads([(0, 0, 2 * part)], [hidden], [dys], [None])
    received, down = lax.optimization_barrier((received, down))
    parts = pl.pallas_call(
        cores_kernel,
        in_specs=[VM, VM],
        out_specs=[VM] * n_chip,
        out_shape=[sds(block_shape, BF)] * n_chip,
        compiler_params=params(small),
        name="cores",
    )(keep, received)
    arrived = [swap(parts[k], k, 0, 1) for k in range(n_chip - 1, 0, -1)]
    down, grad_gate = grads([(0, 2 * part, 4 * part), (0, 6 * part, 3 * part)] + whole, [hidden, gpg], [dys, xs], [down, None])
    arrived, down, grad_gate = lax.optimization_barrier((arrived, down, grad_gate))
    summed = pl.pallas_call(
        functools.partial(chips_kernel, n_chip, slots),
        in_specs=[VM] * (n_chip + 2),
        out_specs=[VM] * n_e,
        out_shape=[sds((tok, 2 * width), BF)] * n_e,
        scratch_shapes=[pltpu.VMEM(block_shape, F32)],
        compiler_params=params(small),
        name="chips",
    )(info, other, parts[0], *arrived)
    home = [summed[0]] + [swap(summed[k], 0, k, 1) for k in range(n_e - 1, 0, -1)]
    grad_down, grad_up = grads(
        [(0, 9 * part, 3 * part)] + whole, [hidden, gpu], [dys, xs], [down, None]
    )
    home, grad_down, grad_up = lax.optimization_barrier((home, grad_down, grad_up))
    mixed, grad_tokens = pl.pallas_call(
        home_kernel,
        in_specs=[VM] * n_e,
        out_specs=[VM] * 2,
        out_shape=[sds((tok, width), BF)] * 2,
        compiler_params=params(4),
        name="home",
    )(*home)
    return mixed, grad_tokens, grad_gate[None], grad_up[None], grad_down[None]


def solution(mesh):
    return jax.shard_map(
        per_device,
        mesh=mesh,
        in_specs=(
            P("dp", "expert"),
            P("dp", "expert"),
            P("dp", None),
            P("dp", None),
            P("expert", "dp", None),
            P("expert", "dp", None),
            P("expert", "dp", None),
        ),
        out_specs=(
            P("dp", "expert"),
            P("dp", "expert"),
            P("expert", "dp", None),
            P("expert", "dp", None),
            P("expert", "dp", None),
        ),
        check_vma=False,
    )
```

time: 52.2 us -> 48.8 us (0.935)
  waiting for transfers between devices: 11.8 us -> 7.56 us
    ppermute x13 -> x14, waiting for transfers between devices: 11.8 us -> 7.56 us  [swap(): lax.ppermute(x, ('dp', 'expert'), [(i * n_e + j, (i ^ 2 * chips + core) *...]
    ppermute x13 -> x14, starting transfers between devices: 17.4 us -> 17.8 us  [swap(): lax.ppermute(x, ('dp', 'expert'), [(i * n_e + j, (i ^ 2 * chips + core) *...]
  transfers between devices with their start and end apart: 13 -> 14, of which waited for: 10 -> 7; matrix products, arithmetic and copies ran while one was open for 0% -> 0% of each run, Pallas kernels for 19% -> 21%
where the time goes in v4:
time: 48.8 us; the launch traced here: 48.4 us
  Pallas kernels  20.2 us (41%)
  starting transfers between devices  17.8 us (36%)
  waiting for transfers between devices  7.56 us (15%)
  local copies, waits for them, and re-layouts  1.37 us (3%)
  between operations  0.75 us (2%)
  other arithmetic  0.74 us (2%)
    ppermute x14, starting transfers between devices, swap(): lax.ppermute(x, ('dp', 'expert'), [(i * n_e + j, (i ^ 2 * chips + core) *...  17.8 us
    pallas_call x3, Pallas kernels, grads(): pl.pallas_call(functools.partial(grads_kernel, jobs, n, len(kept)), in_sp...  9.99 us
    pallas_call x1, Pallas kernels, per_device(): pl.pallas_call(functools.partial(expert_kernel, tile=tile, cols=256, slot...  8.93 us
    ppermute x14, waiting for transfers between devices, swap(): lax.ppermute(x, ('dp', 'expert'), [(i * n_e + j, (i ^ 2 * chips + core) *...  7.56 us
    unnamed x10, local copies, waits for them, and re-layouts  1.37 us
  transfers between devices with their start and end apart: 14, of which 7 were waited for; matrix products, arithmetic and copies ran while one was open for 0% of the time, Pallas kernels for 21%

profile of v4, /device:TPU:0, one launch (start us, length us, event | category | flops | bytes accessed | tf_op | source)
XLA Modules:
  0.0 48.4 jit_solution(2265278094557786545)
XLA Ops:
  0.6 0.7 %maximum_bitcast_fusion.a_ref = bf16[1,12,1024]{2,1,0:T(8,128)(2,1)S(1)} fusion(bf16[12,512]{1,0:T(8,128)(2,1)} %param.8, bf16[12,512]{1,0:T(8,128)(2,1)} %param.7), kind=kLoop, calls=%fused_computation | loop fusion | flops 49152 | bytes 49152 | tf_op jit(solution)/shard_map/broadcast_in_dim | solution.py:308
  1.4 3.5 %collective-permute-start = (bf16[1,12,1024]{2,1,0:T(8,128)(2,1)S(1)}, bf16[1,12,1024]{2,1,0:T(8,128)(2,1)S(1)}, u32[]{:S(2)}, u32[]{:S(2)}) collective-permute-start(bf16[1,12,1024]{2,1,0:T(8,128)(2,1)S(1)} %maximum_bitcast_fusion.a_ref), channel_id=1, source_target_pairs={{0,6},{1,7},{2,4},{3,5},{4,2},{5,3},{6,0},{7,1},{8,14},{9,15},{10,... | collective-permute-start | bytes 73736 | tf_op jit(solution)/shard_map/ppermute | solution.py:292
  4.9 0.0 copy-start.3
  4.9 0.7 %copy-done.3 = s32[12,2]{0,1:T(2,128)S(1)} copy-done((s32[12,2]{0,1:T(2,128)S(1)}, s32[12,2]{0,1:T(2,128)}, u32[]{:S(2)}) %copy-start.3) | copy-done | bytes 120
  5.5 0.0 copy-start.4
  5.5 0.7 %copy-done.4 = f32[12,2]{0,1:T(2,128)S(1)} copy-done((f32[12,2]{0,1:T(2,128)S(1)}, f32[12,2]{0,1:T(2,128)}, u32[]{:S(2)}) %copy-start.4) | copy-done | bytes 120
  6.2 0.0 copy-start
  6.2 0.0 copy-start.1
  6.2 0.0 copy-start.2
  6.2 0.2 share.1.mine_ref
  6.4 0.2 collective-permute-done.b_ref
  6.6 1.8 %collective-permute-start.2 = (bf16[2,12,1024]{2,1,0:T(8,128)(2,1)S(1)}, bf16[2,12,1024]{2,1,0:T(8,128)(2,1)S(1)}, u32[]{:S(2)}, u32[]{:S(2)}) collective-permute-start(bf16[2,12,1024]{2,1,0:T(8,128)(2,1)S(1)} %pair.1.a_ref), channel_id=1, source_target_pairs={{0,5},{1,4},{2,7},{3,6},{4,1},{5,0},{6,3},{7,2},{8,13},{9,12},{10,... | collective-permute-start | bytes 147464 | tf_op jit(solution)/shard_map/ppermute | solution.py:292
  8.5 0.4 collective-permute-start.1
  8.9 0.8 %collective-permute-done.1.other_ref = f32[48,128]{1,0:T(8,128)S(1)} collective-permute-done((f32[48,128]{1,0:T(8,128)S(1)}, f32[48,128]{1,0:T(8,128)S(1)}, u32[]{:S(2)}, u32[]{:S(2)}) %collective-permute-start.1) | collective-permute-done | bytes 24608 | tf_op jit(solution)/shard_map/ppermute | solution.py:292
  9.7 0.9 %collective-permute-done.2.b_ref = bf16[2,12,1024]{2,1,0:T(8,128)(2,1)S(1)} collective-permute-done((bf16[2,12,1024]{2,1,0:T(8,128)(2,1)S(1)}, bf16[2,12,1024]{2,1,0:T(8,128)(2,1)S(1)}, u32[]{:S(2)}, u32[]{:S(2)}) %collective-permute-start.2) | collective-permute-done | bytes 49184 | tf_op jit(solution)/shard_map/ppermute | solution.py:292
  10.7 0.2 join.1.refs_0_
  10.8 2.8 %collective-permute-start.5 = (bf16[8,4608]{1,0:T(8,128)(2,1)S(1)}, bf16[8,4608]{1,0:T(8,128)(2,1)S(1)}, u32[]{:S(2)}, u32[]{:S(2)}) collective-permute-start(bf16[8,4608]{1,0:T(8,128)(2,1)S(1)} %join.1.refs_0_), channel_id=1, source_target_pairs={{0,28},{1,29},{2,30},{3,31},{4,24},{5,25},{6,26},{7,27},{8,20},{9,... | collective-permute-start | bytes 221192 | tf_op jit(solution)/shard_map/ppermute | solution.py:292
  13.7 0.5 %collective-permute-start.4 = (bf16[8,4608]{1,0:T(8,128)(2,1)S(1)}, bf16[8,4608]{1,0:T(8,128)(2,1)S(1)}, u32[]{:S(2)}, u32[]{:S(2)}) collective-permute-start(bf16[8,4608]{1,0:T(8,128)(2,1)S(1)} %join.1.refs_0_), channel_id=1, source_target_pairs={{0,20},{1,21},{2,22},{3,23},{4,16},{5,17},{6,18},{7,19},{8,28},{9,... | collective-permute-start | bytes 221192 | tf_op jit(solution)/shard_map/ppermute | solution.py:292
  14.2 0.2 collective-permute-start.3
  14.4 2.0 %collective-permute-done.5.refs_3_ = bf16[8,4608]{1,0:T(8,128)(2,1)S(1)} collective-permute-done((bf16[8,4608]{1,0:T(8,128)(2,1)S(1)}, bf16[8,4608]{1,0:T(8,128)(2,1)S(1)}, u32[]{:S(2)}, u32[]{:S(2)}) %collective-permute-start.5) | collective-permute-done | bytes 73760 | tf_op jit(solution)/shard_map/ppermute | solution.py:292
  16.4 1.3 %collective-permute-done.4.refs_2_ = bf16[8,4608]{1,0:T(8,128)(2,1)S(1)} collective-permute-done((bf16[8,4608]{1,0:T(8,128)(2,1)S(1)}, bf16[8,4608]{1,0:T(8,128)(2,1)S(1)}, u32[]{:S(2)}, u32[]{:S(2)}) %collective-permute-start.4) | collective-permute-done | bytes 73760 | tf_op jit(solution)/shard_map/ppermute | solution.py:292
  17.7 0.7 %collective-permute-done.3.refs_1_ = bf16[8,4608]{1,0:T(8,128)(2,1)S(1)} collective-permute-done((bf16[8,4608]{1,0:T(8,128)(2,1)S(1)}, bf16[8,4608]{1,0:T(8,128)(2,1)S(1)}, u32[]{:S(2)}, u32[]{:S(2)}) %collective-permute-start.3) | collective-permute-done | bytes 73760 | tf_op jit(solution)/shard_map/ppermute | solution.py:292
  18.4 0.2 collective-permute-start.6
  18.7 1.4 %collective-permute-done.6.far_ref = bf16[4,8,4608]{2,1,0:T(8,128)(2,1)S(1)} collective-permute-done((bf16[4,8,4608]{2,1,0:T(8,128)(2,1)S(1)}, bf16[4,8,4608]{2,1,0:T(8,128)(2,1)S(1)}, u32[]{:S(2)}, u32[]{:S(2)}) %collective-permute-start.6) | collective-permute-done | bytes 294944 | tf_op jit(solution)/shard_map/ppermute | solution.py:292
  20.1 0.0 copy-done
  20.1 0.0 copy-done.1
  20.1 0.0 copy-done.2
  20.1 8.9 %expert.1 = (bf16[4,8,4608]{2,1,0:T(8,128)(2,1)S(1)}, bf16[4,8,4608]{2,1,0:T(8,128)(2,1)S(1)}, bf16[128,2048]{1,0:T(8,128)(2,1)S(1)}, bf16[128,2048]{1,0:T(8,128...) custom-call(bf16[4,8,4608]{2,1,0:T(8,128)(2,1)S(1)} %stack.1.near_ref, ...), custom_call_target="tpu_custom_call" | custom-call | flops 4831838208 | bytes 18874368 | tf_op jit(solution)/shard_map/expert/pallas_call | solution.py:344
  29.0 0.2 collective-permute-start.7
  29.3 1.4 %grads.3.refs_4_ = bf16[1536,2048]{1,0:T(8,128)(2,1)} custom-call(bf16[1536,128]{1,0:T(8,128)(2,1)S(1)} %get-tuple-element.45.refs_0_, bf16[128,2048]{1,0:T(8,128)(2,1)S(1)} %get-tuple-element.46.refs_1_.refs_2_), custom_call_target="tpu_custom_call" | custom-call | flops 134217728 | bytes 1572864 | tf_op jit(solution)/shard_map/grads/pallas_call | solution.py:252
  30.7 0.0 collective-permute-done.7.got_ref
  30.7 0.1 cores.1
  30.8 1.5 %collective-permute-start.8 = (bf16[8,4608]{1,0:T(8,128)(2,1)S(1)}, bf16[8,4608]{1,0:T(8,128)(2,1)S(1)}, u32[]{:S(2)}, u32[]{:S(2)}) collective-permute-start(bf16[8,4608]{1,0:T(8,128)(2,1)S(1)} %get-tuple-element.49), channel_id=1, source_target_pairs={{0,28},{1,29},{2,30},{3,31},{4,24},{5,25},{6,26},{7,27},{8,20},{9,... | collective-permute-start | bytes 221192 | tf_op jit(solution)/shard_map/ppermute | solution.py:292
  32.3 1.3 %collective-permute-start.9 = (bf16[8,4608]{1,0:T(8,128)(2,1)S(1)}, bf16[8,4608]{1,0:T(8,128)(2,1)S(1)}, u32[]{:S(2)}, u32[]{:S(2)}) collective-permute-start(bf16[8,4608]{1,0:T(8,128)(2,1)S(1)} %get-tuple-element.50), channel_id=1, source_target_pairs={{0,20},{1,21},{2,22},{3,23},{4,16},{5,17},{6,18},{7,19},{8,28},{9,... | collective-permute-start | bytes 221192 | tf_op jit(solution)/shard_map/ppermute | solution.py:292
  33.6 0.4 collective-permute-start.10
  34.0 4.7 %grads.4 = (bf16[1536,2048]{1,0:T(8,128)(2,1)}, bf16[1536,2048]{1,0:T(8,128)(2,1)}) custom-call(bf16[1536,128]{1,0:T(8,128)(2,1)S(1)} %get-tuple-element.45.refs_0_, bf16[1536,128]{1,0:T(8,128)(2,1)S(1)} %get-tuple-element.52.refs_1_, bf16[128,2048]{1,0:T(8,128)(2,1)S(1)} %get-tuple-element.46.refs_1_.refs_2_, ...), custom_call_target="tpu_custom_call", output_to_operand_aliasing={{0}: (4, {})} | custom-call | flops 1275068416 | bytes 14942208 | tf_op jit(solution)/shard_map/grads/pallas_call | solution.py:252
  38.8 0.0 collective-permute-done.8.refs_1_
  38.8 0.0 collective-permute-done.9.refs_2_
  38.8 0.0 collective-permute-done.10.refs_3_
  38.8 0.2 chips.1
  39.0 4.3 %collective-permute-start.11 = (bf16[12,1024]{1,0:T(8,128)(2,1)S(1)}, bf16[12,1024]{1,0:T(8,128)(2,1)S(1)}, u32[]{:S(2)}, u32[]{:S(2)}) collective-permute-start(bf16[12,1024]{1,0:T(8,128)(2,1)S(1)} %get-tuple-element.61), channel_id=1, source_target_pairs={{0,7},{1,6},{2,5},{3,4},{4,3},{5,2},{6,1},{7,0},{8,15},{9,14},{10,... | collective-permute-start | bytes 73736 | tf_op jit(solution)/shard_map/ppermute | solution.py:292
  43.3 0.0 collective-permute-start.12
  43.3 0.6 %collective-permute-start.13 = (bf16[12,1024]{1,0:T(8,128)(2,1)S(1)}, bf16[12,1024]{1,0:T(8,128)(2,1)S(1)}, u32[]{:S(2)}, u32[]{:S(2)}) collective-permute-start(bf16[12,1024]{1,0:T(8,128)(2,1)S(1)} %get-tuple-element.63), channel_id=1, source_target_pairs={{0,5},{1,4},{2,7},{3,6},{4,1},{5,0},{6,3},{7,2},{8,13},{9,12},{10,... | collective-permute-start | bytes 73736 | tf_op jit(solution)/shard_map/ppermute | solution.py:292
  43.9 3.8 %grads.5 = (bf16[1536,2048]{1,0:T(8,128)(2,1)}, bf16[1536,2048]{1,0:T(8,128)(2,1)}) custom-call(bf16[1536,128]{1,0:T(8,128)(2,1)S(1)} %get-tuple-element.45.refs_0_, bf16[1536,128]{1,0:T(8,128)(2,1)S(1)} %get-tuple-element.64.refs_1_, bf16[128,2048]{1,0:T(8,128)(2,1)S(1)} %get-tuple-element.46.refs_1_.refs_2_, ...), custom_call_target="tpu_custom_call", output_to_operand_aliasing={{0}: (4, {})} | custom-call | flops 1006632960 | bytes 11796480 | tf_op jit(solution)/shard_map/grads/pallas_call | solution.py:252
  47.7 0.0 collective-permute-done.11.refs_1_
  47.7 0.0 collective-permute-done.12.refs_2_
  47.8 0.0 collective-permute-done.13.refs_3_
  47.8 0.6 %home.1 = (bf16[12,512]{1,0:T(8,128)(2,1)}, bf16[12,512]{1,0:T(8,128)(2,1)}) custom-call(bf16[12,1024]{1,0:T(8,128)(2,1)S(1)} %get-tuple-element.68.refs_0_, bf16[12,1024]{1,0:T(8,128)(2,1)S(1)} %collective-permute-done.11.refs_1_, bf16[12,1024]{1,0:T(8,128)(2,1)S(1)} %collective-permute-done.12.refs_2_, bf16[12,1024]{1,0:T(8,128)(2,1)S(1)} %collective-permute-done.13.refs_3_), custom_call_target="tpu_custom_call" | custom-call | tf_op jit(solution)/shard_map/home/pallas_call | solution.py:390
  (2 shorter events, 0.0 us)
Async XLA Ops:
  1.4 5.3 %collective-permute-start = (bf16[1,12,1024]{2,1,0:T(8,128)(2,1)S(1)}, bf16[1,12,1024]{2,1,0:T(8,128)(2,1)S(1)}, u32[]{:S(2)}, u32[]{:S(2)}) collective-permute-start(bf16[1,12,1024]{2,1,0:T(8,128)(2,1)S(1)} %maximum_bitcast_fusion.a_ref), channel_id=1, source_target_pairs={{0,6},{1,7},{2,4},{3,5},{4,2},{5,3},{6,0},{7,1},{8,14},{9,15},{10,... | collective-permute-start | bytes 73736 | tf_op jit(solution)/shard_map/ppermute | solution.py:292
  4.9 0.7 %copy-start.3 = (s32[12,2]{0,1:T(2,128)S(1)}, s32[12,2]{0,1:T(2,128)}, u32[]{:S(2)}) copy-start(s32[12,2]{0,1:T(2,128)} %param.9) | copy-start | bytes 292
  5.5 0.7 %copy-start.4 = (f32[12,2]{0,1:T(2,128)S(1)}, f32[12,2]{0,1:T(2,128)}, u32[]{:S(2)}) copy-start(f32[12,2]{0,1:T(2,128)} %param.10) | copy-start | bytes 292
  6.2 13.9 %copy-start = (bf16[1,1536,2048]{2,1,0:T(8,128)(2,1)S(1)}, bf16[1,1536,2048]{2,1,0:T(8,128)(2,1)}, u32[]{:S(2)}) copy-start(bf16[1,1536,2048]{2,1,0:T(8,128)(2,1)} %param.11) | copy-start | bytes 18874372
  6.2 13.9 %copy-start.1 = (bf16[1,1536,2048]{2,1,0:T(8,128)(2,1)S(1)}, bf16[1,1536,2048]{2,1,0:T(8,128)(2,1)}, u32[]{:S(2)}) copy-start(bf16[1,1536,2048]{2,1,0:T(8,128)(2,1)} %param.12) | copy-start | bytes 18874372
  6.2 13.9 %copy-start.2 = (bf16[1,1536,2048]{2,1,0:T(8,128)(2,1)S(1)}, bf16[1,1536,2048]{2,1,0:T(8,128)(2,1)}, u32[]{:S(2)}) copy-start(bf16[1,1536,2048]{2,1,0:T(8,128)(2,1)} %param.13) | copy-start | bytes 18874372
  6.6 4.0 %collective-permute-start.2 = (bf16[2,12,1024]{2,1,0:T(8,128)(2,1)S(1)}, bf16[2,12,1024]{2,1,0:T(8,128)(2,1)S(1)}, u32[]{:S(2)}, u32[]{:S(2)}) collective-permute-start(bf16[2,12,1024]{2,1,0:T(8,128)(2,1)S(1)} %pair.1.a_ref), channel_id=1, source_target_pairs={{0,5},{1,4},{2,7},{3,6},{4,1},{5,0},{6,3},{7,2},{8,13},{9,12},{10,... | collective-permute-start | bytes 147464 | tf_op jit(solution)/shard_map/ppermute | solution.py:292
  8.5 1.2 %collective-permute-start.1 = (f32[48,128]{1,0:T(8,128)S(1)}, f32[48,128]{1,0:T(8,128)S(1)}, u32[]{:S(2)}, u32[]{:S(2)}) collective-permute-start(f32[48,128]{1,0:T(8,128)S(1)} %share.1.mine_ref), channel_id=1, source_target_pairs={{0,4},{1,5},{2,6},{3,7},{4,0},{5,1},{6,2},{7,3},{8,12},{9,13},{10,... | collective-permute-start | bytes 73736 | tf_op jit(solution)/shard_map/ppermute | solution.py:292
  10.8 5.5 %collective-permute-start.5 = (bf16[8,4608]{1,0:T(8,128)(2,1)S(1)}, bf16[8,4608]{1,0:T(8,128)(2,1)S(1)}, u32[]{:S(2)}, u32[]{:S(2)}) collective-permute-start(bf16[8,4608]{1,0:T(8,128)(2,1)S(1)} %join.1.refs_0_), channel_id=1, source_target_pairs={{0,28},{1,29},{2,30},{3,31},{4,24},{5,25},{6,26},{7,27},{8,20},{9,... | collective-permute-start | bytes 221192 | tf_op jit(solution)/shard_map/ppermute | solution.py:292
  13.7 4.0 %collective-permute-start.4 = (bf16[8,4608]{1,0:T(8,128)(2,1)S(1)}, bf16[8,4608]{1,0:T(8,128)(2,1)S(1)}, u32[]{:S(2)}, u32[]{:S(2)}) collective-permute-start(bf16[8,4608]{1,0:T(8,128)(2,1)S(1)} %join.1.refs_0_), channel_id=1, source_target_pairs={{0,20},{1,21},{2,22},{3,23},{4,16},{5,17},{6,18},{7,19},{8,28},{9,... | collective-permute-start | bytes 221192 | tf_op jit(solution)/shard_map/ppermute | solution.py:292
  14.2 4.2 %collective-permute-start.3 = (bf16[8,4608]{1,0:T(8,128)(2,1)S(1)}, bf16[8,4608]{1,0:T(8,128)(2,1)S(1)}, u32[]{:S(2)}, u32[]{:S(2)}) collective-permute-start(bf16[8,4608]{1,0:T(8,128)(2,1)S(1)} %join.1.refs_0_), channel_id=1, source_target_pairs={{0,12},{1,13},{2,14},{3,15},{4,8},{5,9},{6,10},{7,11},{8,4},{9,5},... | collective-permute-start | bytes 221192 | tf_op jit(solution)/shard_map/ppermute | solution.py:292
  18.4 1.6 %collective-permute-start.6 = (bf16[4,8,4608]{2,1,0:T(8,128)(2,1)S(1)}, bf16[4,8,4608]{2,1,0:T(8,128)(2,1)S(1)}, u32[]{:S(2)}, u32[]{:S(2)}) collective-permute-start(bf16[4,8,4608]{2,1,0:T(8,128)(2,1)S(1)} %stack.1.near_ref), channel_id=1, source_target_pairs={{0,4},{1,5},{2,6},{3,7},{4,0},{5,1},{6,2},{7,3},{8,12},{9,13},{10,... | collective-permute-start | bytes 884744 | tf_op jit(solution)/shard_map/ppermute | solution.py:292
  29.0 1.6 %collective-permute-start.7 = (bf16[4,8,4608]{2,1,0:T(8,128)(2,1)S(1)}, bf16[4,8,4608]{2,1,0:T(8,128)(2,1)S(1)}, u32[]{:S(2)}, u32[]{:S(2)}) collective-permute-start(bf16[4,8,4608]{2,1,0:T(8,128)(2,1)S(1)} %get-tuple-element.44), channel_id=1, source_target_pairs={{0,4},{1,5},{2,6},{3,7},{4,0},{5,1},{6,2},{7,3},{8,12},{9,13},{10,... | collective-permute-start | bytes 884744 | tf_op jit(solution)/shard_map/ppermute | solution.py:292
  30.8 8.0 %collective-permute-start.8 = (bf16[8,4608]{1,0:T(8,128)(2,1)S(1)}, bf16[8,4608]{1,0:T(8,128)(2,1)S(1)}, u32[]{:S(2)}, u32[]{:S(2)}) collective-permute-start(bf16[8,4608]{1,0:T(8,128)(2,1)S(1)} %get-tuple-element.49), channel_id=1, source_target_pairs={{0,28},{1,29},{2,30},{3,31},{4,24},{5,25},{6,26},{7,27},{8,20},{9,... | collective-permute-start | bytes 221192 | tf_op jit(solution)/shard_map/ppermute | solution.py:292
  32.3 6.5 %collective-permute-start.9 = (bf16[8,4608]{1,0:T(8,128)(2,1)S(1)}, bf16[8,4608]{1,0:T(8,128)(2,1)S(1)}, u32[]{:S(2)}, u32[]{:S(2)}) collective-permute-start(bf16[8,4608]{1,0:T(8,128)(2,1)S(1)} %get-tuple-element.50), channel_id=1, source_target_pairs={{0,20},{1,21},{2,22},{3,23},{4,16},{5,17},{6,18},{7,19},{8,28},{9,... | collective-permute-start | bytes 221192 | tf_op jit(solution)/shard_map/ppermute | solution.py:292
  33.6 5.2 %collective-permute-start.10 = (bf16[8,4608]{1,0:T(8,128)(2,1)S(1)}, bf16[8,4608]{1,0:T(8,128)(2,1)S(1)}, u32[]{:S(2)}, u32[]{:S(2)}) collective-permute-start(bf16[8,4608]{1,0:T(8,128)(2,1)S(1)} %get-tuple-element.51), channel_id=1, source_target_pairs={{0,12},{1,13},{2,14},{3,15},{4,8},{5,9},{6,10},{7,11},{8,4},{9,5},... | collective-permute-start | bytes 221192 | tf_op jit(solution)/shard_map/ppermute | solution.py:292
  39.0 8.7 %collective-permute-start.11 = (bf16[12,1024]{1,0:T(8,128)(2,1)S(1)}, bf16[12,1024]{1,0:T(8,128)(2,1)S(1)}, u32[]{:S(2)}, u32[]{:S(2)}) collective-permute-start(bf16[12,1024]{1,0:T(8,128)(2,1)S(1)} %get-tuple-element.61), channel_id=1, source_target_pairs={{0,7},{1,6},{2,5},{3,4},{4,3},{5,2},{6,1},{7,0},{8,15},{9,14},{10,... | collective-permute-start | bytes 73736 | tf_op jit(solution)/shard_map/ppermute | solution.py:292
  43.3 4.4 %collective-permute-start.12 = (bf16[12,1024]{1,0:T(8,128)(2,1)S(1)}, bf16[12,1024]{1,0:T(8,128)(2,1)S(1)}, u32[]{:S(2)}, u32[]{:S(2)}) collective-permute-start(bf16[12,1024]{1,0:T(8,128)(2,1)S(1)} %get-tuple-element.62), channel_id=1, source_target_pairs={{0,6},{1,7},{2,4},{3,5},{4,2},{5,3},{6,0},{7,1},{8,14},{9,15},{10,... | collective-permute-start | bytes 73736 | tf_op jit(solution)/shard_map/ppermute | solution.py:292
  43.3 4.4 %collective-permute-start.13 = (bf16[12,1024]{1,0:T(8,128)(2,1)S(1)}, bf16[12,1024]{1,0:T(8,128)(2,1)S(1)}, u32[]{:S(2)}, u32[]{:S(2)}) collective-permute-start(bf16[12,1024]{1,0:T(8,128)(2,1)S(1)} %get-tuple-element.63), channel_id=1, source_target_pairs={{0,5},{1,4},{2,7},{3,6},{4,1},{5,0},{6,3},{7,2},{8,13},{9,12},{10,... | collective-permute-start | bytes 73736 | tf_op jit(solution)/shard_map/ppermute | solution.py:292

commit v5 on v4

--- a/solution.py
+++ b/solution.py
@@ -96,19 +96,13 @@
         out_ref[:, 2 * d :] = tail_ref[...].astype(BF)
 
 
-def stack_kernel(*refs):
-    out_ref = refs[-1]
-    for k, ref in enumerate(refs[:-1]):
-        out_ref[k] = ref[...]
-
-
-def expert_kernel(
-    near_ref, far_ref, wg_ref, wu_ref, wd_ref,
-    keep_ref, send_ref, xs_ref, dys_ref, hidt_ref, gpgt_ref, gput_ref,
+def expert_kernel(*refs, n, tile, cols, slots):
+    nears, fars = refs[:n], refs[n : 2 * n]
+    (
+        wg_ref, wu_ref, wd_ref, keep_ref, send_ref, xs_ref, dys_ref,
+        hidt_ref, gpgt_ref, gput_ref,
     hid_ref, gpg_ref, gpu_ref, tail_ref,
-    *, tile, cols, slots,
-):
-    n = near_ref.shape[0]
+    ) = refs[2 * n :]
     f, d = wg_ref.shape
     width = d // lax.axis_size("expert")
     piece = 2 * d // EIGHT
@@ -120,7 +114,7 @@
             @pl.when(odd(me ^ j) == crossed)
             def _(j=j, crossed=crossed):
                 for b in range(n):
-                    near, far = near_ref.at[b], far_ref.at[b]
+                    near, far = nears[b], fars[b]
                     if crossed ^ (b > 0):
                         near, far = far, near
                     for at, ref in ((b * ROWS, near), ((n + b) * ROWS, far)):
@@ -182,18 +176,14 @@
 def grads_kernel(jobs, n, n_old, *refs):
     lefts, rights = refs[:n], refs[n : 2 * n]
     outs, (buf, sems) = refs[2 * n + n_old : 3 * n + n_old], refs[3 * n + n_old :]
-    slots = buf.shape[0]
     copies = []
     for i, (a, start, size) in enumerate(jobs):
-        slot = i % slots
-        if i >= slots:
-            copies[i - slots].wait()
         rows = pl.ds(start, size)
-        buf[slot, :size] = dot_nn(lefts[a][rows, :], rights[a][...]).astype(BF)
-        copy = pltpu.make_async_copy(buf.at[slot, pl.ds(0, size)], outs[a].at[rows, :], sems.at[slot])
+        buf[i, :size] = dot_nn(lefts[a][rows, :], rights[a][...]).astype(BF)
+        copy = pltpu.make_async_copy(buf.at[i, pl.ds(0, size)], outs[a].at[rows, :], sems.at[i])
         copy.start()
         copies.append(copy)
-    for copy in copies[-slots:]:
+    for copy in copies:
         copy.wait()
 
 
@@ -242,21 +232,27 @@
     grad_ref[...] = total[:, width:].astype(BF)
 
 
-def grads(jobs, lefts, rights, old):
+def grads(spans, lefts, rights, old):
     n = len(lefts)
     f, rows = lefts[0].shape
     d = rights[0].shape[1]
     kept = [a for a in range(n) if old[a] is not None]
-    size = max(job[2] for job in jobs)
+    size = f // 12
+    jobs = [
+        (a, at, min(size, stop - at)) for a, start, stop in spans for at in range(start, stop, size)
+    ]
     done = sum(job[2] for job in jobs)
     return pl.pallas_call(
         functools.partial(grads_kernel, jobs, n, len(kept)),
         in_specs=[VM] * (2 * n) + [HBM] * len(kept),
         out_specs=[HBM] * n,
         out_shape=[jax.ShapeDtypeStruct((f, d), BF)] * n,
-        scratch_shapes=[pltpu.VMEM((3, size, d), BF), pltpu.SemaphoreType.DMA((3,))],
+        scratch_shapes=[
+            pltpu.VMEM((len(jobs), size, d), BF),
+            pltpu.SemaphoreType.DMA((len(jobs),)),
+        ],
         input_output_aliases={2 * n + i: a for i, a in enumerate(kept)},
-        compiler_params=params(((6 * size * d + n * 2 * rows * (f + d)) >> 20) + 4),
+        compiler_params=params(((2 * len(jobs) * size * d + n * 2 * rows * (f + d)) >> 20) + 4),
         cost_estimate=pl.CostEstimate(
             flops=2 * rows * done * d, bytes_accessed=3 * done * d, transcendentals=0
         ),
@@ -283,7 +279,7 @@
     tok, width = tokens.shape
     d = width * n_e
     f = w_gate.shape[1]
-    tile = 256 if f % 256 == 0 else f
+    tile = 384 if f % 384 == 0 else f
     rows = n_dp * ROWS
     n_chip = n_dp // 2
     sds = jax.ShapeDtypeStruct
@@ -337,13 +333,12 @@
             mine = stack(pair_kernel, [mine, got], (len(patterns), tok, 2 * width), "pair")
         hop //= 2
     blocks = [block] + [swap(block, k, 0, 1) for k in range(1, n_chip)]
-    near = stack(stack_kernel, blocks, (n_chip,) + block_shape, "stack")
-    far = swap(near, 0, 0, 1)
+    blocks = blocks + [swap(b, 0, 0, 1) for b in blocks]
 
     held = 2 * f * d + rows * (16 * d + 12 * f)
     keep, send, xs, dys, hidden, gpg, gpu = pl.pallas_call(
-        functools.partial(expert_kernel, tile=tile, cols=256, slots=slots),
-        in_specs=[VM] * 5,
+        functools.partial(expert_kernel, n=n_chip, tile=tile, cols=256, slots=slots),
+        in_specs=[VM] * (2 * n_chip + 3),
         out_specs=[VM] * 7,
         out_shape=[sds((n_chip,) + block_shape, BF)] * 2
         + [sds((rows, d), BF)] * 2
@@ -355,12 +350,11 @@
             flops=12 * rows * f * d, bytes_accessed=6 * f * d, transcendentals=rows * f
         ),
         name="expert",
-    )(near, far, w_gate[0], w_up[0], w_down[0])
+    )(*blocks, w_gate[0], w_up[0], w_down[0])
 
     received = swap(send, 0, 0, 1)
-    third, part = f // 3, f // 12
-    whole = [(1, i * third, third) for i in range(3)]
-    (down,) = grads([(0, 0, 2 * part)], [hidden], [dys], [None])
+    part = f // 24
+    (down,) = grads([(0, 0, 6 * part)], [hidden], [dys], [None])
     received, down = lax.optimization_barrier((received, down))
     parts = pl.pallas_call(
         cores_kernel,
@@ -371,7 +365,7 @@
         name="cores",
     )(keep, received)
     arrived = [swap(parts[k], k, 0, 1) for k in range(n_chip - 1, 0, -1)]
-    down, grad_gate = grads([(0, 2 * part, 4 * part), (0, 6 * part, 3 * part)] + whole, [hidden, gpg], [dys, xs], [down, None])
+    down, grad_gate = grads([(0, 6 * part, 18 * part), (1, 0, f)], [hidden, gpg], [dys, xs], [down, None])
     arrived, down, grad_gate = lax.optimization_barrier((arrived, down, grad_gate))
     summed = pl.pallas_call(
         functools.partial(chips_kernel, n_chip, slots),
@@ -384,7 +378,7 @@
     )(info, other, parts[0], *arrived)
     home = [summed[0]] + [swap(summed[k], 0, k, 1) for k in range(n_e - 1, 0, -1)]
     grad_down, grad_up = grads(
-        [(0, 9 * part, 3 * part)] + whole, [hidden, gpu], [dys, xs], [down, None]
+        [(0, 18 * part, f), (1, 0, f)], [hidden, gpu], [dys, xs], [down, None]
     )
     home, grad_down, grad_up = lax.optimization_barrier((home, grad_down, grad_up))
     mixed, grad_tokens = pl.pallas_call(

time: 48.8 us -> 47.1 us (0.965)
  Pallas kernels: 20.2 us -> 18.7 us
  waiting for transfers between devices: 7.56 us -> 6.74 us
  starting transfers between devices: 17.8 us -> 18.5 us
    pallas_call x3, Pallas kernels: 9.99 us -> 9.02 us  [grads(): pl.pallas_call(functools.partial(grads_kernel, jobs, n, len(kept)), in_sp...]
    ppermute x14 -> x17, waiting for transfers between devices: 7.56 us -> 6.74 us  [swap(): lax.ppermute(x, ('dp', 'expert'), [(i * n_e + j, (i ^ 2 * chips + core) *...]
    ppermute x14 -> x17, starting transfers between devices: 17.8 us -> 18.5 us  [swap(): lax.ppermute(x, ('dp', 'expert'), [(i * n_e + j, (i ^ 2 * chips + core) *...]
    pallas_call x1, Pallas kernels: 8.93 us -> 8.4 us  [per_device(): pl.pallas_call(functools.partial(expert_kernel, n=n_chip, tile=tile, cols...]
  transfers between devices with their start and end apart: 14 -> 17, of which waited for: 7 -> 10; matrix products, arithmetic and copies ran while one was open for 0% -> 0% of each run, Pallas kernels for 21% -> 20%
where the time goes in v5:
time: 47.1 us; the launch traced here: 46.8 us
  Pallas kernels  18.7 us (40%)
  starting transfers between devices  18.5 us (39%)
  waiting for transfers between devices  6.74 us (14%)
  local copies, waits for them, and re-layouts  1.37 us (3%)
  other arithmetic  0.74 us (2%)
  between operations  0.73 us (2%)
    ppermute x17, starting transfers between devices, swap(): lax.ppermute(x, ('dp', 'expert'), [(i * n_e + j, (i ^ 2 * chips + core) *...  18.5 us
    pallas_call x3, Pallas kernels, grads(): pl.pallas_call(functools.partial(grads_kernel, jobs, n, len(kept)), in_sp...  9.02 us
    pallas_call x1, Pallas kernels, per_device(): pl.pallas_call(functools.partial(expert_kernel, n=n_chip, tile=tile, cols...  8.4 us
    ppermute x17, waiting for transfers between devices, swap(): lax.ppermute(x, ('dp', 'expert'), [(i * n_e + j, (i ^ 2 * chips + core) *...  6.74 us
    unnamed x10, local copies, waits for them, and re-layouts  1.37 us
  transfers between devices with their start and end apart: 17, of which 10 were waited for; matrix products, arithmetic and copies ran while one was open for 0% of the time, Pallas kernels for 20%

profile of v5, /device:TPU:0, one launch (start us, length us, event | category | flops | bytes accessed | tf_op | source)
XLA Modules:
  0.0 46.8 jit_solution(6124236433606280061)
XLA Ops:
  0.6 0.7 %maximum_bitcast_fusion.a_ref = bf16[1,12,1024]{2,1,0:T(8,128)(2,1)S(1)} fusion(bf16[12,512]{1,0:T(8,128)(2,1)} %param.8, bf16[12,512]{1,0:T(8,128)(2,1)} %param.7), kind=kLoop, calls=%fused_computation | loop fusion | flops 49152 | bytes 49152 | tf_op jit(solution)/shard_map/broadcast_in_dim | solution.py:304
  1.4 3.5 %collective-permute-start = (bf16[1,12,1024]{2,1,0:T(8,128)(2,1)S(1)}, bf16[1,12,1024]{2,1,0:T(8,128)(2,1)S(1)}, u32[]{:S(2)}, u32[]{:S(2)}) collective-permute-start(bf16[1,12,1024]{2,1,0:T(8,128)(2,1)S(1)} %maximum_bitcast_fusion.a_ref), channel_id=1, source_target_pairs={{0,6},{1,7},{2,4},{3,5},{4,2},{5,3},{6,0},{7,1},{8,14},{9,15},{10,... | collective-permute-start | bytes 73736 | tf_op jit(solution)/shard_map/ppermute | solution.py:288
  4.9 0.0 copy-start.3
  4.9 0.7 %copy-done.3 = s32[12,2]{0,1:T(2,128)S(1)} copy-done((s32[12,2]{0,1:T(2,128)S(1)}, s32[12,2]{0,1:T(2,128)}, u32[]{:S(2)}) %copy-start.3) | copy-done | bytes 120
  5.5 0.0 copy-start.4
  5.5 0.7 %copy-done.4 = f32[12,2]{0,1:T(2,128)S(1)} copy-done((f32[12,2]{0,1:T(2,128)S(1)}, f32[12,2]{0,1:T(2,128)}, u32[]{:S(2)}) %copy-start.4) | copy-done | bytes 120
  6.2 0.0 copy-start
  6.2 0.0 copy-start.1
  6.2 0.0 copy-start.2
  6.2 0.2 share.1.mine_ref
  6.4 0.2 collective-permute-done.b_ref
  6.6 1.8 %collective-permute-start.2 = (bf16[2,12,1024]{2,1,0:T(8,128)(2,1)S(1)}, bf16[2,12,1024]{2,1,0:T(8,128)(2,1)S(1)}, u32[]{:S(2)}, u32[]{:S(2)}) collective-permute-start(bf16[2,12,1024]{2,1,0:T(8,128)(2,1)S(1)} %pair.1.a_ref), channel_id=1, source_target_pairs={{0,5},{1,4},{2,7},{3,6},{4,1},{5,0},{6,3},{7,2},{8,13},{9,12},{10,... | collective-permute-start | bytes 147464 | tf_op jit(solution)/shard_map/ppermute | solution.py:288
  8.5 0.4 collective-permute-start.1
  8.9 0.8 %collective-permute-done.1.other_ref = f32[48,128]{1,0:T(8,128)S(1)} collective-permute-done((f32[48,128]{1,0:T(8,128)S(1)}, f32[48,128]{1,0:T(8,128)S(1)}, u32[]{:S(2)}, u32[]{:S(2)}) %collective-permute-start.1) | collective-permute-done | bytes 24608 | tf_op jit(solution)/shard_map/ppermute | solution.py:288
  9.7 0.9 %collective-permute-done.2.b_ref = bf16[2,12,1024]{2,1,0:T(8,128)(2,1)S(1)} collective-permute-done((bf16[2,12,1024]{2,1,0:T(8,128)(2,1)S(1)}, bf16[2,12,1024]{2,1,0:T(8,128)(2,1)S(1)}, u32[]{:S(2)}, u32[]{:S(2)}) %collective-permute-start.2) | collective-permute-done | bytes 49184 | tf_op jit(solution)/shard_map/ppermute | solution.py:288
  10.7 0.2 join.1.refs_0_
  10.8 2.8 %collective-permute-start.5 = (bf16[8,4608]{1,0:T(8,128)(2,1)S(1)}, bf16[8,4608]{1,0:T(8,128)(2,1)S(1)}, u32[]{:S(2)}, u32[]{:S(2)}) collective-permute-start(bf16[8,4608]{1,0:T(8,128)(2,1)S(1)} %join.1.refs_0_), channel_id=1, source_target_pairs={{0,28},{1,29},{2,30},{3,31},{4,24},{5,25},{6,26},{7,27},{8,20},{9,... | collective-permute-start | bytes 221192 | tf_op jit(solution)/shard_map/ppermute | solution.py:288
  13.7 0.5 %collective-permute-start.4 = (bf16[8,4608]{1,0:T(8,128)(2,1)S(1)}, bf16[8,4608]{1,0:T(8,128)(2,1)S(1)}, u32[]{:S(2)}, u32[]{:S(2)}) collective-permute-start(bf16[8,4608]{1,0:T(8,128)(2,1)S(1)} %join.1.refs_0_), channel_id=1, source_target_pairs={{0,20},{1,21},{2,22},{3,23},{4,16},{5,17},{6,18},{7,19},{8,28},{9,... | collective-permute-start | bytes 221192 | tf_op jit(solution)/shard_map/ppermute | solution.py:288
  14.2 0.2 collective-permute-start.3
  14.4 0.1 collective-permute-start.6
  14.4 1.9 %collective-permute-done.5.refs_3_ = bf16[8,4608]{1,0:T(8,128)(2,1)S(1)} collective-permute-done((bf16[8,4608]{1,0:T(8,128)(2,1)S(1)}, bf16[8,4608]{1,0:T(8,128)(2,1)S(1)}, u32[]{:S(2)}, u32[]{:S(2)}) %collective-permute-start.5) | collective-permute-done | bytes 73760 | tf_op jit(solution)/shard_map/ppermute | solution.py:288
  16.4 0.0 collective-permute-start.9
  16.4 1.3 %collective-permute-done.4.refs_2_ = bf16[8,4608]{1,0:T(8,128)(2,1)S(1)} collective-permute-done((bf16[8,4608]{1,0:T(8,128)(2,1)S(1)}, bf16[8,4608]{1,0:T(8,128)(2,1)S(1)}, u32[]{:S(2)}, u32[]{:S(2)}) %collective-permute-start.4) | collective-permute-done | bytes 73760 | tf_op jit(solution)/shard_map/ppermute | solution.py:288
  17.7 0.7 %collective-permute-start.8 = (bf16[8,4608]{1,0:T(8,128)(2,1)S(1)}, bf16[8,4608]{1,0:T(8,128)(2,1)S(1)}, u32[]{:S(2)}, u32[]{:S(2)}) collective-permute-start(bf16[8,4608]{1,0:T(8,128)(2,1)S(1)} %collective-permute-done.4.refs_2_), channel_id=1, source_target_pairs={{0,4},{1,5},{2,6},{3,7},{4,0},{5,1},{6,2},{7,3},{8,12},{9,13},{10,... | collective-permute-start | bytes 221192 | tf_op jit(solution)/shard_map/ppermute | solution.py:288
  18.4 0.1 collective-permute-done.3.refs_1_
  18.4 0.1 collective-permute-start.7
  18.6 0.0 collective-permute-done.6.refs_4_
  18.6 0.0 collective-permute-done.9.refs_7_
  18.6 0.7 %collective-permute-done.8.refs_6_ = bf16[8,4608]{1,0:T(8,128)(2,1)S(1)} collective-permute-done((bf16[8,4608]{1,0:T(8,128)(2,1)S(1)}, bf16[8,4608]{1,0:T(8,128)(2,1)S(1)}, u32[]{:S(2)}, u32[]{:S(2)}) %collective-permute-start.8) | collective-permute-done | bytes 73760 | tf_op jit(solution)/shard_map/ppermute | solution.py:288
  19.3 0.4 collective-permute-done.7.refs_5_
  19.7 0.0 copy-done
  19.7 0.0 copy-done.1
  19.7 0.0 copy-done.2
  19.7 8.4 %expert.1 = (bf16[4,8,4608]{2,1,0:T(8,128)(2,1)S(1)}, bf16[4,8,4608]{2,1,0:T(8,128)(2,1)S(1)}, bf16[128,2048]{1,0:T(8,128)(2,1)S(1)}, bf16[128,2048]{1,0:T(8,128...) custom-call(bf16[8,4608]{1,0:T(8,128)(2,1)S(1)} %join.1.refs_0_, ...), custom_call_target="tpu_custom_call" | custom-call | flops 4831838208 | bytes 18874368 | tf_op jit(solution)/shard_map/expert/pallas_call | solution.py:339
  28.1 0.2 collective-permute-start.10
  28.3 1.4 %grads.3.refs_4_ = bf16[1536,2048]{1,0:T(8,128)(2,1)} custom-call(bf16[1536,128]{1,0:T(8,128)(2,1)S(1)} %get-tuple-element.45.refs_0_, bf16[128,2048]{1,0:T(8,128)(2,1)S(1)} %get-tuple-element.46.refs_1_.refs_2_), custom_call_target="tpu_custom_call" | custom-call | flops 201326592 | bytes 2359296 | tf_op jit(solution)/shard_map/grads/pallas_call | solution.py:245
  29.8 0.0 collective-permute-done.10.got_ref
  29.8 0.1 cores.1
  29.9 1.6 %collective-permute-start.11 = (bf16[8,4608]{1,0:T(8,128)(2,1)S(1)}, bf16[8,4608]{1,0:T(8,128)(2,1)S(1)}, u32[]{:S(2)}, u32[]{:S(2)}) collective-permute-start(bf16[8,4608]{1,0:T(8,128)(2,1)S(1)} %get-tuple-element.49), channel_id=1, source_target_pairs={{0,28},{1,29},{2,30},{3,31},{4,24},{5,25},{6,26},{7,27},{8,20},{9,... | collective-permute-start | bytes 221192 | tf_op jit(solution)/shard_map/ppermute | solution.py:288
  31.5 1.5 %collective-permute-start.12 = (bf16[8,4608]{1,0:T(8,128)(2,1)S(1)}, bf16[8,4608]{1,0:T(8,128)(2,1)S(1)}, u32[]{:S(2)}, u32[]{:S(2)}) collective-permute-start(bf16[8,4608]{1,0:T(8,128)(2,1)S(1)} %get-tuple-element.50), channel_id=1, source_target_pairs={{0,20},{1,21},{2,22},{3,23},{4,16},{5,17},{6,18},{7,19},{8,28},{9,... | collective-permute-start | bytes 221192 | tf_op jit(solution)/shard_map/ppermute | solution.py:288
  33.0 0.1 collective-permute-start.13
  33.1 4.0 %grads.4 = (bf16[1536,2048]{1,0:T(8,128)(2,1)}, bf16[1536,2048]{1,0:T(8,128)(2,1)}) custom-call(bf16[1536,128]{1,0:T(8,128)(2,1)S(1)} %get-tuple-element.45.refs_0_, bf16[1536,128]{1,0:T(8,128)(2,1)S(1)} %get-tuple-element.52.refs_1_, bf16[128,2048]{1,0:T(8,128)(2,1)S(1)} %get-tuple-element.46.refs_1_.refs_2_, ...), custom_call_target="tpu_custom_call", output_to_operand_aliasing={{0}: (4, {})} | custom-call | flops 1207959552 | bytes 14155776 | tf_op jit(solution)/shard_map/grads/pallas_call | solution.py:245
  37.1 0.0 collective-permute-done.11.refs_1_
  37.2 0.0 collective-permute-done.12.refs_2_
  37.2 0.1 collective-permute-done.13.refs_3_
  37.3 0.2 chips.1
  37.5 4.4 %collective-permute-start.14 = (bf16[12,1024]{1,0:T(8,128)(2,1)S(1)}, bf16[12,1024]{1,0:T(8,128)(2,1)S(1)}, u32[]{:S(2)}, u32[]{:S(2)}) collective-permute-start(bf16[12,1024]{1,0:T(8,128)(2,1)S(1)} %get-tuple-element.61), channel_id=1, source_target_pairs={{0,7},{1,6},{2,5},{3,4},{4,3},{5,2},{6,1},{7,0},{8,15},{9,14},{10,... | collective-permute-start | bytes 73736 | tf_op jit(solution)/shard_map/ppermute | solution.py:288
  41.9 0.0 collective-permute-start.15
  41.9 0.5 %collective-permute-start.16 = (bf16[12,1024]{1,0:T(8,128)(2,1)S(1)}, bf16[12,1024]{1,0:T(8,128)(2,1)S(1)}, u32[]{:S(2)}, u32[]{:S(2)}) collective-permute-start(bf16[12,1024]{1,0:T(8,128)(2,1)S(1)} %get-tuple-element.63), channel_id=1, source_target_pairs={{0,5},{1,4},{2,7},{3,6},{4,1},{5,0},{6,3},{7,2},{8,13},{9,12},{10,... | collective-permute-start | bytes 73736 | tf_op jit(solution)/shard_map/ppermute | solution.py:288
  42.4 3.5 %grads.5 = (bf16[1536,2048]{1,0:T(8,128)(2,1)}, bf16[1536,2048]{1,0:T(8,128)(2,1)}) custom-call(bf16[1536,128]{1,0:T(8,128)(2,1)S(1)} %get-tuple-element.45.refs_0_, bf16[1536,128]{1,0:T(8,128)(2,1)S(1)} %get-tuple-element.64.refs_1_, bf16[128,2048]{1,0:T(8,128)(2,1)S(1)} %get-tuple-element.46.refs_1_.refs_2_, ...), custom_call_target="tpu_custom_call", output_to_operand_aliasing={{0}: (4, {})} | custom-call | flops 1006632960 | bytes 11796480 | tf_op jit(solution)/shard_map/grads/pallas_call | solution.py:245
  45.9 0.0 collective-permute-done.14.refs_1_
  46.0 0.2 collective-permute-done.15.refs_2_
  46.1 0.0 collective-permute-done.16.refs_3_
  46.1 0.6 %home.1 = (bf16[12,512]{1,0:T(8,128)(2,1)}, bf16[12,512]{1,0:T(8,128)(2,1)}) custom-call(bf16[12,1024]{1,0:T(8,128)(2,1)S(1)} %get-tuple-element.68.refs_0_, bf16[12,1024]{1,0:T(8,128)(2,1)S(1)} %collective-permute-done.14.refs_1_, bf16[12,1024]{1,0:T(8,128)(2,1)S(1)} %collective-permute-done.15.refs_2_, bf16[12,1024]{1,0:T(8,128)(2,1)S(1)} %collective-permute-done.16.refs_3_), custom_call_target="tpu_custom_call" | custom-call | tf_op jit(solution)/shard_map/home/pallas_call | solution.py:384
  (1 shorter events, 0.0 us)
Async XLA Ops:
  1.4 5.3 %collective-permute-start = (bf16[1,12,1024]{2,1,0:T(8,128)(2,1)S(1)}, bf16[1,12,1024]{2,1,0:T(8,128)(2,1)S(1)}, u32[]{:S(2)}, u32[]{:S(2)}) collective-permute-start(bf16[1,12,1024]{2,1,0:T(8,128)(2,1)S(1)} %maximum_bitcast_fusion.a_ref), channel_id=1, source_target_pairs={{0,6},{1,7},{2,4},{3,5},{4,2},{5,3},{6,0},{7,1},{8,14},{9,15},{10,... | collective-permute-start | bytes 73736 | tf_op jit(solution)/shard_map/ppermute | solution.py:288
  4.9 0.7 %copy-start.3 = (s32[12,2]{0,1:T(2,128)S(1)}, s32[12,2]{0,1:T(2,128)}, u32[]{:S(2)}) copy-start(s32[12,2]{0,1:T(2,128)} %param.9) | copy-start | bytes 292
  5.5 0.7 %copy-start.4 = (f32[12,2]{0,1:T(2,128)S(1)}, f32[12,2]{0,1:T(2,128)}, u32[]{:S(2)}) copy-start(f32[12,2]{0,1:T(2,128)} %param.10) | copy-start | bytes 292
  6.2 13.5 %copy-start = (bf16[1,1536,2048]{2,1,0:T(8,128)(2,1)S(1)}, bf16[1,1536,2048]{2,1,0:T(8,128)(2,1)}, u32[]{:S(2)}) copy-start(bf16[1,1536,2048]{2,1,0:T(8,128)(2,1)} %param.11) | copy-start | bytes 18874372
  6.2 13.5 %copy-start.1 = (bf16[1,1536,2048]{2,1,0:T(8,128)(2,1)S(1)}, bf16[1,1536,2048]{2,1,0:T(8,128)(2,1)}, u32[]{:S(2)}) copy-start(bf16[1,1536,2048]{2,1,0:T(8,128)(2,1)} %param.12) | copy-start | bytes 18874372
  6.2 13.5 %copy-start.2 = (bf16[1,1536,2048]{2,1,0:T(8,128)(2,1)S(1)}, bf16[1,1536,2048]{2,1,0:T(8,128)(2,1)}, u32[]{:S(2)}) copy-start(bf16[1,1536,2048]{2,1,0:T(8,128)(2,1)} %param.13) | copy-start | bytes 18874372
  6.6 4.0 %collective-permute-start.2 = (bf16[2,12,1024]{2,1,0:T(8,128)(2,1)S(1)}, bf16[2,12,1024]{2,1,0:T(8,128)(2,1)S(1)}, u32[]{:S(2)}, u32[]{:S(2)}) collective-permute-start(bf16[2,12,1024]{2,1,0:T(8,128)(2,1)S(1)} %pair.1.a_ref), channel_id=1, source_target_pairs={{0,5},{1,4},{2,7},{3,6},{4,1},{5,0},{6,3},{7,2},{8,13},{9,12},{10,... | collective-permute-start | bytes 147464 | tf_op jit(solution)/shard_map/ppermute | solution.py:288
  8.5 1.2 %collective-permute-start.1 = (f32[48,128]{1,0:T(8,128)S(1)}, f32[48,128]{1,0:T(8,128)S(1)}, u32[]{:S(2)}, u32[]{:S(2)}) collective-permute-start(f32[48,128]{1,0:T(8,128)S(1)} %share.1.mine_ref), channel_id=1, source_target_pairs={{0,4},{1,5},{2,6},{3,7},{4,0},{5,1},{6,2},{7,3},{8,12},{9,13},{10,... | collective-permute-start | bytes 73736 | tf_op jit(solution)/shard_map/ppermute | solution.py:288
  10.8 5.5 %collective-permute-start.5 = (bf16[8,4608]{1,0:T(8,128)(2,1)S(1)}, bf16[8,4608]{1,0:T(8,128)(2,1)S(1)}, u32[]{:S(2)}, u32[]{:S(2)}) collective-permute-start(bf16[8,4608]{1,0:T(8,128)(2,1)S(1)} %join.1.refs_0_), channel_id=1, source_target_pairs={{0,28},{1,29},{2,30},{3,31},{4,24},{5,25},{6,26},{7,27},{8,20},{9,... | collective-permute-start | bytes 221192 | tf_op jit(solution)/shard_map/ppermute | solution.py:288
  13.7 4.0 %collective-permute-start.4 = (bf16[8,4608]{1,0:T(8,128)(2,1)S(1)}, bf16[8,4608]{1,0:T(8,128)(2,1)S(1)}, u32[]{:S(2)}, u32[]{:S(2)}) collective-permute-start(bf16[8,4608]{1,0:T(8,128)(2,1)S(1)} %join.1.refs_0_), channel_id=1, source_target_pairs={{0,20},{1,21},{2,22},{3,23},{4,16},{5,17},{6,18},{7,19},{8,28},{9,... | collective-permute-start | bytes 221192 | tf_op jit(solution)/shard_map/ppermute | solution.py:288
  14.2 4.2 %collective-permute-start.3 = (bf16[8,4608]{1,0:T(8,128)(2,1)S(1)}, bf16[8,4608]{1,0:T(8,128)(2,1)S(1)}, u32[]{:S(2)}, u32[]{:S(2)}) collective-permute-start(bf16[8,4608]{1,0:T(8,128)(2,1)S(1)} %join.1.refs_0_), channel_id=1, source_target_pairs={{0,12},{1,13},{2,14},{3,15},{4,8},{5,9},{6,10},{7,11},{8,4},{9,5},... | collective-permute-start | bytes 221192 | tf_op jit(solution)/shard_map/ppermute | solution.py:288
  14.4 4.2 %collective-permute-start.6 = (bf16[8,4608]{1,0:T(8,128)(2,1)S(1)}, bf16[8,4608]{1,0:T(8,128)(2,1)S(1)}, u32[]{:S(2)}, u32[]{:S(2)}) collective-permute-start(bf16[8,4608]{1,0:T(8,128)(2,1)S(1)} %join.1.refs_0_), channel_id=1, source_target_pairs={{0,4},{1,5},{2,6},{3,7},{4,0},{5,1},{6,2},{7,3},{8,12},{9,13},{10,... | collective-permute-start | bytes 221192 | tf_op jit(solution)/shard_map/ppermute | solution.py:288
  16.4 2.2 %collective-permute-start.9 = (bf16[8,4608]{1,0:T(8,128)(2,1)S(1)}, bf16[8,4608]{1,0:T(8,128)(2,1)S(1)}, u32[]{:S(2)}, u32[]{:S(2)}) collective-permute-start(bf16[8,4608]{1,0:T(8,128)(2,1)S(1)} %collective-permute-done.5.refs_3_), channel_id=1, source_target_pairs={{0,4},{1,5},{2,6},{3,7},{4,0},{5,1},{6,2},{7,3},{8,12},{9,13},{10,... | collective-permute-start | bytes 221192 | tf_op jit(solution)/shard_map/ppermute | solution.py:288
  17.7 1.6 %collective-permute-start.8 = (bf16[8,4608]{1,0:T(8,128)(2,1)S(1)}, bf16[8,4608]{1,0:T(8,128)(2,1)S(1)}, u32[]{:S(2)}, u32[]{:S(2)}) collective-permute-start(bf16[8,4608]{1,0:T(8,128)(2,1)S(1)} %collective-permute-done.4.refs_2_), channel_id=1, source_target_pairs={{0,4},{1,5},{2,6},{3,7},{4,0},{5,1},{6,2},{7,3},{8,12},{9,13},{10,... | collective-permute-start | bytes 221192 | tf_op jit(solution)/shard_map/ppermute | solution.py:288
  18.4 1.3 %collective-permute-start.7 = (bf16[8,4608]{1,0:T(8,128)(2,1)S(1)}, bf16[8,4608]{1,0:T(8,128)(2,1)S(1)}, u32[]{:S(2)}, u32[]{:S(2)}) collective-permute-start(bf16[8,4608]{1,0:T(8,128)(2,1)S(1)} %collective-permute-done.3.refs_1_), channel_id=1, source_target_pairs={{0,4},{1,5},{2,6},{3,7},{4,0},{5,1},{6,2},{7,3},{8,12},{9,13},{10,... | collective-permute-start | bytes 221192 | tf_op jit(solution)/shard_map/ppermute | solution.py:288
  28.1 1.7 %collective-permute-start.10 = (bf16[4,8,4608]{2,1,0:T(8,128)(2,1)S(1)}, bf16[4,8,4608]{2,1,0:T(8,128)(2,1)S(1)}, u32[]{:S(2)}, u32[]{:S(2)}) collective-permute-start(bf16[4,8,4608]{2,1,0:T(8,128)(2,1)S(1)} %get-tuple-element.44), channel_id=1, source_target_pairs={{0,4},{1,5},{2,6},{3,7},{4,0},{5,1},{6,2},{7,3},{8,12},{9,13},{10,... | collective-permute-start | bytes 884744 | tf_op jit(solution)/shard_map/ppermute | solution.py:288
  29.9 7.3 %collective-permute-start.11 = (bf16[8,4608]{1,0:T(8,128)(2,1)S(1)}, bf16[8,4608]{1,0:T(8,128)(2,1)S(1)}, u32[]{:S(2)}, u32[]{:S(2)}) collective-permute-start(bf16[8,4608]{1,0:T(8,128)(2,1)S(1)} %get-tuple-element.49), channel_id=1, source_target_pairs={{0,28},{1,29},{2,30},{3,31},{4,24},{5,25},{6,26},{7,27},{8,20},{9,... | collective-permute-start | bytes 221192 | tf_op jit(solution)/shard_map/ppermute | solution.py:288
  31.5 5.7 %collective-permute-start.12 = (bf16[8,4608]{1,0:T(8,128)(2,1)S(1)}, bf16[8,4608]{1,0:T(8,128)(2,1)S(1)}, u32[]{:S(2)}, u32[]{:S(2)}) collective-permute-start(bf16[8,4608]{1,0:T(8,128)(2,1)S(1)} %get-tuple-element.50), channel_id=1, source_target_pairs={{0,20},{1,21},{2,22},{3,23},{4,16},{5,17},{6,18},{7,19},{8,28},{9,... | collective-permute-start | bytes 221192 | tf_op jit(solution)/shard_map/ppermute | solution.py:288
  33.0 4.2 %collective-permute-start.13 = (bf16[8,4608]{1,0:T(8,128)(2,1)S(1)}, bf16[8,4608]{1,0:T(8,128)(2,1)S(1)}, u32[]{:S(2)}, u32[]{:S(2)}) collective-permute-start(bf16[8,4608]{1,0:T(8,128)(2,1)S(1)} %get-tuple-element.51), channel_id=1, source_target_pairs={{0,12},{1,13},{2,14},{3,15},{4,8},{5,9},{6,10},{7,11},{8,4},{9,5},... | collective-permute-start | bytes 221192 | tf_op jit(solution)/shard_map/ppermute | solution.py:288
  37.5 8.4 %collective-permute-start.14 = (bf16[12,1024]{1,0:T(8,128)(2,1)S(1)}, bf16[12,1024]{1,0:T(8,128)(2,1)S(1)}, u32[]{:S(2)}, u32[]{:S(2)}) collective-permute-start(bf16[12,1024]{1,0:T(8,128)(2,1)S(1)} %get-tuple-element.61), channel_id=1, source_target_pairs={{0,7},{1,6},{2,5},{3,4},{4,3},{5,2},{6,1},{7,0},{8,15},{9,14},{10,... | collective-permute-start | bytes 73736 | tf_op jit(solution)/shard_map/ppermute | solution.py:288
  41.9 4.2 %collective-permute-start.15 = (bf16[12,1024]{1,0:T(8,128)(2,1)S(1)}, bf16[12,1024]{1,0:T(8,128)(2,1)S(1)}, u32[]{:S(2)}, u32[]{:S(2)}) collective-permute-start(bf16[12,1024]{1,0:T(8,128)(2,1)S(1)} %get-tuple-element.62), channel_id=1, source_target_pairs={{0,6},{1,7},{2,4},{3,5},{4,2},{5,3},{6,0},{7,1},{8,14},{9,15},{10,... | collective-permute-start | bytes 73736 | tf_op jit(solution)/shard_map/ppermute | solution.py:288
  41.9 4.2 %collective-permute-start.16 = (bf16[12,1024]{1,0:T(8,128)(2,1)S(1)}, bf16[12,1024]{1,0:T(8,128)(2,1)S(1)}, u32[]{:S(2)}, u32[]{:S(2)}) collective-permute-start(bf16[12,1024]{1,0:T(8,128)(2,1)S(1)} %get-tuple-element.63), channel_id=1, source_target_pairs={{0,5},{1,4},{2,7},{3,6},{4,1},{5,0},{6,3},{7,2},{8,13},{9,12},{10,... | collective-permute-start | bytes 73736 | tf_op jit(solution)/shard_map/ppermute | solution.py:288

commit v6 on v5

--- a/solution.py
+++ b/solution.py
@@ -46,11 +46,21 @@
     at = lax.broadcasted_iota(jnp.int32, (ROWS, tok), 0).astype(F32)
     pick = jnp.where(at == slot, routed, 0.0)
     weight = jnp.sum(pick * gate, axis=1, keepdims=True)
-    out_ref[...] = jnp.zeros_like(out_ref)
+    at = lax.broadcasted_iota(jnp.int32, (tok, ROWS), 1).astype(F32)
+    back = jnp.where(at == slot_col, routed_col, 0.0)
     out_ref[:ROWS] = jnp.broadcast_to(weight, (ROWS, lanes))
-    out_ref[ROWS : 2 * ROWS, :tok] = pick
-    at = lax.broadcasted_iota(jnp.int32, (tok, lanes), 1).astype(F32)
-    out_ref[2 * ROWS : 2 * ROWS + tok] = jnp.where(at == slot_col, routed_col, 0.0)
+    for i in range(2):
+        out_ref[ROWS * (1 + i) : ROWS * (2 + i)] = dot_nn(pick, shifted((tok, lanes), tok * i))
+    total = jnp.zeros((2 * tok, lanes), F32)
+    for i in range(2):
+        wide = dot_nn(back, shifted((ROWS, lanes), ROWS * i))
+        total = total + dot_nn(shifted((2 * tok, tok), -tok * i), wide)
+    out_ref[3 * ROWS :] = total
+
+
+def shifted(shape, by):
+    row = lax.broadcasted_iota(jnp.int32, shape, 0)
+    return jnp.where(row + by == lax.broadcasted_iota(jnp.int32, shape, 1), 1.0, 0.0)
 
 
 def odd(k):
@@ -77,16 +87,15 @@
 
 
 def join_kernel(patterns, slots, mine_ref, other_ref, a_ref, b_ref, out_ref, tail_ref):
-    half, tok, width = a_ref.shape
-    width //= 2
+    half, pair, width = a_ref.shape
     d = len(patterns) * width
     me = lax.axis_index("expert")
     for i, k in enumerate(patterns):
         info = other_ref if odd(k) else mine_ref
         block = a_ref[i] if i < half else b_ref[i - half]
-        picked = dot_nn(info[ROWS : 2 * ROWS, :tok].astype(BF), block)
-        dys = info[:ROWS, :1] * picked[:, width:]
-        for at, rows in ((0, picked[:, :width]), (d, dys)):
+        picked = dot_nn(info[ROWS : 3 * ROWS, :pair].astype(BF), block)
+        dys = info[:ROWS, :1] * picked[ROWS:]
+        for at, rows in ((0, picked[:ROWS]), (d, dys)):
             column = at + (me ^ k) * width
             out_ref[:, lanes_at(column, width)] = rows[:EIGHT].astype(BF)
             for x in range(slots - EIGHT):
@@ -194,8 +203,7 @@
 
 def chips_kernel(n, slots, mine_ref, other_ref, *refs):
     ins, outs, total_ref = refs[:n], refs[n:-1], refs[-1]
-    tok, width = outs[0].shape
-    width //= 2
+    width = outs[0].shape[1]
     d = len(outs) * width
     total = ins[0][...].astype(F32)
     for ref in ins[1:]:
@@ -216,20 +224,20 @@
         info = other_ref if k else mine_ref
         column = (me ^ k) * width
         rows = jnp.concatenate(
-            [(info[:ROWS, :1] * rows_at(column)).astype(BF), rows_at(d + column).astype(BF)], axis=1
+            [(info[:ROWS, :1] * rows_at(column)).astype(BF), rows_at(d + column).astype(BF)], axis=0
         )
-        back = info[2 * ROWS : 2 * ROWS + tok, :ROWS].astype(BF)
+        back = info[3 * ROWS :, : 2 * ROWS].astype(BF)
         out_ref[...] = dot_nn(back, rows).astype(BF)
 
 
 def home_kernel(*refs):
     ins, (mixed_ref, grad_ref) = refs[:-2], refs[-2:]
-    width = mixed_ref.shape[1]
+    tok = mixed_ref.shape[0]
     total = ins[0][...].astype(F32)
     for ref in ins[1:]:
         total = total + ref[...].astype(F32)
-    mixed_ref[...] = total[:, :width].astype(BF)
-    grad_ref[...] = total[:, width:].astype(BF)
+    mixed_ref[...] = total[:tok].astype(BF)
+    grad_ref[...] = total[tok:].astype(BF)
 
 
 def grads(spans, lefts, rights, old):
@@ -301,7 +309,7 @@
     tail = max(0, slots - EIGHT) * piece
     block_shape = (EIGHT, 2 * d + tail)
     tail_scratch = (EIGHT, max(tail, 128))
-    mine = jnp.concatenate([tokens, cotangent], axis=1)[None]
+    mine = jnp.concatenate([tokens, cotangent], axis=0)[None]
     patterns, hop, first = [0], n_e // 2, True
     while hop:
         patterns = patterns + [p ^ hop for p in patterns]
@@ -311,7 +319,7 @@
                 share_kernel,
                 in_specs=[VM, VM],
                 out_specs=VM,
-                out_shape=sds((3 * ROWS, 128), F32),
+                out_shape=sds((3 * ROWS + 2 * tok, 128), F32),
                 compiler_params=params(2),
                 cost_estimate=pl.CostEstimate(
                     flops=40 * rows * f * d, bytes_accessed=24 * f * d, transcendentals=0
@@ -330,7 +338,7 @@
                 [pltpu.VMEM(tail_scratch, F32)],
             )
         else:
-            mine = stack(pair_kernel, [mine, got], (len(patterns), tok, 2 * width), "pair")
+            mine = stack(pair_kernel, [mine, got], (len(patterns), 2 * tok, width), "pair")
         hop //= 2
     blocks = [block] + [swap(block, k, 0, 1) for k in range(1, n_chip)]
     blocks = blocks + [swap(b, 0, 0, 1) for b in blocks]
@@ -371,7 +379,7 @@
         functools.partial(chips_kernel, n_chip, slots),
         in_specs=[VM] * (n_chip + 2),
         out_specs=[VM] * n_e,
-        out_shape=[sds((tok, 2 * width), BF)] * n_e,
+        out_shape=[sds((2 * tok, width), BF)] * n_e,
         scratch_shapes=[pltpu.VMEM(block_shape, F32)],
         compiler_params=params(small),
         name="chips",

time: 47.1 us -> 46.4 us (0.985)
  starting transfers between devices: 18.5 us -> 18 us
  transfers between devices with their start and end apart: 17 -> 17, of which waited for: 10 -> 8; matrix products, arithmetic and copies ran while one was open for 0% -> 0% of each run, Pallas kernels for 20% -> 20%
where the time goes in v6:
time: 46.4 us; the launch traced here: 46 us
  Pallas kernels  18.8 us (41%)
  starting transfers between devices  18 us (39%)
  waiting for transfers between devices  6.32 us (14%)
  local copies, waits for them, and re-layouts  1.37 us (3%)
  other arithmetic  0.75 us (2%)
  between operations  0.74 us (2%)
    ppermute x17, starting transfers between devices, swap(): lax.ppermute(x, ('dp', 'expert'), [(i * n_e + j, (i ^ 2 * chips + core) *...  18 us
    pallas_call x3, Pallas kernels, grads(): pl.pallas_call(functools.partial(grads_kernel, jobs, n, len(kept)), in_sp...  9.02 us
    pallas_call x1, Pallas kernels, per_device(): pl.pallas_call(functools.partial(expert_kernel, n=n_chip, tile=tile, cols...  8.38 us
    ppermute x17, waiting for transfers between devices, swap(): lax.ppermute(x, ('dp', 'expert'), [(i * n_e + j, (i ^ 2 * chips + core) *...  6.32 us
    unnamed x10, local copies, waits for them, and re-layouts  1.37 us
  transfers between devices with their start and end apart: 17, of which 8 were waited for; matrix products, arithmetic and copies ran while one was open for 0% of the time, Pallas kernels for 20%

profile of v6, /device:TPU:0, one launch (start us, length us, event | category | flops | bytes accessed | tf_op | source)
XLA Modules:
  0.0 46.0 jit_solution(13673103669153156448)
XLA Ops:
  0.6 0.7 %maximum_bitcast_fusion.a_ref = bf16[1,24,512]{2,1,0:T(8,128)(2,1)S(1)} fusion(bf16[12,512]{1,0:T(8,128)(2,1)} %param.8, bf16[12,512]{1,0:T(8,128)(2,1)} %param.7), kind=kLoop, calls=%fused_computation | loop fusion | flops 49152 | bytes 49152 | tf_op jit(solution)/shard_map/broadcast_in_dim | solution.py:312
  1.4 3.5 %collective-permute-start = (bf16[1,24,512]{2,1,0:T(8,128)(2,1)S(1)}, bf16[1,24,512]{2,1,0:T(8,128)(2,1)S(1)}, u32[]{:S(2)}, u32[]{:S(2)}) collective-permute-start(bf16[1,24,512]{2,1,0:T(8,128)(2,1)S(1)} %maximum_bitcast_fusion.a_ref), channel_id=1, source_target_pairs={{0,6},{1,7},{2,4},{3,5},{4,2},{5,3},{6,0},{7,1},{8,14},{9,15},{10,... | collective-permute-start | bytes 73736 | tf_op jit(solution)/shard_map/ppermute | solution.py:296
  4.9 0.0 copy-start.3
  4.9 0.7 %copy-done.3 = s32[12,2]{0,1:T(2,128)S(1)} copy-done((s32[12,2]{0,1:T(2,128)S(1)}, s32[12,2]{0,1:T(2,128)}, u32[]{:S(2)}) %copy-start.3) | copy-done | bytes 120
  5.6 0.0 copy-start.4
  5.6 0.7 %copy-done.4 = f32[12,2]{0,1:T(2,128)S(1)} copy-done((f32[12,2]{0,1:T(2,128)S(1)}, f32[12,2]{0,1:T(2,128)}, u32[]{:S(2)}) %copy-start.4) | copy-done | bytes 120
  6.3 0.0 copy-start
  6.3 0.0 copy-start.1
  6.3 0.0 copy-start.2
  6.3 0.3 share.1.mine_ref
  6.6 0.0 collective-permute-done.b_ref
  6.6 1.9 %collective-permute-start.2 = (bf16[2,24,512]{2,1,0:T(8,128)(2,1)S(1)}, bf16[2,24,512]{2,1,0:T(8,128)(2,1)S(1)}, u32[]{:S(2)}, u32[]{:S(2)}) collective-permute-start(bf16[2,24,512]{2,1,0:T(8,128)(2,1)S(1)} %pair.1.a_ref), channel_id=1, source_target_pairs={{0,5},{1,4},{2,7},{3,6},{4,1},{5,0},{6,3},{7,2},{8,13},{9,12},{10,... | collective-permute-start | bytes 147464 | tf_op jit(solution)/shard_map/ppermute | solution.py:296
  8.6 0.2 collective-permute-start.1
  8.8 1.0 %collective-permute-done.1.other_ref = f32[72,128]{1,0:T(8,128)S(1)} collective-permute-done((f32[72,128]{1,0:T(8,128)S(1)}, f32[72,128]{1,0:T(8,128)S(1)}, u32[]{:S(2)}, u32[]{:S(2)}) %collective-permute-start.1) | collective-permute-done | bytes 36896 | tf_op jit(solution)/shard_map/ppermute | solution.py:296
  9.8 0.6 %collective-permute-done.2.b_ref = bf16[2,24,512]{2,1,0:T(8,128)(2,1)S(1)} collective-permute-done((bf16[2,24,512]{2,1,0:T(8,128)(2,1)S(1)}, bf16[2,24,512]{2,1,0:T(8,128)(2,1)S(1)}, u32[]{:S(2)}, u32[]{:S(2)}) %collective-permute-start.2) | collective-permute-done | bytes 49184 | tf_op jit(solution)/shard_map/ppermute | solution.py:296
  10.3 0.2 join.1.refs_0_
  10.5 2.7 %collective-permute-start.5 = (bf16[8,4608]{1,0:T(8,128)(2,1)S(1)}, bf16[8,4608]{1,0:T(8,128)(2,1)S(1)}, u32[]{:S(2)}, u32[]{:S(2)}) collective-permute-start(bf16[8,4608]{1,0:T(8,128)(2,1)S(1)} %join.1.refs_0_), channel_id=1, source_target_pairs={{0,28},{1,29},{2,30},{3,31},{4,24},{5,25},{6,26},{7,27},{8,20},{9,... | collective-permute-start | bytes 221192 | tf_op jit(solution)/shard_map/ppermute | solution.py:296
  13.2 0.4 collective-permute-start.4
  13.6 0.3 collective-permute-start.3
  13.9 0.0 collective-permute-start.6
  14.0 1.9 %collective-permute-done.5.refs_3_ = bf16[8,4608]{1,0:T(8,128)(2,1)S(1)} collective-permute-done((bf16[8,4608]{1,0:T(8,128)(2,1)S(1)}, bf16[8,4608]{1,0:T(8,128)(2,1)S(1)}, u32[]{:S(2)}, u32[]{:S(2)}) %collective-permute-start.5) | collective-permute-done | bytes 73760 | tf_op jit(solution)/shard_map/ppermute | solution.py:296
  15.8 0.0 collective-permute-start.9
  15.9 1.6 %collective-permute-done.4.refs_2_ = bf16[8,4608]{1,0:T(8,128)(2,1)S(1)} collective-permute-done((bf16[8,4608]{1,0:T(8,128)(2,1)S(1)}, bf16[8,4608]{1,0:T(8,128)(2,1)S(1)}, u32[]{:S(2)}, u32[]{:S(2)}) %collective-permute-start.4) | collective-permute-done | bytes 73760 | tf_op jit(solution)/shard_map/ppermute | solution.py:296
  17.4 0.5 %collective-permute-start.8 = (bf16[8,4608]{1,0:T(8,128)(2,1)S(1)}, bf16[8,4608]{1,0:T(8,128)(2,1)S(1)}, u32[]{:S(2)}, u32[]{:S(2)}) collective-permute-start(bf16[8,4608]{1,0:T(8,128)(2,1)S(1)} %collective-permute-done.4.refs_2_), channel_id=1, source_target_pairs={{0,4},{1,5},{2,6},{3,7},{4,0},{5,1},{6,2},{7,3},{8,12},{9,13},{10,... | collective-permute-start | bytes 221192 | tf_op jit(solution)/shard_map/ppermute | solution.py:296
  17.9 0.0 collective-permute-done.3.refs_1_
  17.9 0.1 collective-permute-start.7
  18.0 0.0 collective-permute-done.6.refs_4_
  18.0 0.0 collective-permute-done.9.refs_7_
  18.0 0.8 %collective-permute-done.8.refs_6_ = bf16[8,4608]{1,0:T(8,128)(2,1)S(1)} collective-permute-done((bf16[8,4608]{1,0:T(8,128)(2,1)S(1)}, bf16[8,4608]{1,0:T(8,128)(2,1)S(1)}, u32[]{:S(2)}, u32[]{:S(2)}) %collective-permute-start.8) | collective-permute-done | bytes 73760 | tf_op jit(solution)/shard_map/ppermute | solution.py:296
  18.8 0.4 collective-permute-done.7.refs_5_
  19.2 0.0 copy-done
  19.2 0.0 copy-done.1
  19.2 0.0 copy-done.2
  19.2 8.4 %expert.1 = (bf16[4,8,4608]{2,1,0:T(8,128)(2,1)S(1)}, bf16[4,8,4608]{2,1,0:T(8,128)(2,1)S(1)}, bf16[128,2048]{1,0:T(8,128)(2,1)S(1)}, bf16[128,2048]{1,0:T(8,128...) custom-call(bf16[8,4608]{1,0:T(8,128)(2,1)S(1)} %join.1.refs_0_, ...), custom_call_target="tpu_custom_call" | custom-call | flops 4831838208 | bytes 18874368 | tf_op jit(solution)/shard_map/expert/pallas_call | solution.py:347
  27.6 0.2 collective-permute-start.10
  27.8 1.4 %grads.3.refs_4_ = bf16[1536,2048]{1,0:T(8,128)(2,1)} custom-call(bf16[1536,128]{1,0:T(8,128)(2,1)S(1)} %get-tuple-element.45.refs_0_, bf16[128,2048]{1,0:T(8,128)(2,1)S(1)} %get-tuple-element.46.refs_1_.refs_2_), custom_call_target="tpu_custom_call" | custom-call | flops 201326592 | bytes 2359296 | tf_op jit(solution)/shard_map/grads/pallas_call | solution.py:253
  29.3 0.0 collective-permute-done.10.got_ref
  29.3 0.1 cores.1
  29.3 1.9 %collective-permute-start.11 = (bf16[8,4608]{1,0:T(8,128)(2,1)S(1)}, bf16[8,4608]{1,0:T(8,128)(2,1)S(1)}, u32[]{:S(2)}, u32[]{:S(2)}) collective-permute-start(bf16[8,4608]{1,0:T(8,128)(2,1)S(1)} %get-tuple-element.49), channel_id=1, source_target_pairs={{0,28},{1,29},{2,30},{3,31},{4,24},{5,25},{6,26},{7,27},{8,20},{9,... | collective-permute-start | bytes 221192 | tf_op jit(solution)/shard_map/ppermute | solution.py:296
  31.2 1.3 %collective-permute-start.12 = (bf16[8,4608]{1,0:T(8,128)(2,1)S(1)}, bf16[8,4608]{1,0:T(8,128)(2,1)S(1)}, u32[]{:S(2)}, u32[]{:S(2)}) collective-permute-start(bf16[8,4608]{1,0:T(8,128)(2,1)S(1)} %get-tuple-element.50), channel_id=1, source_target_pairs={{0,20},{1,21},{2,22},{3,23},{4,16},{5,17},{6,18},{7,19},{8,28},{9,... | collective-permute-start | bytes 221192 | tf_op jit(solution)/shard_map/ppermute | solution.py:296
  32.5 0.1 collective-permute-start.13
  32.6 4.0 %grads.4 = (bf16[1536,2048]{1,0:T(8,128)(2,1)}, bf16[1536,2048]{1,0:T(8,128)(2,1)}) custom-call(bf16[1536,128]{1,0:T(8,128)(2,1)S(1)} %get-tuple-element.45.refs_0_, bf16[1536,128]{1,0:T(8,128)(2,1)S(1)} %get-tuple-element.52.refs_1_, bf16[128,2048]{1,0:T(8,128)(2,1)S(1)} %get-tuple-element.46.refs_1_.refs_2_, ...), custom_call_target="tpu_custom_call", output_to_operand_aliasing={{0}: (4, {})} | custom-call | flops 1207959552 | bytes 14155776 | tf_op jit(solution)/shard_map/grads/pallas_call | solution.py:253
  36.6 0.0 collective-permute-done.11.refs_1_
  36.6 0.0 collective-permute-done.12.refs_2_
  36.6 0.1 collective-permute-done.13.refs_3_
  36.7 0.2 chips.1
  36.9 4.3 %collective-permute-start.14 = (bf16[24,512]{1,0:T(8,128)(2,1)S(1)}, bf16[24,512]{1,0:T(8,128)(2,1)S(1)}, u32[]{:S(2)}, u32[]{:S(2)}) collective-permute-start(bf16[24,512]{1,0:T(8,128)(2,1)S(1)} %get-tuple-element.61), channel_id=1, source_target_pairs={{0,7},{1,6},{2,5},{3,4},{4,3},{5,2},{6,1},{7,0},{8,15},{9,14},{10,... | collective-permute-start | bytes 73736 | tf_op jit(solution)/shard_map/ppermute | solution.py:296
  41.2 0.0 collective-permute-start.15
  41.2 0.5 %collective-permute-start.16 = (bf16[24,512]{1,0:T(8,128)(2,1)S(1)}, bf16[24,512]{1,0:T(8,128)(2,1)S(1)}, u32[]{:S(2)}, u32[]{:S(2)}) collective-permute-start(bf16[24,512]{1,0:T(8,128)(2,1)S(1)} %get-tuple-element.63), channel_id=1, source_target_pairs={{0,5},{1,4},{2,7},{3,6},{4,1},{5,0},{6,3},{7,2},{8,13},{9,12},{10,... | collective-permute-start | bytes 73736 | tf_op jit(solution)/shard_map/ppermute | solution.py:296
  41.8 3.5 %grads.5 = (bf16[1536,2048]{1,0:T(8,128)(2,1)}, bf16[1536,2048]{1,0:T(8,128)(2,1)}) custom-call(bf16[1536,128]{1,0:T(8,128)(2,1)S(1)} %get-tuple-element.45.refs_0_, bf16[1536,128]{1,0:T(8,128)(2,1)S(1)} %get-tuple-element.64.refs_1_, bf16[128,2048]{1,0:T(8,128)(2,1)S(1)} %get-tuple-element.46.refs_1_.refs_2_, ...), custom_call_target="tpu_custom_call", output_to_operand_aliasing={{0}: (4, {})} | custom-call | flops 1006632960 | bytes 11796480 | tf_op jit(solution)/shard_map/grads/pallas_call | solution.py:253
  45.3 0.0 collective-permute-done.14.refs_1_
  45.3 0.1 collective-permute-done.15.refs_2_
  45.4 0.0 collective-permute-done.16.refs_3_
  45.4 0.6 %home.1 = (bf16[12,512]{1,0:T(8,128)(2,1)}, bf16[12,512]{1,0:T(8,128)(2,1)}) custom-call(bf16[24,512]{1,0:T(8,128)(2,1)S(1)} %get-tuple-element.68.refs_0_, bf16[24,512]{1,0:T(8,128)(2,1)S(1)} %collective-permute-done.14.refs_1_, bf16[24,512]{1,0:T(8,128)(2,1)S(1)} %collective-permute-done.15.refs_2_, bf16[24,512]{1,0:T(8,128)(2,1)S(1)} %collective-permute-done.16.refs_3_), custom_call_target="tpu_custom_call" | custom-call | tf_op jit(solution)/shard_map/home/pallas_call | solution.py:392
  (1 shorter events, 0.0 us)
Async XLA Ops:
  1.4 5.2 %collective-permute-start = (bf16[1,24,512]{2,1,0:T(8,128)(2,1)S(1)}, bf16[1,24,512]{2,1,0:T(8,128)(2,1)S(1)}, u32[]{:S(2)}, u32[]{:S(2)}) collective-permute-start(bf16[1,24,512]{2,1,0:T(8,128)(2,1)S(1)} %maximum_bitcast_fusion.a_ref), channel_id=1, source_target_pairs={{0,6},{1,7},{2,4},{3,5},{4,2},{5,3},{6,0},{7,1},{8,14},{9,15},{10,... | collective-permute-start | bytes 73736 | tf_op jit(solution)/shard_map/ppermute | solution.py:296
  4.9 0.7 %copy-start.3 = (s32[12,2]{0,1:T(2,128)S(1)}, s32[12,2]{0,1:T(2,128)}, u32[]{:S(2)}) copy-start(s32[12,2]{0,1:T(2,128)} %param.9) | copy-start | bytes 292
  5.6 0.7 %copy-start.4 = (f32[12,2]{0,1:T(2,128)S(1)}, f32[12,2]{0,1:T(2,128)}, u32[]{:S(2)}) copy-start(f32[12,2]{0,1:T(2,128)} %param.10) | copy-start | bytes 292
  6.3 12.9 %copy-start = (bf16[1,1536,2048]{2,1,0:T(8,128)(2,1)S(1)}, bf16[1,1536,2048]{2,1,0:T(8,128)(2,1)}, u32[]{:S(2)}) copy-start(bf16[1,1536,2048]{2,1,0:T(8,128)(2,1)} %param.11) | copy-start | bytes 18874372
  6.3 12.9 %copy-start.1 = (bf16[1,1536,2048]{2,1,0:T(8,128)(2,1)S(1)}, bf16[1,1536,2048]{2,1,0:T(8,128)(2,1)}, u32[]{:S(2)}) copy-start(bf16[1,1536,2048]{2,1,0:T(8,128)(2,1)} %param.12) | copy-start | bytes 18874372
  6.3 12.9 %copy-start.2 = (bf16[1,1536,2048]{2,1,0:T(8,128)(2,1)S(1)}, bf16[1,1536,2048]{2,1,0:T(8,128)(2,1)}, u32[]{:S(2)}) copy-start(bf16[1,1536,2048]{2,1,0:T(8,128)(2,1)} %param.13) | copy-start | bytes 18874372
  6.6 3.7 %collective-permute-start.2 = (bf16[2,24,512]{2,1,0:T(8,128)(2,1)S(1)}, bf16[2,24,512]{2,1,0:T(8,128)(2,1)S(1)}, u32[]{:S(2)}, u32[]{:S(2)}) collective-permute-start(bf16[2,24,512]{2,1,0:T(8,128)(2,1)S(1)} %pair.1.a_ref), channel_id=1, source_target_pairs={{0,5},{1,4},{2,7},{3,6},{4,1},{5,0},{6,3},{7,2},{8,13},{9,12},{10,... | collective-permute-start | bytes 147464 | tf_op jit(solution)/shard_map/ppermute | solution.py:296
  8.6 1.2 %collective-permute-start.1 = (f32[72,128]{1,0:T(8,128)S(1)}, f32[72,128]{1,0:T(8,128)S(1)}, u32[]{:S(2)}, u32[]{:S(2)}) collective-permute-start(f32[72,128]{1,0:T(8,128)S(1)} %share.1.mine_ref), channel_id=1, source_target_pairs={{0,4},{1,5},{2,6},{3,7},{4,0},{5,1},{6,2},{7,3},{8,12},{9,13},{10,... | collective-permute-start | bytes 110600 | tf_op jit(solution)/shard_map/ppermute | solution.py:296
  10.5 5.3 %collective-permute-start.5 = (bf16[8,4608]{1,0:T(8,128)(2,1)S(1)}, bf16[8,4608]{1,0:T(8,128)(2,1)S(1)}, u32[]{:S(2)}, u32[]{:S(2)}) collective-permute-start(bf16[8,4608]{1,0:T(8,128)(2,1)S(1)} %join.1.refs_0_), channel_id=1, source_target_pairs={{0,28},{1,29},{2,30},{3,31},{4,24},{5,25},{6,26},{7,27},{8,20},{9,... | collective-permute-start | bytes 221192 | tf_op jit(solution)/shard_map/ppermute | solution.py:296
  13.2 4.2 %collective-permute-start.4 = (bf16[8,4608]{1,0:T(8,128)(2,1)S(1)}, bf16[8,4608]{1,0:T(8,128)(2,1)S(1)}, u32[]{:S(2)}, u32[]{:S(2)}) collective-permute-start(bf16[8,4608]{1,0:T(8,128)(2,1)S(1)} %join.1.refs_0_), channel_id=1, source_target_pairs={{0,20},{1,21},{2,22},{3,23},{4,16},{5,17},{6,18},{7,19},{8,28},{9,... | collective-permute-start | bytes 221192 | tf_op jit(solution)/shard_map/ppermute | solution.py:296
  13.6 4.3 %collective-permute-start.3 = (bf16[8,4608]{1,0:T(8,128)(2,1)S(1)}, bf16[8,4608]{1,0:T(8,128)(2,1)S(1)}, u32[]{:S(2)}, u32[]{:S(2)}) collective-permute-start(bf16[8,4608]{1,0:T(8,128)(2,1)S(1)} %join.1.refs_0_), channel_id=1, source_target_pairs={{0,12},{1,13},{2,14},{3,15},{4,8},{5,9},{6,10},{7,11},{8,4},{9,5},... | collective-permute-start | bytes 221192 | tf_op jit(solution)/shard_map/ppermute | solution.py:296
  13.9 4.0 %collective-permute-start.6 = (bf16[8,4608]{1,0:T(8,128)(2,1)S(1)}, bf16[8,4608]{1,0:T(8,128)(2,1)S(1)}, u32[]{:S(2)}, u32[]{:S(2)}) collective-permute-start(bf16[8,4608]{1,0:T(8,128)(2,1)S(1)} %join.1.refs_0_), channel_id=1, source_target_pairs={{0,4},{1,5},{2,6},{3,7},{4,0},{5,1},{6,2},{7,3},{8,12},{9,13},{10,... | collective-permute-start | bytes 221192 | tf_op jit(solution)/shard_map/ppermute | solution.py:296
  15.8 2.2 %collective-permute-start.9 = (bf16[8,4608]{1,0:T(8,128)(2,1)S(1)}, bf16[8,4608]{1,0:T(8,128)(2,1)S(1)}, u32[]{:S(2)}, u32[]{:S(2)}) collective-permute-start(bf16[8,4608]{1,0:T(8,128)(2,1)S(1)} %collective-permute-done.5.refs_3_), channel_id=1, source_target_pairs={{0,4},{1,5},{2,6},{3,7},{4,0},{5,1},{6,2},{7,3},{8,12},{9,13},{10,... | collective-permute-start | bytes 221192 | tf_op jit(solution)/shard_map/ppermute | solution.py:296
  17.4 1.4 %collective-permute-start.8 = (bf16[8,4608]{1,0:T(8,128)(2,1)S(1)}, bf16[8,4608]{1,0:T(8,128)(2,1)S(1)}, u32[]{:S(2)}, u32[]{:S(2)}) collective-permute-start(bf16[8,4608]{1,0:T(8,128)(2,1)S(1)} %collective-permute-done.4.refs_2_), channel_id=1, source_target_pairs={{0,4},{1,5},{2,6},{3,7},{4,0},{5,1},{6,2},{7,3},{8,12},{9,13},{10,... | collective-permute-start | bytes 221192 | tf_op jit(solution)/shard_map/ppermute | solution.py:296
  17.9 1.3 %collective-permute-start.7 = (bf16[8,4608]{1,0:T(8,128)(2,1)S(1)}, bf16[8,4608]{1,0:T(8,128)(2,1)S(1)}, u32[]{:S(2)}, u32[]{:S(2)}) collective-permute-start(bf16[8,4608]{1,0:T(8,128)(2,1)S(1)} %collective-permute-done.3.refs_1_), channel_id=1, source_target_pairs={{0,4},{1,5},{2,6},{3,7},{4,0},{5,1},{6,2},{7,3},{8,12},{9,13},{10,... | collective-permute-start | bytes 221192 | tf_op jit(solution)/shard_map/ppermute | solution.py:296
  27.6 1.7 %collective-permute-start.10 = (bf16[4,8,4608]{2,1,0:T(8,128)(2,1)S(1)}, bf16[4,8,4608]{2,1,0:T(8,128)(2,1)S(1)}, u32[]{:S(2)}, u32[]{:S(2)}) collective-permute-start(bf16[4,8,4608]{2,1,0:T(8,128)(2,1)S(1)} %get-tuple-element.44), channel_id=1, source_target_pairs={{0,4},{1,5},{2,6},{3,7},{4,0},{5,1},{6,2},{7,3},{8,12},{9,13},{10,... | collective-permute-start | bytes 884744 | tf_op jit(solution)/shard_map/ppermute | solution.py:296
  29.3 7.3 %collective-permute-start.11 = (bf16[8,4608]{1,0:T(8,128)(2,1)S(1)}, bf16[8,4608]{1,0:T(8,128)(2,1)S(1)}, u32[]{:S(2)}, u32[]{:S(2)}) collective-permute-start(bf16[8,4608]{1,0:T(8,128)(2,1)S(1)} %get-tuple-element.49), channel_id=1, source_target_pairs={{0,28},{1,29},{2,30},{3,31},{4,24},{5,25},{6,26},{7,27},{8,20},{9,... | collective-permute-start | bytes 221192 | tf_op jit(solution)/shard_map/ppermute | solution.py:296
  31.2 5.4 %collective-permute-start.12 = (bf16[8,4608]{1,0:T(8,128)(2,1)S(1)}, bf16[8,4608]{1,0:T(8,128)(2,1)S(1)}, u32[]{:S(2)}, u32[]{:S(2)}) collective-permute-start(bf16[8,4608]{1,0:T(8,128)(2,1)S(1)} %get-tuple-element.50), channel_id=1, source_target_pairs={{0,20},{1,21},{2,22},{3,23},{4,16},{5,17},{6,18},{7,19},{8,28},{9,... | collective-permute-start | bytes 221192 | tf_op jit(solution)/shard_map/ppermute | solution.py:296
  32.5 4.2 %collective-permute-start.13 = (bf16[8,4608]{1,0:T(8,128)(2,1)S(1)}, bf16[8,4608]{1,0:T(8,128)(2,1)S(1)}, u32[]{:S(2)}, u32[]{:S(2)}) collective-permute-start(bf16[8,4608]{1,0:T(8,128)(2,1)S(1)} %get-tuple-element.51), channel_id=1, source_target_pairs={{0,12},{1,13},{2,14},{3,15},{4,8},{5,9},{6,10},{7,11},{8,4},{9,5},... | collective-permute-start | bytes 221192 | tf_op jit(solution)/shard_map/ppermute | solution.py:296
  36.9 8.4 %collective-permute-start.14 = (bf16[24,512]{1,0:T(8,128)(2,1)S(1)}, bf16[24,512]{1,0:T(8,128)(2,1)S(1)}, u32[]{:S(2)}, u32[]{:S(2)}) collective-permute-start(bf16[24,512]{1,0:T(8,128)(2,1)S(1)} %get-tuple-element.61), channel_id=1, source_target_pairs={{0,7},{1,6},{2,5},{3,4},{4,3},{5,2},{6,1},{7,0},{8,15},{9,14},{10,... | collective-permute-start | bytes 73736 | tf_op jit(solution)/shard_map/ppermute | solution.py:296
  41.2 4.2 %collective-permute-start.15 = (bf16[24,512]{1,0:T(8,128)(2,1)S(1)}, bf16[24,512]{1,0:T(8,128)(2,1)S(1)}, u32[]{:S(2)}, u32[]{:S(2)}) collective-permute-start(bf16[24,512]{1,0:T(8,128)(2,1)S(1)} %get-tuple-element.62), channel_id=1, source_target_pairs={{0,6},{1,7},{2,4},{3,5},{4,2},{5,3},{6,0},{7,1},{8,14},{9,15},{10,... | collective-permute-start | bytes 73736 | tf_op jit(solution)/shard_map/ppermute | solution.py:296
  41.2 4.2 %collective-permute-start.16 = (bf16[24,512]{1,0:T(8,128)(2,1)S(1)}, bf16[24,512]{1,0:T(8,128)(2,1)S(1)}, u32[]{:S(2)}, u32[]{:S(2)}) collective-permute-start(bf16[24,512]{1,0:T(8,128)(2,1)S(1)} %get-tuple-element.63), channel_id=1, source_target_pairs={{0,5},{1,4},{2,7},{3,6},{4,1},{5,0},{6,3},{7,2},{8,13},{9,12},{10,... | collective-permute-start | bytes 73736 | tf_op jit(solution)/shard_map/ppermute | solution.py:296

commit v7 on v6

--- a/solution.py
+++ b/solution.py
@@ -384,7 +384,9 @@
         compiler_params=params(small),
         name="chips",
     )(info, other, parts[0], *arrived)
-    home = [summed[0]] + [swap(summed[k], 0, k, 1) for k in range(n_e - 1, 0, -1)]
+    home = [summed[0]] + [
+        swap(summed[k], 0, k, 1) for k in sorted(range(1, n_e), key=lambda k: (k != n_e // 2, -k))
+    ]
     grad_down, grad_up = grads(
         [(0, 18 * part, f), (1, 0, f)], [hidden, gpu], [dys, xs], [down, None]
     )

time: 46.4 us -> 46.3 us (level)
  transfers between devices with their start and end apart: 17 -> 17, of which waited for: 8 -> 7; matrix products, arithmetic and copies ran while one was open for 0% -> 0% of each run, Pallas kernels for 20% -> 20%
where the time goes in v7:
time: 46.3 us; the launch traced here: 45.9 us
  Pallas kernels  18.8 us (41%)
  starting transfers between devices  17.9 us (39%)
  waiting for transfers between devices  6.27 us (14%)
  local copies, waits for them, and re-layouts  1.37 us (3%)
  between operations  0.76 us (2%)
  other arithmetic  0.75 us (2%)
    ppermute x17, starting transfers between devices, swap(): lax.ppermute(x, ('dp', 'expert'), [(i * n_e + j, (i ^ 2 * chips + core) *...  17.9 us
    pallas_call x3, Pallas kernels, grads(): pl.pallas_call(functools.partial(grads_kernel, jobs, n, len(kept)), in_sp...  9.02 us
    pallas_call x1, Pallas kernels, per_device(): pl.pallas_call(functools.partial(expert_kernel, n=n_chip, tile=tile, cols...  8.38 us
    ppermute x17, waiting for transfers between devices, swap(): lax.ppermute(x, ('dp', 'expert'), [(i * n_e + j, (i ^ 2 * chips + core) *...  6.27 us
    unnamed x10, local copies, waits for them, and re-layouts  1.37 us
  transfers between devices with their start and end apart: 17, of which 7 were waited for; matrix products, arithmetic and copies ran while one was open for 0% of the time, Pallas kernels for 20%

profile of v7, /device:TPU:0, one launch (start us, length us, event | category | flops | bytes accessed | tf_op | source)
XLA Modules:
  0.0 45.9 jit_solution(6296157075495793316)
XLA Ops:
  0.6 0.7 %maximum_bitcast_fusion.a_ref = bf16[1,24,512]{2,1,0:T(8,128)(2,1)S(1)} fusion(bf16[12,512]{1,0:T(8,128)(2,1)} %param.8, bf16[12,512]{1,0:T(8,128)(2,1)} %param.7), kind=kLoop, calls=%fused_computation | loop fusion | flops 49152 | bytes 49152 | tf_op jit(solution)/shard_map/broadcast_in_dim | solution.py:312
  1.4 3.5 %collective-permute-start = (bf16[1,24,512]{2,1,0:T(8,128)(2,1)S(1)}, bf16[1,24,512]{2,1,0:T(8,128)(2,1)S(1)}, u32[]{:S(2)}, u32[]{:S(2)}) collective-permute-start(bf16[1,24,512]{2,1,0:T(8,128)(2,1)S(1)} %maximum_bitcast_fusion.a_ref), channel_id=1, source_target_pairs={{0,6},{1,7},{2,4},{3,5},{4,2},{5,3},{6,0},{7,1},{8,14},{9,15},{10,... | collective-permute-start | bytes 73736 | tf_op jit(solution)/shard_map/ppermute | solution.py:296
  4.9 0.0 copy-start.3
  4.9 0.7 %copy-done.3 = s32[12,2]{0,1:T(2,128)S(1)} copy-done((s32[12,2]{0,1:T(2,128)S(1)}, s32[12,2]{0,1:T(2,128)}, u32[]{:S(2)}) %copy-start.3) | copy-done | bytes 120
  5.6 0.0 copy-start.4
  5.6 0.7 %copy-done.4 = f32[12,2]{0,1:T(2,128)S(1)} copy-done((f32[12,2]{0,1:T(2,128)S(1)}, f32[12,2]{0,1:T(2,128)}, u32[]{:S(2)}) %copy-start.4) | copy-done | bytes 120
  6.3 0.0 copy-start
  6.3 0.0 copy-start.1
  6.3 0.0 copy-start.2
  6.3 0.3 share.1.mine_ref
  6.6 0.0 collective-permute-done.b_ref
  6.6 1.9 %collective-permute-start.2 = (bf16[2,24,512]{2,1,0:T(8,128)(2,1)S(1)}, bf16[2,24,512]{2,1,0:T(8,128)(2,1)S(1)}, u32[]{:S(2)}, u32[]{:S(2)}) collective-permute-start(bf16[2,24,512]{2,1,0:T(8,128)(2,1)S(1)} %pair.1.a_ref), channel_id=1, source_target_pairs={{0,5},{1,4},{2,7},{3,6},{4,1},{5,0},{6,3},{7,2},{8,13},{9,12},{10,... | collective-permute-start | bytes 147464 | tf_op jit(solution)/shard_map/ppermute | solution.py:296
  8.6 0.2 collective-permute-start.1
  8.8 1.0 %collective-permute-done.1.other_ref = f32[72,128]{1,0:T(8,128)S(1)} collective-permute-done((f32[72,128]{1,0:T(8,128)S(1)}, f32[72,128]{1,0:T(8,128)S(1)}, u32[]{:S(2)}, u32[]{:S(2)}) %collective-permute-start.1) | collective-permute-done | bytes 36896 | tf_op jit(solution)/shard_map/ppermute | solution.py:296
  9.8 0.6 %collective-permute-done.2.b_ref = bf16[2,24,512]{2,1,0:T(8,128)(2,1)S(1)} collective-permute-done((bf16[2,24,512]{2,1,0:T(8,128)(2,1)S(1)}, bf16[2,24,512]{2,1,0:T(8,128)(2,1)S(1)}, u32[]{:S(2)}, u32[]{:S(2)}) %collective-permute-start.2) | collective-permute-done | bytes 49184 | tf_op jit(solution)/shard_map/ppermute | solution.py:296
  10.3 0.2 join.1.refs_0_
  10.5 2.7 %collective-permute-start.5 = (bf16[8,4608]{1,0:T(8,128)(2,1)S(1)}, bf16[8,4608]{1,0:T(8,128)(2,1)S(1)}, u32[]{:S(2)}, u32[]{:S(2)}) collective-permute-start(bf16[8,4608]{1,0:T(8,128)(2,1)S(1)} %join.1.refs_0_), channel_id=1, source_target_pairs={{0,28},{1,29},{2,30},{3,31},{4,24},{5,25},{6,26},{7,27},{8,20},{9,... | collective-permute-start | bytes 221192 | tf_op jit(solution)/shard_map/ppermute | solution.py:296
  13.2 0.4 collective-permute-start.4
  13.6 0.3 collective-permute-start.3
  13.9 0.0 collective-permute-start.6
  14.0 1.9 %collective-permute-done.5.refs_3_ = bf16[8,4608]{1,0:T(8,128)(2,1)S(1)} collective-permute-done((bf16[8,4608]{1,0:T(8,128)(2,1)S(1)}, bf16[8,4608]{1,0:T(8,128)(2,1)S(1)}, u32[]{:S(2)}, u32[]{:S(2)}) %collective-permute-start.5) | collective-permute-done | bytes 73760 | tf_op jit(solution)/shard_map/ppermute | solution.py:296
  15.8 0.0 collective-permute-start.9
  15.9 1.6 %collective-permute-done.4.refs_2_ = bf16[8,4608]{1,0:T(8,128)(2,1)S(1)} collective-permute-done((bf16[8,4608]{1,0:T(8,128)(2,1)S(1)}, bf16[8,4608]{1,0:T(8,128)(2,1)S(1)}, u32[]{:S(2)}, u32[]{:S(2)}) %collective-permute-start.4) | collective-permute-done | bytes 73760 | tf_op jit(solution)/shard_map/ppermute | solution.py:296
  17.4 0.5 %collective-permute-start.8 = (bf16[8,4608]{1,0:T(8,128)(2,1)S(1)}, bf16[8,4608]{1,0:T(8,128)(2,1)S(1)}, u32[]{:S(2)}, u32[]{:S(2)}) collective-permute-start(bf16[8,4608]{1,0:T(8,128)(2,1)S(1)} %collective-permute-done.4.refs_2_), channel_id=1, source_target_pairs={{0,4},{1,5},{2,6},{3,7},{4,0},{5,1},{6,2},{7,3},{8,12},{9,13},{10,... | collective-permute-start | bytes 221192 | tf_op jit(solution)/shard_map/ppermute | solution.py:296
  17.9 0.0 collective-permute-done.3.refs_1_
  17.9 0.1 collective-permute-start.7
  18.0 0.0 collective-permute-done.6.refs_4_
  18.0 0.0 collective-permute-done.9.refs_7_
  18.0 0.8 %collective-permute-done.8.refs_6_ = bf16[8,4608]{1,0:T(8,128)(2,1)S(1)} collective-permute-done((bf16[8,4608]{1,0:T(8,128)(2,1)S(1)}, bf16[8,4608]{1,0:T(8,128)(2,1)S(1)}, u32[]{:S(2)}, u32[]{:S(2)}) %collective-permute-start.8) | collective-permute-done | bytes 73760 | tf_op jit(solution)/shard_map/ppermute | solution.py:296
  18.8 0.4 collective-permute-done.7.refs_5_
  19.2 0.0 copy-done
  19.2 0.0 copy-done.1
  19.2 0.0 copy-done.2
  19.2 8.4 %expert.1 = (bf16[4,8,4608]{2,1,0:T(8,128)(2,1)S(1)}, bf16[4,8,4608]{2,1,0:T(8,128)(2,1)S(1)}, bf16[128,2048]{1,0:T(8,128)(2,1)S(1)}, bf16[128,2048]{1,0:T(8,128...) custom-call(bf16[8,4608]{1,0:T(8,128)(2,1)S(1)} %join.1.refs_0_, ...), custom_call_target="tpu_custom_call" | custom-call | flops 4831838208 | bytes 18874368 | tf_op jit(solution)/shard_map/expert/pallas_call | solution.py:347
  27.6 0.2 collective-permute-start.10
  27.8 1.4 %grads.3.refs_4_ = bf16[1536,2048]{1,0:T(8,128)(2,1)} custom-call(bf16[1536,128]{1,0:T(8,128)(2,1)S(1)} %get-tuple-element.45.refs_0_, bf16[128,2048]{1,0:T(8,128)(2,1)S(1)} %get-tuple-element.46.refs_1_.refs_2_), custom_call_target="tpu_custom_call" | custom-call | flops 201326592 | bytes 2359296 | tf_op jit(solution)/shard_map/grads/pallas_call | solution.py:253
  29.3 0.0 collective-permute-done.10.got_ref
  29.3 0.1 cores.1
  29.3 1.9 %collective-permute-start.11 = (bf16[8,4608]{1,0:T(8,128)(2,1)S(1)}, bf16[8,4608]{1,0:T(8,128)(2,1)S(1)}, u32[]{:S(2)}, u32[]{:S(2)}) collective-permute-start(bf16[8,4608]{1,0:T(8,128)(2,1)S(1)} %get-tuple-element.49), channel_id=1, source_target_pairs={{0,28},{1,29},{2,30},{3,31},{4,24},{5,25},{6,26},{7,27},{8,20},{9,... | collective-permute-start | bytes 221192 | tf_op jit(solution)/shard_map/ppermute | solution.py:296
  31.2 1.3 %collective-permute-start.12 = (bf16[8,4608]{1,0:T(8,128)(2,1)S(1)}, bf16[8,4608]{1,0:T(8,128)(2,1)S(1)}, u32[]{:S(2)}, u32[]{:S(2)}) collective-permute-start(bf16[8,4608]{1,0:T(8,128)(2,1)S(1)} %get-tuple-element.50), channel_id=1, source_target_pairs={{0,20},{1,21},{2,22},{3,23},{4,16},{5,17},{6,18},{7,19},{8,28},{9,... | collective-permute-start | bytes 221192 | tf_op jit(solution)/shard_map/ppermute | solution.py:296
  32.5 0.1 collective-permute-start.13
  32.6 4.0 %grads.4 = (bf16[1536,2048]{1,0:T(8,128)(2,1)}, bf16[1536,2048]{1,0:T(8,128)(2,1)}) custom-call(bf16[1536,128]{1,0:T(8,128)(2,1)S(1)} %get-tuple-element.45.refs_0_, bf16[1536,128]{1,0:T(8,128)(2,1)S(1)} %get-tuple-element.52.refs_1_, bf16[128,2048]{1,0:T(8,128)(2,1)S(1)} %get-tuple-element.46.refs_1_.refs_2_, ...), custom_call_target="tpu_custom_call", output_to_operand_aliasing={{0}: (4, {})} | custom-call | flops 1207959552 | bytes 14155776 | tf_op jit(solution)/shard_map/grads/pallas_call | solution.py:253
  36.6 0.0 collective-permute-done.11.refs_1_
  36.6 0.0 collective-permute-done.12.refs_2_
  36.6 0.1 collective-permute-done.13.refs_3_
  36.7 0.2 chips.1
  36.9 2.8 %collective-permute-start.14 = (bf16[24,512]{1,0:T(8,128)(2,1)S(1)}, bf16[24,512]{1,0:T(8,128)(2,1)S(1)}, u32[]{:S(2)}, u32[]{:S(2)}) collective-permute-start(bf16[24,512]{1,0:T(8,128)(2,1)S(1)} %get-tuple-element.61), channel_id=1, source_target_pairs={{0,6},{1,7},{2,4},{3,5},{4,2},{5,3},{6,0},{7,1},{8,14},{9,15},{10,... | collective-permute-start | bytes 73736 | tf_op jit(solution)/shard_map/ppermute | solution.py:296
  39.7 1.6 %collective-permute-start.15 = (bf16[24,512]{1,0:T(8,128)(2,1)S(1)}, bf16[24,512]{1,0:T(8,128)(2,1)S(1)}, u32[]{:S(2)}, u32[]{:S(2)}) collective-permute-start(bf16[24,512]{1,0:T(8,128)(2,1)S(1)} %get-tuple-element.62), channel_id=1, source_target_pairs={{0,7},{1,6},{2,5},{3,4},{4,3},{5,2},{6,1},{7,0},{8,15},{9,14},{10,... | collective-permute-start | bytes 73736 | tf_op jit(solution)/shard_map/ppermute | solution.py:296
  41.3 0.4 collective-permute-start.16
  41.7 3.5 %grads.5 = (bf16[1536,2048]{1,0:T(8,128)(2,1)}, bf16[1536,2048]{1,0:T(8,128)(2,1)}) custom-call(bf16[1536,128]{1,0:T(8,128)(2,1)S(1)} %get-tuple-element.45.refs_0_, bf16[1536,128]{1,0:T(8,128)(2,1)S(1)} %get-tuple-element.64.refs_1_, bf16[128,2048]{1,0:T(8,128)(2,1)S(1)} %get-tuple-element.46.refs_1_.refs_2_, ...), custom_call_target="tpu_custom_call", output_to_operand_aliasing={{0}: (4, {})} | custom-call | flops 1006632960 | bytes 11796480 | tf_op jit(solution)/shard_map/grads/pallas_call | solution.py:253
  45.2 0.0 collective-permute-done.14.refs_1_
  45.2 0.0 collective-permute-done.15.refs_2_
  45.3 0.0 collective-permute-done.16.refs_3_
  45.3 0.6 %home.1 = (bf16[12,512]{1,0:T(8,128)(2,1)}, bf16[12,512]{1,0:T(8,128)(2,1)}) custom-call(bf16[24,512]{1,0:T(8,128)(2,1)S(1)} %get-tuple-element.68.refs_0_, bf16[24,512]{1,0:T(8,128)(2,1)S(1)} %collective-permute-done.14.refs_1_, bf16[24,512]{1,0:T(8,128)(2,1)S(1)} %collective-permute-done.15.refs_2_, bf16[24,512]{1,0:T(8,128)(2,1)S(1)} %collective-permute-done.16.refs_3_), custom_call_target="tpu_custom_call" | custom-call | tf_op jit(solution)/shard_map/home/pallas_call | solution.py:394
  (1 shorter events, 0.0 us)
Async XLA Ops:
  1.4 5.2 %collective-permute-start = (bf16[1,24,512]{2,1,0:T(8,128)(2,1)S(1)}, bf16[1,24,512]{2,1,0:T(8,128)(2,1)S(1)}, u32[]{:S(2)}, u32[]{:S(2)}) collective-permute-start(bf16[1,24,512]{2,1,0:T(8,128)(2,1)S(1)} %maximum_bitcast_fusion.a_ref), channel_id=1, source_target_pairs={{0,6},{1,7},{2,4},{3,5},{4,2},{5,3},{6,0},{7,1},{8,14},{9,15},{10,... | collective-permute-start | bytes 73736 | tf_op jit(solution)/shard_map/ppermute | solution.py:296
  4.9 0.7 %copy-start.3 = (s32[12,2]{0,1:T(2,128)S(1)}, s32[12,2]{0,1:T(2,128)}, u32[]{:S(2)}) copy-start(s32[12,2]{0,1:T(2,128)} %param.9) | copy-start | bytes 292
  5.6 0.7 %copy-start.4 = (f32[12,2]{0,1:T(2,128)S(1)}, f32[12,2]{0,1:T(2,128)}, u32[]{:S(2)}) copy-start(f32[12,2]{0,1:T(2,128)} %param.10) | copy-start | bytes 292
  6.3 12.9 %copy-start = (bf16[1,1536,2048]{2,1,0:T(8,128)(2,1)S(1)}, bf16[1,1536,2048]{2,1,0:T(8,128)(2,1)}, u32[]{:S(2)}) copy-start(bf16[1,1536,2048]{2,1,0:T(8,128)(2,1)} %param.11) | copy-start | bytes 18874372
  6.3 12.9 %copy-start.1 = (bf16[1,1536,2048]{2,1,0:T(8,128)(2,1)S(1)}, bf16[1,1536,2048]{2,1,0:T(8,128)(2,1)}, u32[]{:S(2)}) copy-start(bf16[1,1536,2048]{2,1,0:T(8,128)(2,1)} %param.12) | copy-start | bytes 18874372
  6.3 12.9 %copy-start.2 = (bf16[1,1536,2048]{2,1,0:T(8,128)(2,1)S(1)}, bf16[1,1536,2048]{2,1,0:T(8,128)(2,1)}, u32[]{:S(2)}) copy-start(bf16[1,1536,2048]{2,1,0:T(8,128)(2,1)} %param.13) | copy-start | bytes 18874372
  6.6 3.7 %collective-permute-start.2 = (bf16[2,24,512]{2,1,0:T(8,128)(2,1)S(1)}, bf16[2,24,512]{2,1,0:T(8,128)(2,1)S(1)}, u32[]{:S(2)}, u32[]{:S(2)}) collective-permute-start(bf16[2,24,512]{2,1,0:T(8,128)(2,1)S(1)} %pair.1.a_ref), channel_id=1, source_target_pairs={{0,5},{1,4},{2,7},{3,6},{4,1},{5,0},{6,3},{7,2},{8,13},{9,12},{10,... | collective-permute-start | bytes 147464 | tf_op jit(solution)/shard_map/ppermute | solution.py:296
  8.6 1.2 %collective-permute-start.1 = (f32[72,128]{1,0:T(8,128)S(1)}, f32[72,128]{1,0:T(8,128)S(1)}, u32[]{:S(2)}, u32[]{:S(2)}) collective-permute-start(f32[72,128]{1,0:T(8,128)S(1)} %share.1.mine_ref), channel_id=1, source_target_pairs={{0,4},{1,5},{2,6},{3,7},{4,0},{5,1},{6,2},{7,3},{8,12},{9,13},{10,... | collective-permute-start | bytes 110600 | tf_op jit(solution)/shard_map/ppermute | solution.py:296
  10.5 5.3 %collective-permute-start.5 = (bf16[8,4608]{1,0:T(8,128)(2,1)S(1)}, bf16[8,4608]{1,0:T(8,128)(2,1)S(1)}, u32[]{:S(2)}, u32[]{:S(2)}) collective-permute-start(bf16[8,4608]{1,0:T(8,128)(2,1)S(1)} %join.1.refs_0_), channel_id=1, source_target_pairs={{0,28},{1,29},{2,30},{3,31},{4,24},{5,25},{6,26},{7,27},{8,20},{9,... | collective-permute-start | bytes 221192 | tf_op jit(solution)/shard_map/ppermute | solution.py:296
  13.2 4.2 %collective-permute-start.4 = (bf16[8,4608]{1,0:T(8,128)(2,1)S(1)}, bf16[8,4608]{1,0:T(8,128)(2,1)S(1)}, u32[]{:S(2)}, u32[]{:S(2)}) collective-permute-start(bf16[8,4608]{1,0:T(8,128)(2,1)S(1)} %join.1.refs_0_), channel_id=1, source_target_pairs={{0,20},{1,21},{2,22},{3,23},{4,16},{5,17},{6,18},{7,19},{8,28},{9,... | collective-permute-start | bytes 221192 | tf_op jit(solution)/shard_map/ppermute | solution.py:296
  13.6 4.3 %collective-permute-start.3 = (bf16[8,4608]{1,0:T(8,128)(2,1)S(1)}, bf16[8,4608]{1,0:T(8,128)(2,1)S(1)}, u32[]{:S(2)}, u32[]{:S(2)}) collective-permute-start(bf16[8,4608]{1,0:T(8,128)(2,1)S(1)} %join.1.refs_0_), channel_id=1, source_target_pairs={{0,12},{1,13},{2,14},{3,15},{4,8},{5,9},{6,10},{7,11},{8,4},{9,5},... | collective-permute-start | bytes 221192 | tf_op jit(solution)/shard_map/ppermute | solution.py:296
  13.9 4.0 %collective-permute-start.6 = (bf16[8,4608]{1,0:T(8,128)(2,1)S(1)}, bf16[8,4608]{1,0:T(8,128)(2,1)S(1)}, u32[]{:S(2)}, u32[]{:S(2)}) collective-permute-start(bf16[8,4608]{1,0:T(8,128)(2,1)S(1)} %join.1.refs_0_), channel_id=1, source_target_pairs={{0,4},{1,5},{2,6},{3,7},{4,0},{5,1},{6,2},{7,3},{8,12},{9,13},{10,... | collective-permute-start | bytes 221192 | tf_op jit(solution)/shard_map/ppermute | solution.py:296
  15.8 2.2 %collective-permute-start.9 = (bf16[8,4608]{1,0:T(8,128)(2,1)S(1)}, bf16[8,4608]{1,0:T(8,128)(2,1)S(1)}, u32[]{:S(2)}, u32[]{:S(2)}) collective-permute-start(bf16[8,4608]{1,0:T(8,128)(2,1)S(1)} %collective-permute-done.5.refs_3_), channel_id=1, source_target_pairs={{0,4},{1,5},{2,6},{3,7},{4,0},{5,1},{6,2},{7,3},{8,12},{9,13},{10,... | collective-permute-start | bytes 221192 | tf_op jit(solution)/shard_map/ppermute | solution.py:296
  17.4 1.4 %collective-permute-start.8 = (bf16[8,4608]{1,0:T(8,128)(2,1)S(1)}, bf16[8,4608]{1,0:T(8,128)(2,1)S(1)}, u32[]{:S(2)}, u32[]{:S(2)}) collective-permute-start(bf16[8,4608]{1,0:T(8,128)(2,1)S(1)} %collective-permute-done.4.refs_2_), channel_id=1, source_target_pairs={{0,4},{1,5},{2,6},{3,7},{4,0},{5,1},{6,2},{7,3},{8,12},{9,13},{10,... | collective-permute-start | bytes 221192 | tf_op jit(solution)/shard_map/ppermute | solution.py:296
  17.9 1.3 %collective-permute-start.7 = (bf16[8,4608]{1,0:T(8,128)(2,1)S(1)}, bf16[8,4608]{1,0:T(8,128)(2,1)S(1)}, u32[]{:S(2)}, u32[]{:S(2)}) collective-permute-start(bf16[8,4608]{1,0:T(8,128)(2,1)S(1)} %collective-permute-done.3.refs_1_), channel_id=1, source_target_pairs={{0,4},{1,5},{2,6},{3,7},{4,0},{5,1},{6,2},{7,3},{8,12},{9,13},{10,... | collective-permute-start | bytes 221192 | tf_op jit(solution)/shard_map/ppermute | solution.py:296
  27.6 1.7 %collective-permute-start.10 = (bf16[4,8,4608]{2,1,0:T(8,128)(2,1)S(1)}, bf16[4,8,4608]{2,1,0:T(8,128)(2,1)S(1)}, u32[]{:S(2)}, u32[]{:S(2)}) collective-permute-start(bf16[4,8,4608]{2,1,0:T(8,128)(2,1)S(1)} %get-tuple-element.44), channel_id=1, source_target_pairs={{0,4},{1,5},{2,6},{3,7},{4,0},{5,1},{6,2},{7,3},{8,12},{9,13},{10,... | collective-permute-start | bytes 884744 | tf_op jit(solution)/shard_map/ppermute | solution.py:296
  29.3 7.3 %collective-permute-start.11 = (bf16[8,4608]{1,0:T(8,128)(2,1)S(1)}, bf16[8,4608]{1,0:T(8,128)(2,1)S(1)}, u32[]{:S(2)}, u32[]{:S(2)}) collective-permute-start(bf16[8,4608]{1,0:T(8,128)(2,1)S(1)} %get-tuple-element.49), channel_id=1, source_target_pairs={{0,28},{1,29},{2,30},{3,31},{4,24},{5,25},{6,26},{7,27},{8,20},{9,... | collective-permute-start | bytes 221192 | tf_op jit(solution)/shard_map/ppermute | solution.py:296
  31.2 5.4 %collective-permute-start.12 = (bf16[8,4608]{1,0:T(8,128)(2,1)S(1)}, bf16[8,4608]{1,0:T(8,128)(2,1)S(1)}, u32[]{:S(2)}, u32[]{:S(2)}) collective-permute-start(bf16[8,4608]{1,0:T(8,128)(2,1)S(1)} %get-tuple-element.50), channel_id=1, source_target_pairs={{0,20},{1,21},{2,22},{3,23},{4,16},{5,17},{6,18},{7,19},{8,28},{9,... | collective-permute-start | bytes 221192 | tf_op jit(solution)/shard_map/ppermute | solution.py:296
  32.5 4.2 %collective-permute-start.13 = (bf16[8,4608]{1,0:T(8,128)(2,1)S(1)}, bf16[8,4608]{1,0:T(8,128)(2,1)S(1)}, u32[]{:S(2)}, u32[]{:S(2)}) collective-permute-start(bf16[8,4608]{1,0:T(8,128)(2,1)S(1)} %get-tuple-element.51), channel_id=1, source_target_pairs={{0,12},{1,13},{2,14},{3,15},{4,8},{5,9},{6,10},{7,11},{8,4},{9,5},... | collective-permute-start | bytes 221192 | tf_op jit(solution)/shard_map/ppermute | solution.py:296
  36.9 8.3 %collective-permute-start.14 = (bf16[24,512]{1,0:T(8,128)(2,1)S(1)}, bf16[24,512]{1,0:T(8,128)(2,1)S(1)}, u32[]{:S(2)}, u32[]{:S(2)}) collective-permute-start(bf16[24,512]{1,0:T(8,128)(2,1)S(1)} %get-tuple-element.61), channel_id=1, source_target_pairs={{0,6},{1,7},{2,4},{3,5},{4,2},{5,3},{6,0},{7,1},{8,14},{9,15},{10,... | collective-permute-start | bytes 73736 | tf_op jit(solution)/shard_map/ppermute | solution.py:296
  39.7 5.5 %collective-permute-start.15 = (bf16[24,512]{1,0:T(8,128)(2,1)S(1)}, bf16[24,512]{1,0:T(8,128)(2,1)S(1)}, u32[]{:S(2)}, u32[]{:S(2)}) collective-permute-start(bf16[24,512]{1,0:T(8,128)(2,1)S(1)} %get-tuple-element.62), channel_id=1, source_target_pairs={{0,7},{1,6},{2,5},{3,4},{4,3},{5,2},{6,1},{7,0},{8,15},{9,14},{10,... | collective-permute-start | bytes 73736 | tf_op jit(solution)/shard_map/ppermute | solution.py:296
  41.3 4.0 %collective-permute-start.16 = (bf16[24,512]{1,0:T(8,128)(2,1)S(1)}, bf16[24,512]{1,0:T(8,128)(2,1)S(1)}, u32[]{:S(2)}, u32[]{:S(2)}) collective-permute-start(bf16[24,512]{1,0:T(8,128)(2,1)S(1)} %get-tuple-element.63), channel_id=1, source_target_pairs={{0,5},{1,4},{2,7},{3,6},{4,1},{5,0},{6,3},{7,2},{8,13},{9,12},{10,... | collective-permute-start | bytes 73736 | tf_op jit(solution)/shard_map/ppermute | solution.py:296

commit v8 on v7

--- a/solution.py
+++ b/solution.py
@@ -245,7 +245,7 @@
     f, rows = lefts[0].shape
     d = rights[0].shape[1]
     kept = [a for a in range(n) if old[a] is not None]
-    size = f // 12
+    size = f // (24 if n == 1 else 12)
     jobs = [
         (a, at, min(size, stop - at)) for a, start, stop in spans for at in range(start, stop, size)
     ]

time: 46.3 us -> 46.2 us (level)
  no operation moved by 1% of the time
where the time goes in v8:
time: 46.2 us; the launch traced here: 45.9 us
  Pallas kernels  18.8 us (41%)
  starting transfers between devices  17.9 us (39%)
  waiting for transfers between devices  6.28 us (14%)
  local copies, waits for them, and re-layouts  1.37 us (3%)
  between operations  0.76 us (2%)
  other arithmetic  0.75 us (2%)
    ppermute x17, starting transfers between devices, swap(): lax.ppermute(x, ('dp', 'expert'), [(i * n_e + j, (i ^ 2 * chips + core) *...  17.9 us
    pallas_call x3, Pallas kernels, grads(): pl.pallas_call(functools.partial(grads_kernel, jobs, n, len(kept)), in_sp...  8.98 us
    pallas_call x1, Pallas kernels, per_device(): pl.pallas_call(functools.partial(expert_kernel, n=n_chip, tile=tile, cols...  8.38 us
    ppermute x17, waiting for transfers between devices, swap(): lax.ppermute(x, ('dp', 'expert'), [(i * n_e + j, (i ^ 2 * chips + core) *...  6.28 us
    unnamed x10, local copies, waits for them, and re-layouts  1.37 us
  transfers between devices with their start and end apart: 17, of which 7 were waited for; matrix products, arithmetic and copies ran while one was open for 0% of the time, Pallas kernels for 20%

profile of v8, /device:TPU:0, one launch (start us, length us, event | category | flops | bytes accessed | tf_op | source)
XLA Modules:
  0.0 45.9 jit_solution(2233819543717504660)
XLA Ops:
  0.6 0.7 %maximum_bitcast_fusion.a_ref = bf16[1,24,512]{2,1,0:T(8,128)(2,1)S(1)} fusion(bf16[12,512]{1,0:T(8,128)(2,1)} %param.8, bf16[12,512]{1,0:T(8,128)(2,1)} %param.7), kind=kLoop, calls=%fused_computation | loop fusion | flops 49152 | bytes 49152 | tf_op jit(solution)/shard_map/broadcast_in_dim | solution.py:312
  1.4 3.5 %collective-permute-start = (bf16[1,24,512]{2,1,0:T(8,128)(2,1)S(1)}, bf16[1,24,512]{2,1,0:T(8,128)(2,1)S(1)}, u32[]{:S(2)}, u32[]{:S(2)}) collective-permute-start(bf16[1,24,512]{2,1,0:T(8,128)(2,1)S(1)} %maximum_bitcast_fusion.a_ref), channel_id=1, source_target_pairs={{0,6},{1,7},{2,4},{3,5},{4,2},{5,3},{6,0},{7,1},{8,14},{9,15},{10,... | collective-permute-start | bytes 73736 | tf_op jit(solution)/shard_map/ppermute | solution.py:296
  4.9 0.0 copy-start.3
  4.9 0.7 %copy-done.3 = s32[12,2]{0,1:T(2,128)S(1)} copy-done((s32[12,2]{0,1:T(2,128)S(1)}, s32[12,2]{0,1:T(2,128)}, u32[]{:S(2)}) %copy-start.3) | copy-done | bytes 120
  5.6 0.0 copy-start.4
  5.6 0.7 %copy-done.4 = f32[12,2]{0,1:T(2,128)S(1)} copy-done((f32[12,2]{0,1:T(2,128)S(1)}, f32[12,2]{0,1:T(2,128)}, u32[]{:S(2)}) %copy-start.4) | copy-done | bytes 120
  6.3 0.0 copy-start
  6.3 0.0 copy-start.1
  6.3 0.0 copy-start.2
  6.3 0.3 share.1.mine_ref
  6.6 0.0 collective-permute-done.b_ref
  6.6 1.9 %collective-permute-start.2 = (bf16[2,24,512]{2,1,0:T(8,128)(2,1)S(1)}, bf16[2,24,512]{2,1,0:T(8,128)(2,1)S(1)}, u32[]{:S(2)}, u32[]{:S(2)}) collective-permute-start(bf16[2,24,512]{2,1,0:T(8,128)(2,1)S(1)} %pair.1.a_ref), channel_id=1, source_target_pairs={{0,5},{1,4},{2,7},{3,6},{4,1},{5,0},{6,3},{7,2},{8,13},{9,12},{10,... | collective-permute-start | bytes 147464 | tf_op jit(solution)/shard_map/ppermute | solution.py:296
  8.6 0.2 collective-permute-start.1
  8.8 1.0 %collective-permute-done.1.other_ref = f32[72,128]{1,0:T(8,128)S(1)} collective-permute-done((f32[72,128]{1,0:T(8,128)S(1)}, f32[72,128]{1,0:T(8,128)S(1)}, u32[]{:S(2)}, u32[]{:S(2)}) %collective-permute-start.1) | collective-permute-done | bytes 36896 | tf_op jit(solution)/shard_map/ppermute | solution.py:296
  9.8 0.6 %collective-permute-done.2.b_ref = bf16[2,24,512]{2,1,0:T(8,128)(2,1)S(1)} collective-permute-done((bf16[2,24,512]{2,1,0:T(8,128)(2,1)S(1)}, bf16[2,24,512]{2,1,0:T(8,128)(2,1)S(1)}, u32[]{:S(2)}, u32[]{:S(2)}) %collective-permute-start.2) | collective-permute-done | bytes 49184 | tf_op jit(solution)/shard_map/ppermute | solution.py:296
  10.3 0.2 join.1.refs_0_
  10.5 2.7 %collective-permute-start.5 = (bf16[8,4608]{1,0:T(8,128)(2,1)S(1)}, bf16[8,4608]{1,0:T(8,128)(2,1)S(1)}, u32[]{:S(2)}, u32[]{:S(2)}) collective-permute-start(bf16[8,4608]{1,0:T(8,128)(2,1)S(1)} %join.1.refs_0_), channel_id=1, source_target_pairs={{0,28},{1,29},{2,30},{3,31},{4,24},{5,25},{6,26},{7,27},{8,20},{9,... | collective-permute-start | bytes 221192 | tf_op jit(solution)/shard_map/ppermute | solution.py:296
  13.2 0.4 collective-permute-start.4
  13.6 0.3 collective-permute-start.3
  13.9 0.0 collective-permute-start.6
  14.0 1.9 %collective-permute-done.5.refs_3_ = bf16[8,4608]{1,0:T(8,128)(2,1)S(1)} collective-permute-done((bf16[8,4608]{1,0:T(8,128)(2,1)S(1)}, bf16[8,4608]{1,0:T(8,128)(2,1)S(1)}, u32[]{:S(2)}, u32[]{:S(2)}) %collective-permute-start.5) | collective-permute-done | bytes 73760 | tf_op jit(solution)/shard_map/ppermute | solution.py:296
  15.8 0.0 collective-permute-start.9
  15.9 1.6 %collective-permute-done.4.refs_2_ = bf16[8,4608]{1,0:T(8,128)(2,1)S(1)} collective-permute-done((bf16[8,4608]{1,0:T(8,128)(2,1)S(1)}, bf16[8,4608]{1,0:T(8,128)(2,1)S(1)}, u32[]{:S(2)}, u32[]{:S(2)}) %collective-permute-start.4) | collective-permute-done | bytes 73760 | tf_op jit(solution)/shard_map/ppermute | solution.py:296
  17.4 0.5 %collective-permute-start.8 = (bf16[8,4608]{1,0:T(8,128)(2,1)S(1)}, bf16[8,4608]{1,0:T(8,128)(2,1)S(1)}, u32[]{:S(2)}, u32[]{:S(2)}) collective-permute-start(bf16[8,4608]{1,0:T(8,128)(2,1)S(1)} %collective-permute-done.4.refs_2_), channel_id=1, source_target_pairs={{0,4},{1,5},{2,6},{3,7},{4,0},{5,1},{6,2},{7,3},{8,12},{9,13},{10,... | collective-permute-start | bytes 221192 | tf_op jit(solution)/shard_map/ppermute | solution.py:296
  17.9 0.0 collective-permute-done.3.refs_1_
  17.9 0.1 collective-permute-start.7
  18.0 0.0 collective-permute-done.6.refs_4_
  18.0 0.0 collective-permute-done.9.refs_7_
  18.0 0.8 %collective-permute-done.8.refs_6_ = bf16[8,4608]{1,0:T(8,128)(2,1)S(1)} collective-permute-done((bf16[8,4608]{1,0:T(8,128)(2,1)S(1)}, bf16[8,4608]{1,0:T(8,128)(2,1)S(1)}, u32[]{:S(2)}, u32[]{:S(2)}) %collective-permute-start.8) | collective-permute-done | bytes 73760 | tf_op jit(solution)/shard_map/ppermute | solution.py:296
  18.8 0.4 collective-permute-done.7.refs_5_
  19.2 0.0 copy-done
  19.2 0.0 copy-done.1
  19.2 0.0 copy-done.2
  19.2 8.4 %expert.1 = (bf16[4,8,4608]{2,1,0:T(8,128)(2,1)S(1)}, bf16[4,8,4608]{2,1,0:T(8,128)(2,1)S(1)}, bf16[128,2048]{1,0:T(8,128)(2,1)S(1)}, bf16[128,2048]{1,0:T(8,128...) custom-call(bf16[8,4608]{1,0:T(8,128)(2,1)S(1)} %join.1.refs_0_, ...), custom_call_target="tpu_custom_call" | custom-call | flops 4831838208 | bytes 18874368 | tf_op jit(solution)/shard_map/expert/pallas_call | solution.py:347
  27.6 0.2 collective-permute-start.10
  27.8 1.4 %grads.3.refs_4_ = bf16[1536,2048]{1,0:T(8,128)(2,1)} custom-call(bf16[1536,128]{1,0:T(8,128)(2,1)S(1)} %get-tuple-element.45.refs_0_, bf16[128,2048]{1,0:T(8,128)(2,1)S(1)} %get-tuple-element.46.refs_1_.refs_2_), custom_call_target="tpu_custom_call" | custom-call | flops 201326592 | bytes 2359296 | tf_op jit(solution)/shard_map/grads/pallas_call | solution.py:253
  29.2 0.0 collective-permute-done.10.got_ref
  29.2 0.1 cores.1
  29.3 1.9 %collective-permute-start.11 = (bf16[8,4608]{1,0:T(8,128)(2,1)S(1)}, bf16[8,4608]{1,0:T(8,128)(2,1)S(1)}, u32[]{:S(2)}, u32[]{:S(2)}) collective-permute-start(bf16[8,4608]{1,0:T(8,128)(2,1)S(1)} %get-tuple-element.49), channel_id=1, source_target_pairs={{0,28},{1,29},{2,30},{3,31},{4,24},{5,25},{6,26},{7,27},{8,20},{9,... | collective-permute-start | bytes 221192 | tf_op jit(solution)/shard_map/ppermute | solution.py:296
  31.2 1.3 %collective-permute-start.12 = (bf16[8,4608]{1,0:T(8,128)(2,1)S(1)}, bf16[8,4608]{1,0:T(8,128)(2,1)S(1)}, u32[]{:S(2)}, u32[]{:S(2)}) collective-permute-start(bf16[8,4608]{1,0:T(8,128)(2,1)S(1)} %get-tuple-element.50), channel_id=1, source_target_pairs={{0,20},{1,21},{2,22},{3,23},{4,16},{5,17},{6,18},{7,19},{8,28},{9,... | collective-permute-start | bytes 221192 | tf_op jit(solution)/shard_map/ppermute | solution.py:296
  32.4 0.1 collective-permute-start.13
  32.5 4.0 %grads.4 = (bf16[1536,2048]{1,0:T(8,128)(2,1)}, bf16[1536,2048]{1,0:T(8,128)(2,1)}) custom-call(bf16[1536,128]{1,0:T(8,128)(2,1)S(1)} %get-tuple-element.45.refs_0_, bf16[1536,128]{1,0:T(8,128)(2,1)S(1)} %get-tuple-element.52.refs_1_, bf16[128,2048]{1,0:T(8,128)(2,1)S(1)} %get-tuple-element.46.refs_1_.refs_2_, ...), custom_call_target="tpu_custom_call", output_to_operand_aliasing={{0}: (4, {})} | custom-call | flops 1207959552 | bytes 14155776 | tf_op jit(solution)/shard_map/grads/pallas_call | solution.py:253
  36.6 0.0 collective-permute-done.11.refs_1_
  36.6 0.0 collective-permute-done.12.refs_2_
  36.6 0.1 collective-permute-done.13.refs_3_
  36.7 0.2 chips.1
  36.9 2.8 %collective-permute-start.14 = (bf16[24,512]{1,0:T(8,128)(2,1)S(1)}, bf16[24,512]{1,0:T(8,128)(2,1)S(1)}, u32[]{:S(2)}, u32[]{:S(2)}) collective-permute-start(bf16[24,512]{1,0:T(8,128)(2,1)S(1)} %get-tuple-element.61), channel_id=1, source_target_pairs={{0,6},{1,7},{2,4},{3,5},{4,2},{5,3},{6,0},{7,1},{8,14},{9,15},{10,... | collective-permute-start | bytes 73736 | tf_op jit(solution)/shard_map/ppermute | solution.py:296
  39.7 1.6 %collective-permute-start.15 = (bf16[24,512]{1,0:T(8,128)(2,1)S(1)}, bf16[24,512]{1,0:T(8,128)(2,1)S(1)}, u32[]{:S(2)}, u32[]{:S(2)}) collective-permute-start(bf16[24,512]{1,0:T(8,128)(2,1)S(1)} %get-tuple-element.62), channel_id=1, source_target_pairs={{0,7},{1,6},{2,5},{3,4},{4,3},{5,2},{6,1},{7,0},{8,15},{9,14},{10,... | collective-permute-start | bytes 73736 | tf_op jit(solution)/shard_map/ppermute | solution.py:296
  41.3 0.4 collective-permute-start.16
  41.7 3.5 %grads.5 = (bf16[1536,2048]{1,0:T(8,128)(2,1)}, bf16[1536,2048]{1,0:T(8,128)(2,1)}) custom-call(bf16[1536,128]{1,0:T(8,128)(2,1)S(1)} %get-tuple-element.45.refs_0_, bf16[1536,128]{1,0:T(8,128)(2,1)S(1)} %get-tuple-element.64.refs_1_, bf16[128,2048]{1,0:T(8,128)(2,1)S(1)} %get-tuple-element.46.refs_1_.refs_2_, ...), custom_call_target="tpu_custom_call", output_to_operand_aliasing={{0}: (4, {})} | custom-call | flops 1006632960 | bytes 11796480 | tf_op jit(solution)/shard_map/grads/pallas_call | solution.py:253
  45.2 0.0 collective-permute-done.14.refs_1_
  45.2 0.0 collective-permute-done.15.refs_2_
  45.2 0.0 collective-permute-done.16.refs_3_
  45.2 0.6 %home.1 = (bf16[12,512]{1,0:T(8,128)(2,1)}, bf16[12,512]{1,0:T(8,128)(2,1)}) custom-call(bf16[24,512]{1,0:T(8,128)(2,1)S(1)} %get-tuple-element.68.refs_0_, bf16[24,512]{1,0:T(8,128)(2,1)S(1)} %collective-permute-done.14.refs_1_, bf16[24,512]{1,0:T(8,128)(2,1)S(1)} %collective-permute-done.15.refs_2_, bf16[24,512]{1,0:T(8,128)(2,1)S(1)} %collective-permute-done.16.refs_3_), custom_call_target="tpu_custom_call" | custom-call | tf_op jit(solution)/shard_map/home/pallas_call | solution.py:394
  (1 shorter events, 0.0 us)
Async XLA Ops:
  1.4 5.2 %collective-permute-start = (bf16[1,24,512]{2,1,0:T(8,128)(2,1)S(1)}, bf16[1,24,512]{2,1,0:T(8,128)(2,1)S(1)}, u32[]{:S(2)}, u32[]{:S(2)}) collective-permute-start(bf16[1,24,512]{2,1,0:T(8,128)(2,1)S(1)} %maximum_bitcast_fusion.a_ref), channel_id=1, source_target_pairs={{0,6},{1,7},{2,4},{3,5},{4,2},{5,3},{6,0},{7,1},{8,14},{9,15},{10,... | collective-permute-start | bytes 73736 | tf_op jit(solution)/shard_map/ppermute | solution.py:296
  4.9 0.7 %copy-start.3 = (s32[12,2]{0,1:T(2,128)S(1)}, s32[12,2]{0,1:T(2,128)}, u32[]{:S(2)}) copy-start(s32[12,2]{0,1:T(2,128)} %param.9) | copy-start | bytes 292
  5.6 0.7 %copy-start.4 = (f32[12,2]{0,1:T(2,128)S(1)}, f32[12,2]{0,1:T(2,128)}, u32[]{:S(2)}) copy-start(f32[12,2]{0,1:T(2,128)} %param.10) | copy-start | bytes 292
  6.3 12.9 %copy-start = (bf16[1,1536,2048]{2,1,0:T(8,128)(2,1)S(1)}, bf16[1,1536,2048]{2,1,0:T(8,128)(2,1)}, u32[]{:S(2)}) copy-start(bf16[1,1536,2048]{2,1,0:T(8,128)(2,1)} %param.11) | copy-start | bytes 18874372
  6.3 12.9 %copy-start.1 = (bf16[1,1536,2048]{2,1,0:T(8,128)(2,1)S(1)}, bf16[1,1536,2048]{2,1,0:T(8,128)(2,1)}, u32[]{:S(2)}) copy-start(bf16[1,1536,2048]{2,1,0:T(8,128)(2,1)} %param.12) | copy-start | bytes 18874372
  6.3 12.9 %copy-start.2 = (bf16[1,1536,2048]{2,1,0:T(8,128)(2,1)S(1)}, bf16[1,1536,2048]{2,1,0:T(8,128)(2,1)}, u32[]{:S(2)}) copy-start(bf16[1,1536,2048]{2,1,0:T(8,128)(2,1)} %param.13) | copy-start | bytes 18874372
  6.6 3.7 %collective-permute-start.2 = (bf16[2,24,512]{2,1,0:T(8,128)(2,1)S(1)}, bf16[2,24,512]{2,1,0:T(8,128)(2,1)S(1)}, u32[]{:S(2)}, u32[]{:S(2)}) collective-permute-start(bf16[2,24,512]{2,1,0:T(8,128)(2,1)S(1)} %pair.1.a_ref), channel_id=1, source_target_pairs={{0,5},{1,4},{2,7},{3,6},{4,1},{5,0},{6,3},{7,2},{8,13},{9,12},{10,... | collective-permute-start | bytes 147464 | tf_op jit(solution)/shard_map/ppermute | solution.py:296
  8.6 1.2 %collective-permute-start.1 = (f32[72,128]{1,0:T(8,128)S(1)}, f32[72,128]{1,0:T(8,128)S(1)}, u32[]{:S(2)}, u32[]{:S(2)}) collective-permute-start(f32[72,128]{1,0:T(8,128)S(1)} %share.1.mine_ref), channel_id=1, source_target_pairs={{0,4},{1,5},{2,6},{3,7},{4,0},{5,1},{6,2},{7,3},{8,12},{9,13},{10,... | collective-permute-start | bytes 110600 | tf_op jit(solution)/shard_map/ppermute | solution.py:296
  10.5 5.3 %collective-permute-start.5 = (bf16[8,4608]{1,0:T(8,128)(2,1)S(1)}, bf16[8,4608]{1,0:T(8,128)(2,1)S(1)}, u32[]{:S(2)}, u32[]{:S(2)}) collective-permute-start(bf16[8,4608]{1,0:T(8,128)(2,1)S(1)} %join.1.refs_0_), channel_id=1, source_target_pairs={{0,28},{1,29},{2,30},{3,31},{4,24},{5,25},{6,26},{7,27},{8,20},{9,... | collective-permute-start | bytes 221192 | tf_op jit(solution)/shard_map/ppermute | solution.py:296
  13.2 4.2 %collective-permute-start.4 = (bf16[8,4608]{1,0:T(8,128)(2,1)S(1)}, bf16[8,4608]{1,0:T(8,128)(2,1)S(1)}, u32[]{:S(2)}, u32[]{:S(2)}) collective-permute-start(bf16[8,4608]{1,0:T(8,128)(2,1)S(1)} %join.1.refs_0_), channel_id=1, source_target_pairs={{0,20},{1,21},{2,22},{3,23},{4,16},{5,17},{6,18},{7,19},{8,28},{9,... | collective-permute-start | bytes 221192 | tf_op jit(solution)/shard_map/ppermute | solution.py:296
  13.6 4.3 %collective-permute-start.3 = (bf16[8,4608]{1,0:T(8,128)(2,1)S(1)}, bf16[8,4608]{1,0:T(8,128)(2,1)S(1)}, u32[]{:S(2)}, u32[]{:S(2)}) collective-permute-start(bf16[8,4608]{1,0:T(8,128)(2,1)S(1)} %join.1.refs_0_), channel_id=1, source_target_pairs={{0,12},{1,13},{2,14},{3,15},{4,8},{5,9},{6,10},{7,11},{8,4},{9,5},... | collective-permute-start | bytes 221192 | tf_op jit(solution)/shard_map/ppermute | solution.py:296
  13.9 4.0 %collective-permute-start.6 = (bf16[8,4608]{1,0:T(8,128)(2,1)S(1)}, bf16[8,4608]{1,0:T(8,128)(2,1)S(1)}, u32[]{:S(2)}, u32[]{:S(2)}) collective-permute-start(bf16[8,4608]{1,0:T(8,128)(2,1)S(1)} %join.1.refs_0_), channel_id=1, source_target_pairs={{0,4},{1,5},{2,6},{3,7},{4,0},{5,1},{6,2},{7,3},{8,12},{9,13},{10,... | collective-permute-start | bytes 221192 | tf_op jit(solution)/shard_map/ppermute | solution.py:296
  15.8 2.2 %collective-permute-start.9 = (bf16[8,4608]{1,0:T(8,128)(2,1)S(1)}, bf16[8,4608]{1,0:T(8,128)(2,1)S(1)}, u32[]{:S(2)}, u32[]{:S(2)}) collective-permute-start(bf16[8,4608]{1,0:T(8,128)(2,1)S(1)} %collective-permute-done.5.refs_3_), channel_id=1, source_target_pairs={{0,4},{1,5},{2,6},{3,7},{4,0},{5,1},{6,2},{7,3},{8,12},{9,13},{10,... | collective-permute-start | bytes 221192 | tf_op jit(solution)/shard_map/ppermute | solution.py:296
  17.4 1.4 %collective-permute-start.8 = (bf16[8,4608]{1,0:T(8,128)(2,1)S(1)}, bf16[8,4608]{1,0:T(8,128)(2,1)S(1)}, u32[]{:S(2)}, u32[]{:S(2)}) collective-permute-start(bf16[8,4608]{1,0:T(8,128)(2,1)S(1)} %collective-permute-done.4.refs_2_), channel_id=1, source_target_pairs={{0,4},{1,5},{2,6},{3,7},{4,0},{5,1},{6,2},{7,3},{8,12},{9,13},{10,... | collective-permute-start | bytes 221192 | tf_op jit(solution)/shard_map/ppermute | solution.py:296
  17.9 1.3 %collective-permute-start.7 = (bf16[8,4608]{1,0:T(8,128)(2,1)S(1)}, bf16[8,4608]{1,0:T(8,128)(2,1)S(1)}, u32[]{:S(2)}, u32[]{:S(2)}) collective-permute-start(bf16[8,4608]{1,0:T(8,128)(2,1)S(1)} %collective-permute-done.3.refs_1_), channel_id=1, source_target_pairs={{0,4},{1,5},{2,6},{3,7},{4,0},{5,1},{6,2},{7,3},{8,12},{9,13},{10,... | collective-permute-start | bytes 221192 | tf_op jit(solution)/shard_map/ppermute | solution.py:296
  27.6 1.7 %collective-permute-start.10 = (bf16[4,8,4608]{2,1,0:T(8,128)(2,1)S(1)}, bf16[4,8,4608]{2,1,0:T(8,128)(2,1)S(1)}, u32[]{:S(2)}, u32[]{:S(2)}) collective-permute-start(bf16[4,8,4608]{2,1,0:T(8,128)(2,1)S(1)} %get-tuple-element.44), channel_id=1, source_target_pairs={{0,4},{1,5},{2,6},{3,7},{4,0},{5,1},{6,2},{7,3},{8,12},{9,13},{10,... | collective-permute-start | bytes 884744 | tf_op jit(solution)/shard_map/ppermute | solution.py:296
  29.3 7.3 %collective-permute-start.11 = (bf16[8,4608]{1,0:T(8,128)(2,1)S(1)}, bf16[8,4608]{1,0:T(8,128)(2,1)S(1)}, u32[]{:S(2)}, u32[]{:S(2)}) collective-permute-start(bf16[8,4608]{1,0:T(8,128)(2,1)S(1)} %get-tuple-element.49), channel_id=1, source_target_pairs={{0,28},{1,29},{2,30},{3,31},{4,24},{5,25},{6,26},{7,27},{8,20},{9,... | collective-permute-start | bytes 221192 | tf_op jit(solution)/shard_map/ppermute | solution.py:296
  31.2 5.4 %collective-permute-start.12 = (bf16[8,4608]{1,0:T(8,128)(2,1)S(1)}, bf16[8,4608]{1,0:T(8,128)(2,1)S(1)}, u32[]{:S(2)}, u32[]{:S(2)}) collective-permute-start(bf16[8,4608]{1,0:T(8,128)(2,1)S(1)} %get-tuple-element.50), channel_id=1, source_target_pairs={{0,20},{1,21},{2,22},{3,23},{4,16},{5,17},{6,18},{7,19},{8,28},{9,... | collective-permute-start | bytes 221192 | tf_op jit(solution)/shard_map/ppermute | solution.py:296
  32.4 4.2 %collective-permute-start.13 = (bf16[8,4608]{1,0:T(8,128)(2,1)S(1)}, bf16[8,4608]{1,0:T(8,128)(2,1)S(1)}, u32[]{:S(2)}, u32[]{:S(2)}) collective-permute-start(bf16[8,4608]{1,0:T(8,128)(2,1)S(1)} %get-tuple-element.51), channel_id=1, source_target_pairs={{0,12},{1,13},{2,14},{3,15},{4,8},{5,9},{6,10},{7,11},{8,4},{9,5},... | collective-permute-start | bytes 221192 | tf_op jit(solution)/shard_map/ppermute | solution.py:296
  36.9 8.3 %collective-permute-start.14 = (bf16[24,512]{1,0:T(8,128)(2,1)S(1)}, bf16[24,512]{1,0:T(8,128)(2,1)S(1)}, u32[]{:S(2)}, u32[]{:S(2)}) collective-permute-start(bf16[24,512]{1,0:T(8,128)(2,1)S(1)} %get-tuple-element.61), channel_id=1, source_target_pairs={{0,6},{1,7},{2,4},{3,5},{4,2},{5,3},{6,0},{7,1},{8,14},{9,15},{10,... | collective-permute-start | bytes 73736 | tf_op jit(solution)/shard_map/ppermute | solution.py:296
  39.7 5.5 %collective-permute-start.15 = (bf16[24,512]{1,0:T(8,128)(2,1)S(1)}, bf16[24,512]{1,0:T(8,128)(2,1)S(1)}, u32[]{:S(2)}, u32[]{:S(2)}) collective-permute-start(bf16[24,512]{1,0:T(8,128)(2,1)S(1)} %get-tuple-element.62), channel_id=1, source_target_pairs={{0,7},{1,6},{2,5},{3,4},{4,3},{5,2},{6,1},{7,0},{8,15},{9,14},{10,... | collective-permute-start | bytes 73736 | tf_op jit(solution)/shard_map/ppermute | solution.py:296
  41.3 4.0 %collective-permute-start.16 = (bf16[24,512]{1,0:T(8,128)(2,1)S(1)}, bf16[24,512]{1,0:T(8,128)(2,1)S(1)}, u32[]{:S(2)}, u32[]{:S(2)}) collective-permute-start(bf16[24,512]{1,0:T(8,128)(2,1)S(1)} %get-tuple-element.63), channel_id=1, source_target_pairs={{0,5},{1,4},{2,7},{3,6},{4,1},{5,0},{6,3},{7,2},{8,13},{9,12},{10,... | collective-permute-start | bytes 73736 | tf_op jit(solution)/shard_map/ppermute | solution.py:296
